TPU v7x, 128 devices: a whole 4x4x4 slice. The times are simulated.
128 devices in a mesh: dp: 8 (over x_lo, y), head: 16 (over x_hi, z, core).
Axes of the slice: x: 4 (x_hi: 2, x_lo: 2; x = x_hi * 2 + x_lo), y: 4, z: 4, core: 2. Of those that a mesh axis runs over, the one named last changes fastest.
Arguments:
- block_input: bfloat16 [16384, 2048], P(('dp', 'head')), may hold values from -6 to 6
- cotangent: bfloat16 [16384, 2048], P(('dp', 'head')), may hold values from -6 to 6
- lengths: int32 [8, 3], P('dp'), may hold values from 1 to 1920, as said below
- gain_a: float32 [2048], replicated, may hold values from 0.5 to 1.5
- based_in: bfloat16 [2048, 2560], P(None, ('head', 'dp')), may hold values from -0.125 to 0.125
- based_out: bfloat16 [2048, 2048], P(('head', 'dp')), may hold values from -1.5 to 1.5
- gain_b: float32 [2048], replicated, may hold values from 0.5 to 1.5
- swa_in: bfloat16 [2048, 6144], P(None, ('head', 'dp')), may hold values from -0.125 to 0.125
- swa_out: bfloat16 [2048, 2048], P(('head', 'dp')), may hold values from -0.5 to 0.5
- gain_c: float32 [2048], replicated, may hold values from 0.5 to 1.5
- mlp_in: bfloat16 [2048, 2, 5632], P(None, None, ('head', 'dp')), may hold values from -0.125 to 0.125
- mlp_down: bfloat16 [5632, 2048], P(('head', 'dp')), may hold values from -0.078125 to 0.078125
Outputs:
- block_output: bfloat16 [16384, 2048], P(('dp', 'head'))
- input_grad: float32 [16384, 2048], P(('dp', 'head'))
- grad_gain_a: float32 [2048], replicated
- grad_based_in: float32 [2048, 2560], P(None, ('head', 'dp'))
- grad_based_out: float32 [2048, 2048], P(('head', 'dp'))
- grad_gain_b: float32 [2048], replicated
- grad_swa_in: float32 [2048, 6144], P(None, ('head', 'dp'))
- grad_swa_out: float32 [2048, 2048], P(('head', 'dp'))
- grad_gain_c: float32 [2048], replicated
- grad_mlp_in: float32 [2048, 2, 5632], P(None, None, ('head', 'dp'))
- grad_mlp_down: float32 [5632, 2048], P(('head', 'dp'))
Inputs may be any that keep to these rules, and one draw needn't show every extreme that they name: `lengths`: in each group the 3 sequences take buckets of 64, 1920 and 64 consecutive slots, in this order; a sequence's tokens open its bucket and padding fills the rest. The middle sequence fills its bucket; each other one has 1 to 64 tokens.
All inputs are finite; a program needn't handle non-finite values.
Results may differ from a plain program's by a relative error of at most 0.033.
Values may be sent and summed in bfloat16 or wider, within the bound.
A program may use at most 192 MiB of HBM per device.

v0:
```python
import math

import jax
import jax.numpy as jnp
from jax import lax
from jax.sharding import PartitionSpec as P

FEAT = 16
HEAD_V = 128
WINDOW = 64


EPSILON = 1e-05


def norm_apply(values, gain):
    scale = lax.rsqrt(jnp.mean(values * values, axis=-1, keepdims=True) + EPSILON)
    return values * scale * gain


def norm_back(values, gain, grads):
    scale = lax.rsqrt(jnp.mean(values * values, axis=-1, keepdims=True) + EPSILON)
    unit_rows = values * scale
    scaled = grads * gain
    value_grad = scale * (scaled - unit_rows * jnp.mean(scaled * unit_rows, axis=-1, keepdims=True))
    return (value_grad, jnp.sum(grads * unit_rows, axis=0))


def layout(length_row, group_tok, half_len):
    slot_ids = jnp.arange(group_tok, dtype=jnp.int32)
    segment = (slot_ids >= half_len).astype(jnp.int32) + (slot_ids >= group_tok - half_len).astype(
        jnp.int32
    )
    bucket_start = jnp.where(
        segment == 0, 0, jnp.where(segment == 1, half_len, group_tok - half_len)
    ).astype(jnp.int32)
    position = slot_ids - bucket_start
    chosen = jnp.where(
        segment == 0, length_row[0], jnp.where(segment == 1, length_row[1], length_row[2])
    )
    return (segment, position, position < chosen)


def turning(position, head_width):
    half_width = head_width // 2
    frequency = jnp.exp(
        -math.log(10000.0) * jnp.arange(half_width, dtype=jnp.float32) * 2.0 / head_width
    )
    angles = position.astype(jnp.float32)[:, None] * frequency[None, :]
    angles = jnp.concatenate([angles, angles], axis=-1)[:, None, :]
    return (jnp.cos(angles), jnp.sin(angles))


def rotate_half(values):
    half_width = values.shape[-1] // 2
    return jnp.concatenate([-values[..., half_width:], values[..., :half_width]], axis=-1)


def rotary(values, cosine, sine_part):
    return values * cosine + rotate_half(values) * sine_part


def rotary_back(grads, cosine, sine_part):
    return grads * cosine - rotate_half(grads * sine_part)


def linear_scores(queries, key_vecs, segment, block_rows, block_index):
    slot_ids = jnp.arange(queries.shape[0], dtype=jnp.int32)
    row_start = block_index * block_rows
    row_block = lax.dynamic_slice_in_dim(queries, row_start, block_rows, 0)
    row_seg = lax.dynamic_slice_in_dim(segment, row_start, block_rows, 0)
    row_slots = row_start + jnp.arange(block_rows, dtype=jnp.int32)
    allowed = (row_seg[:, None] == segment[None, :]) & (row_slots[:, None] >= slot_ids[None, :])
    scores = jnp.einsum(
        "rhf,chf->hrc", row_block, key_vecs, preferred_element_type=jnp.float32
    ) / math.sqrt(queries.shape[-1])
    kernel = jnp.where(allowed[None], 1.0 + scores + 0.5 * scores * scores, 0.0)
    return (row_block, allowed, scores, kernel)


def linear_forward(queries, key_vecs, values, segment, block_rows):

    def one_block(block_index):
        row_block, allowed, scores, kernel = linear_scores(
            queries, key_vecs, segment, block_rows, block_index
        )
        totals = jnp.sum(kernel, axis=-1, keepdims=True)
        weights = (kernel / totals).astype(jnp.bfloat16)
        mixed_out = jnp.einsum("hrc,che->rhe", weights, values, preferred_element_type=jnp.float32)
        return (mixed_out.astype(jnp.bfloat16), totals)

    mixed_out, totals = lax.map(
        one_block, jnp.arange(queries.shape[0] // block_rows, dtype=jnp.int32)
    )
    return (mixed_out.reshape(queries.shape[0], queries.shape[1], values.shape[-1]), totals)


def linear_backward(queries, key_vecs, values, segment, block_rows, totals, mixed_grad):
    root = math.sqrt(queries.shape[-1])

    def one_block(carried, block_index):
        key_grad, value_grad = carried
        row_block, allowed, scores, kernel = linear_scores(
            queries, key_vecs, segment, block_rows, block_index
        )
        block_totals = totals[block_index]
        ratios = kernel / block_totals
        weights = ratios.astype(jnp.bfloat16)
        grad_rows = lax.dynamic_slice_in_dim(mixed_grad, block_index * block_rows, block_rows, 0)
        weight_grad = jnp.einsum(
            "rhe,che->hrc", grad_rows, values, preferred_element_type=jnp.float32
        )
        kernel_grad = (
            weight_grad - jnp.sum(weight_grad * ratios, axis=-1, keepdims=True)
        ) / block_totals
        score_grad = jnp.where(allowed[None], kernel_grad * (1.0 + scores), 0.0).astype(
            jnp.bfloat16
        )
        query_grad = (
            jnp.einsum("hrc,chf->rhf", score_grad, key_vecs, preferred_element_type=jnp.float32)
            / root
        )
        key_grad = (
            key_grad
            + jnp.einsum("hrc,rhf->chf", score_grad, row_block, preferred_element_type=jnp.float32)
            / root
        )
        value_grad = value_grad + jnp.einsum(
            "hrc,rhe->che", weights, grad_rows, preferred_element_type=jnp.float32
        )
        return ((key_grad, value_grad), query_grad)

    start_state = (jnp.zeros(key_vecs.shape, jnp.float32), jnp.zeros(values.shape, jnp.float32))
    block_ids = jnp.arange(queries.shape[0] // block_rows, dtype=jnp.int32)
    (key_grad, value_grad), query_grad = lax.scan(one_block, start_state, block_ids)
    return (query_grad.reshape(queries.shape), key_grad, value_grad)


def window_pairs(tensor, tile_width, fill):
    tiled = tensor.reshape((-1, tile_width) + tensor.shape[1:])
    before = jnp.concatenate([jnp.full_like(tiled[:1], fill), tiled[:-1]], axis=0)
    return jnp.concatenate([before, tiled], axis=1)


def window_scores(queries, key_vecs, segment, tile_width):
    query_tiles = queries.reshape((-1, tile_width) + queries.shape[1:])
    key_pairs = window_pairs(key_vecs, tile_width, 0)
    seg_tiles = segment.reshape(-1, tile_width)
    seg_pairs = window_pairs(segment, tile_width, -1)
    row_ids = jnp.arange(tile_width, dtype=jnp.int32)[:, None]
    col_ids = jnp.arange(2 * tile_width, dtype=jnp.int32)[None, :]
    allowed = (
        (seg_tiles[:, :, None] == seg_pairs[:, None, :])
        & (col_ids > row_ids)
        & (col_ids <= row_ids + tile_width)
    )
    scores = jnp.einsum(
        "tahe,tjhe->thaj", query_tiles, key_pairs, preferred_element_type=jnp.float32
    ) / math.sqrt(queries.shape[-1])
    return (query_tiles, key_pairs, allowed[:, None], scores)


def window_fold(pair_grad, tile_width):
    own_part = pair_grad[:, tile_width:]
    spill_part = jnp.concatenate(
        [pair_grad[1:, :tile_width], jnp.zeros_like(pair_grad[:1, :tile_width])], axis=0
    )
    return (own_part + spill_part).reshape((-1,) + pair_grad.shape[2:])


def window_forward(queries, key_vecs, values, segment, tile_width):
    query_tiles, key_pairs, allowed, scores = window_scores(queries, key_vecs, segment, tile_width)
    value_pairs = window_pairs(values, tile_width, 0)
    row_max = jnp.max(jnp.where(allowed, scores, -1e30), axis=-1, keepdims=True)
    exp_scores = jnp.where(allowed, jnp.exp(scores - row_max), 0.0)
    totals = jnp.sum(exp_scores, axis=-1, keepdims=True)
    prob_weights = (exp_scores / totals).astype(jnp.bfloat16)
    mixed_out = jnp.einsum(
        "thaj,tjhe->tahe", prob_weights, value_pairs, preferred_element_type=jnp.float32
    )
    return (mixed_out.astype(jnp.bfloat16).reshape(values.shape), row_max + jnp.log(totals))


def window_backward(queries, key_vecs, values, segment, tile_width, log_total, mixed_grad):
    query_tiles, key_pairs, allowed, scores = window_scores(queries, key_vecs, segment, tile_width)
    value_pairs = window_pairs(values, tile_width, 0)
    prob_exact = jnp.where(allowed, jnp.exp(scores - log_total), 0.0)
    grad_tiles = mixed_grad.reshape(query_tiles.shape)
    prob_grad = jnp.einsum(
        "tahe,tjhe->thaj", grad_tiles, value_pairs, preferred_element_type=jnp.float32
    )
    score_grad = (
        prob_exact * (prob_grad - jnp.sum(prob_grad * prob_exact, axis=-1, keepdims=True))
    ).astype(jnp.bfloat16)
    root = math.sqrt(queries.shape[-1])
    query_grad = (
        jnp.einsum("thaj,tjhe->tahe", score_grad, key_pairs, preferred_element_type=jnp.float32)
        / root
    )
    key_pair_grad = (
        jnp.einsum("thaj,tahe->tjhe", score_grad, query_tiles, preferred_element_type=jnp.float32)
        / root
    )
    value_pair_grad = jnp.einsum(
        "thaj,tahe->tjhe",
        prob_exact.astype(jnp.bfloat16),
        grad_tiles,
        preferred_element_type=jnp.float32,
    )
    return (
        query_grad.reshape(queries.shape),
        window_fold(key_pair_grad, tile_width),
        window_fold(value_pair_grad, tile_width),
    )


def contract_rows(left_side, right_side):
    return lax.dot_general(
        left_side, right_side, (((0,), (0,)), ((), ())), preferred_element_type=jnp.float32
    )


def contract_cols(left_side, right_side):
    return lax.dot_general(
        left_side, right_side, (((1,), (1,)), ((), ())), preferred_element_type=jnp.float32
    )


def body(
    block_input,
    cotangent,
    lengths,
    gain_a,
    based_in,
    based_out,
    gain_b,
    swa_in,
    swa_out,
    gain_c,
    mlp_in,
    mlp_down,
):
    tok_local = block_input.shape[0]
    group_tok = tok_local * lax.axis_size("head")
    first_slot = lax.axis_index("head") * tok_local
    segment, position, valid_mask = layout(lengths[0], group_tok, tok_local // 2)
    block_rows = min(512, group_tok)
    cosine, sine_part = turning(position, HEAD_V)
    linear_width = 2 * FEAT + HEAD_V
    gathered = (
        lax.all_gather(based_in, "dp", axis=1, tiled=True),
        lax.all_gather(based_out, "dp", axis=0, tiled=True),
        lax.all_gather(swa_in, "dp", axis=1, tiled=True),
        lax.all_gather(swa_out, "dp", axis=0, tiled=True),
        lax.all_gather(mlp_in, "dp", axis=2, tiled=True),
        lax.all_gather(mlp_down, "dp", axis=0, tiled=True),
    )
    lin_in, lin_out, win_in, win_out, ff_in, ff_out = gathered
    ff_flat = ff_in.reshape(ff_in.shape[0], -1)

    def project_out(left_side, right_side):
        return lax.psum_scatter(
            jnp.dot(left_side, right_side, preferred_element_type=jnp.float32).astype(jnp.bfloat16),
            "head",
            scatter_dimension=0,
            tiled=True,
        ).astype(jnp.float32)

    input_local = block_input.astype(jnp.float32)

    def share_rows(rows_local):
        return lax.all_gather(rows_local, "head", axis=0, tiled=True)

    normed_first = share_rows(norm_apply(input_local, gain_a).astype(jnp.bfloat16))
    projected = jnp.dot(normed_first, lin_in, preferred_element_type=jnp.float32).astype(
        jnp.bfloat16
    )
    per_head = projected.reshape(group_tok, -1, linear_width)
    queries = per_head[..., :FEAT]
    key_vecs = per_head[..., FEAT : 2 * FEAT]
    values = per_head[..., 2 * FEAT :]
    mixed_out, totals = linear_forward(queries, key_vecs, values, segment, block_rows)
    mixed_first = mixed_out.reshape(group_tok, -1)
    saved_first = (queries, key_vecs, values, totals)
    middle_local = input_local + project_out(mixed_first, lin_out)
    normed_second = share_rows(norm_apply(middle_local, gain_b).astype(jnp.bfloat16))
    projected = jnp.dot(normed_second, win_in, preferred_element_type=jnp.float32).reshape(
        group_tok, -1, 3 * HEAD_V
    )
    queries = rotary(projected[..., :HEAD_V], cosine, sine_part).astype(jnp.bfloat16)
    key_vecs = rotary(projected[..., HEAD_V : 2 * HEAD_V], cosine, sine_part).astype(jnp.bfloat16)
    values = projected[..., 2 * HEAD_V :].astype(jnp.bfloat16)
    mixed_out, log_total = window_forward(queries, key_vecs, values, segment, WINDOW)
    mixed_second = mixed_out.reshape(group_tok, -1)
    saved_second = (queries, key_vecs, values, log_total)
    late_local = middle_local + project_out(mixed_second, win_out)
    normed_third = share_rows(norm_apply(late_local, gain_c).astype(jnp.bfloat16))
    gate_up = jnp.dot(normed_third, ff_flat, preferred_element_type=jnp.float32)
    ff_width = gate_up.shape[1] // 2
    gate_part = gate_up[:, :ff_width]
    up_part = gate_up[:, ff_width:]
    activated = (jax.nn.silu(gate_part) * up_part).astype(jnp.bfloat16)
    block_output = (late_local + project_out(activated, ff_out)).astype(jnp.bfloat16)
    back_weights = (
        lax.all_gather(based_in, "dp", axis=1, tiled=True),
        lax.all_gather(based_out, "dp", axis=0, tiled=True),
        lax.all_gather(swa_in, "dp", axis=1, tiled=True),
        lax.all_gather(swa_out, "dp", axis=0, tiled=True),
        lax.all_gather(mlp_in, "dp", axis=2, tiled=True),
        lax.all_gather(mlp_down, "dp", axis=0, tiled=True),
    )
    ff_back = back_weights[4].reshape(back_weights[4].shape[0], -1)

    def spread(grad_local):
        return lax.all_gather(grad_local.astype(jnp.bfloat16), "head", axis=0, tiled=True)

    def gather_back(left_side, right_side):
        return lax.psum_scatter(
            contract_cols(left_side, right_side).astype(jnp.bfloat16),
            "head",
            scatter_dimension=0,
            tiled=True,
        ).astype(jnp.float32)

    valid_local = lax.dynamic_slice_in_dim(valid_mask, first_slot, tok_local, 0)
    cot_local = cotangent.astype(jnp.float32) * valid_local[:, None].astype(jnp.float32)
    grad_third = spread(cot_local)
    ff_out_grad = contract_rows(activated, grad_third)
    act_grad = contract_cols(grad_third, back_weights[5])
    sigmoid_gate = jax.nn.sigmoid(gate_part)
    gate_grad = act_grad * up_part * sigmoid_gate * (1.0 + gate_part * (1.0 - sigmoid_gate))
    up_grad = act_grad * gate_part * sigmoid_gate
    gate_up_grad = jnp.concatenate([gate_grad, up_grad], axis=1).astype(jnp.bfloat16)
    ff_in_grad = contract_rows(normed_third, gate_up_grad).reshape(ff_in.shape)
    third_norm_grad, gain_c_grad = norm_back(late_local, gain_c, gather_back(gate_up_grad, ff_back))
    late_grad = cot_local + third_norm_grad
    grad_second = spread(late_grad)
    win_out_grad = contract_rows(mixed_second, grad_second)
    mixed_grad = (
        contract_cols(grad_second, back_weights[3])
        .astype(jnp.bfloat16)
        .reshape(group_tok, -1, HEAD_V)
    )
    queries, key_vecs, values, log_total = saved_second
    query_grad, key_grad, value_grad = window_backward(
        queries, key_vecs, values, segment, WINDOW, log_total, mixed_grad
    )
    proj_grad = jnp.concatenate(
        [
            rotary_back(query_grad, cosine, sine_part),
            rotary_back(key_grad, cosine, sine_part),
            value_grad,
        ],
        axis=-1,
    )
    proj_grad = proj_grad.astype(jnp.bfloat16).reshape(group_tok, -1)
    win_in_grad = contract_rows(normed_second, proj_grad)
    second_norm_grad, gain_b_grad = norm_back(
        middle_local, gain_b, gather_back(proj_grad, back_weights[2])
    )
    middle_grad = late_grad + second_norm_grad
    grad_first = spread(middle_grad)
    lin_out_grad = contract_rows(mixed_first, grad_first)
    mixed_grad = (
        contract_cols(grad_first, back_weights[1])
        .astype(jnp.bfloat16)
        .reshape(group_tok, -1, HEAD_V)
    )
    queries, key_vecs, values, totals = saved_first
    query_grad, key_grad, value_grad = linear_backward(
        queries, key_vecs, values, segment, block_rows, totals, mixed_grad
    )
    proj_grad = (
        jnp.concatenate([query_grad, key_grad, value_grad], axis=-1)
        .astype(jnp.bfloat16)
        .reshape(group_tok, -1)
    )
    lin_in_grad = contract_rows(normed_first, proj_grad)
    first_norm_grad, gain_a_grad = norm_back(
        input_local, gain_a, gather_back(proj_grad, back_weights[0])
    )
    input_grad = middle_grad + first_norm_grad
    weight_grads = (
        lax.psum_scatter(
            lin_in_grad.astype(jnp.bfloat16), "dp", scatter_dimension=1, tiled=True
        ).astype(jnp.float32),
        lax.psum_scatter(
            lin_out_grad.astype(jnp.bfloat16), "dp", scatter_dimension=0, tiled=True
        ).astype(jnp.float32),
        lax.psum_scatter(
            win_in_grad.astype(jnp.bfloat16), "dp", scatter_dimension=1, tiled=True
        ).astype(jnp.float32),
        lax.psum_scatter(
            win_out_grad.astype(jnp.bfloat16), "dp", scatter_dimension=0, tiled=True
        ).astype(jnp.float32),
        lax.psum_scatter(
            ff_in_grad.astype(jnp.bfloat16), "dp", scatter_dimension=2, tiled=True
        ).astype(jnp.float32),
        lax.psum_scatter(
            ff_out_grad.astype(jnp.bfloat16), "dp", scatter_dimension=0, tiled=True
        ).astype(jnp.float32),
    )
    gain_grads = lax.psum((gain_a_grad, gain_b_grad, gain_c_grad), ("dp", "head"))
    return (
        block_output,
        input_grad,
        gain_grads[0],
        weight_grads[0],
        weight_grads[1],
        gain_grads[1],
        weight_grads[2],
        weight_grads[3],
        gain_grads[2],
        weight_grads[4],
        weight_grads[5],
    )


def solution(mesh):
    placed = (
        P(("dp", "head"), None),
        P(("dp", "head"), None),
        P("dp", None),
        P(),
        P(None, ("head", "dp")),
        P(("head", "dp"), None),
        P(),
        P(None, ("head", "dp")),
        P(("head", "dp"), None),
        P(),
        P(None, None, ("head", "dp")),
        P(("head", "dp"), None),
    )
    return jax.shard_map(
        body,
        mesh=mesh,
        in_specs=placed,
        out_specs=(
            P(("dp", "head"), None),
            P(("dp", "head"), None),
            P(),
            P(None, ("head", "dp")),
            P(("head", "dp"), None),
            P(),
            P(None, ("head", "dp")),
            P(("head", "dp"), None),
            P(),
            P(None, None, ("head", "dp")),
            P(("head", "dp"), None),
        ),
        check_vma=False,
    )
```

profile of v0, /device:TPU:0, one launch (start us, length us, event | category | flops | bytes accessed | tf_op | source)
XLA Modules:
  0.0 1562.3 jit_solution(8536800241023942715)
XLA Ops:
  11.4 32.0 %all-gather = bf16[8,20,2048]{2,1,0:T(8,128)(2,1)S(1)} all-gather(bf16[1,20,2048]{2,1,0:T(8,128)(2,1)} %bitcast.271), channel_id=1, replica_groups=mesh['dp'=8,'head'=16] {'dp'}, dimensions={0}, use_global_device_ids=true | all-gather | bytes 737280 | tf_op jit(solution)/shard_map/all_gather | solution.py:251
  43.6 29.9 %all_gather.44 = bf16[128,2048]{1,0:T(8,128)(2,1)S(1)} all-gather(bf16[16,2048]{1,0:T(8,128)(2,1)S(1)} %copy-done.40), channel_id=1, replica_groups=mesh['dp'=8,'head'=16] {'dp'}, dimensions={0}, use_global_device_ids=true | all-gather | bytes 589824 | tf_op jit(solution)/shard_map/all_gather | solution.py:252
  73.5 19.2 %all-gather.12.cloned.1.call-done = bf16[2048,2048]{1,0:T(8,128)(2,1)} async-done(((bf16[128,2048]{1,0:T(8,128)(2,1)}), bf16[2048,2048]{1,0:T(8,128)(2,1)}) %all-gather.12.cloned.1.call-update) | async-done | bytes 8388624 | tf_op jit(solution)/shard_map/all_gather | solution.py:272
  99.4 16.0 %while.33 = (s32[]{:T(128)}, bf16[4,512,1,128]{3,1,2,0:T(8,128)(2,1)S(1)}, f32[4,1,512,1]{2,3,1,0:T(1,128)S(1)}, s32[4]{0:T(128)S(1)}, s32[2048]{0:T(1024)S(1)},...) while((s32[]{:T(128)}, ...), condition=%wide.region_3.4_spmd.clone, body=%wide.region_1.3_spmd.clone.sunk | while | flops 314638336 | bytes 9152715 | solution.py:92
  121.8 99.0 %reduce-scatter.14.cloned.1.call-done = bf16[128,2048]{1,0:T(8,128)(2,1)} async-done(((bf16[2048,2048]{1,0:T(8,128)(2,1)}), bf16[128,2048]{1,0:T(8,128)(2,1)}) %reduce-scatter.14.cloned.1.call-update) | async-done | bytes 524304 | tf_op jit(solution)/shard_map/reduce_scatter | solution.py:262
  224.4 31.8 %all_gather.47 = bf16[128,2048]{1,0:T(8,128)(2,1)} all-gather(bf16[16,2048]{1,0:T(8,128)(2,1)S(1)} %copy-done.41), channel_id=1, replica_groups=mesh['dp'=8,'head'=16] {'dp'}, dimensions={0}, use_global_device_ids=true | all-gather | bytes 589824 | tf_op jit(solution)/shard_map/all_gather | solution.py:254
  257.5 39.6 %all-gather.14.cloned.1.call-done = bf16[2048,2048]{1,0:T(8,128)(2,1)} async-done(((bf16[128,2048]{1,0:T(8,128)(2,1)}), bf16[2048,2048]{1,0:T(8,128)(2,1)}) %all-gather.14.cloned.1.call-update) | async-done | bytes 8388624 | tf_op jit(solution)/shard_map/all_gather | solution.py:272
  297.2 7.4 fusion.124
  321.3 98.4 %reduce-scatter.16.cloned.1.call-done = bf16[128,2048]{1,0:T(8,128)(2,1)} async-done(((bf16[2048,2048]{1,0:T(8,128)(2,1)}), bf16[128,2048]{1,0:T(8,128)(2,1)}) %reduce-scatter.16.cloned.1.call-update) | async-done | bytes 524304 | tf_op jit(solution)/shard_map/reduce_scatter | solution.py:262
  427.3 33.2 %all-gather.28.cloned.1.call-done = bf16[8,44,2048]{2,1,0:T(8,128)(2,1)} async-done(((bf16[1,44,2048]{2,1,0:T(8,128)(2,1)}), bf16[8,44,2048]{2,1,0:T(8,128)(2,1)}) %all-gather.28.cloned.1.call-update) | async-done | bytes 1441808 | tf_op jit(solution)/shard_map/all_gather | solution.py:256
  462.9 41.7 %all-gather.20.cloned.1.call-done = bf16[2048,2,352]{0,1,2:T(2,128)(2,1)} async-done(((bf16[2048,2,44]{0,1,2:T(2,128)(2,1)}), bf16[2048,2,352]{0,1,2:T(2,128)(2,1)}) %all-gather.20.cloned.1.call-update) | async-done | bytes 2883600 | tf_op jit(solution)/shard_map/all_gather | solution.py:255
  509.3 70.6 %all-gather.18.cloned.1.call-done = bf16[2048,2048]{1,0:T(8,128)(2,1)} async-done(((bf16[128,2048]{1,0:T(8,128)(2,1)}), bf16[2048,2048]{1,0:T(8,128)(2,1)}) %all-gather.18.cloned.1.call-update) | async-done | bytes 8388624 | tf_op jit(solution)/shard_map/all_gather | solution.py:272
  580.0 11.2 fusion.125
  591.1 61.7 %all-gather.22.cloned.1.call-done = bf16[2048,2048]{1,0:T(8,128)(2,1)} async-done(((bf16[128,2048]{1,0:T(8,128)(2,1)}), bf16[2048,2048]{1,0:T(8,128)(2,1)}) %all-gather.22.cloned.1.call-update) | async-done | bytes 8388624 | tf_op jit(solution)/shard_map/all_gather | solution.py:315
  652.9 11.0 multiply_convert_fusion.1
  665.5 9.1 convolution_convert_fusion.1
  674.8 100.0 %reduce-scatter.20.cloned.1.call-done = bf16[128,2048]{1,0:T(8,128)(2,1)} async-done(((bf16[2048,2048]{1,0:T(8,128)(2,1)}), bf16[128,2048]{1,0:T(8,128)(2,1)}) %reduce-scatter.20.cloned.1.call-update) | async-done | bytes 524304 | tf_op jit(solution)/shard_map/reduce_scatter | solution.py:318
  779.6 72.0 %all-gather.24.cloned.1.call-done = bf16[2048,2048]{1,0:T(8,128)(2,1)} async-done(((bf16[128,2048]{1,0:T(8,128)(2,1)}), bf16[2048,2048]{1,0:T(8,128)(2,1)}) %all-gather.24.cloned.1.call-update) | async-done | bytes 8388624 | tf_op jit(solution)/shard_map/all_gather | solution.py:315
  881.8 10.1 convolution_convert_fusion.2
  891.9 89.7 %reduce-scatter.22.cloned.1.call-done = bf16[128,2048]{1,0:T(8,128)(2,1)} async-done(((bf16[2048,2048]{1,0:T(8,128)(2,1)}), bf16[128,2048]{1,0:T(8,128)(2,1)}) %reduce-scatter.22.cloned.1.call-update) | async-done | bytes 524304 | tf_op jit(solution)/shard_map/reduce_scatter | solution.py:318
  983.2 103.8 %reduce-scatter.18.cloned.1.call-done = bf16[128,2048]{1,0:T(8,128)(2,1)} async-done(((bf16[2048,2048]{1,0:T(8,128)(2,1)}), bf16[128,2048]{1,0:T(8,128)(2,1)}) %reduce-scatter.18.cloned.1.call-update) | async-done | bytes 524304 | tf_op jit(solution)/shard_map/reduce_scatter | solution.py:262
  1090.4 9.4 convolution_convert_fusion.6
  1110.3 8.5 convolution_convert_fusion.7
  1118.9 43.3 %all-gather.26.cloned.1.call-done = bf16[2048,2048]{1,0:T(8,128)(2,1)} async-done(((bf16[128,2048]{1,0:T(8,128)(2,1)}), bf16[2048,2048]{1,0:T(8,128)(2,1)}) %all-gather.26.cloned.1.call-update) | async-done | bytes 8388624 | tf_op jit(solution)/shard_map/all_gather | solution.py:315
  1167.9 39.4 %while.34 = (s32[]{:T(128)}, f32[2048,1,16]{0,2,1:T(8,128)S(1)}, f32[2048,1,128]{0,2,1:T(8,128)S(1)}, bf16[4,512,1,16]{1,3,2,0:T(8,128)(2,1)S(1)}, s32[4]{0:T(12...) while((s32[]{:T(128)}, f32[2048,1,16]{0,2,1:T(8,128)S(1)}, ...), condition=%wide.region_18.19_spmd.clone.clone, body=%wide.region_16.18_spmd.clone.clone.sunk | while | flops 662282240 | bytes 36940092 | solution.py:135
  1222.1 7.1 convolution_convert_fusion.8
  1234.2 39.1 %fusion.117 = (bf16[2048,24]{0,1:T(8,128)(2,1)S(1)}, bf16[48,2048]{1,0:T(8,128)(2,1)S(1)}) fusion(bf16[2048,160]{0,1:T(8,128)(2,1)S(1)} %convolution_convert_fusion.9, bf16[352,2048]{1,0:T(8,128)(2,1)S(1)} %convolution_convert_fusion.8), kind=kCustom, calls=%all-reduce-scatter.2 | all-reduce-scatter fusion | flops 1179650 | bytes 2392576
  1280.9 18.8 %reduce-scatter.30.cloned.1.call-done = bf16[16,2048]{1,0:T(8,128)(2,1)} async-done(((bf16[128,2048]{1,0:T(8,128)(2,1)}), bf16[16,2048]{1,0:T(8,128)(2,1)}) %reduce-scatter.30.cloned.1.call-update) | async-done | bytes 65552 | tf_op jit(solution)/shard_map/reduce_scatter | solution.py:393
  1301.2 40.3 %reduce-scatter.28.cloned.1.call-done = bf16[2048,48]{0,1:T(8,128)(2,1)} async-done(((bf16[2048,384]{0,1:T(8,128)(2,1)}), bf16[2048,48]{0,1:T(8,128)(2,1)}) %reduce-scatter.28.cloned.1.call-update) | async-done | bytes 196624 | tf_op jit(solution)/shard_map/reduce_scatter | solution.py:390
  1348.2 32.6 %reduce-scatter.26.cloned.1.call-done = bf16[16,2048]{1,0:T(8,128)(2,1)} async-done(((bf16[128,2048]{1,0:T(8,128)(2,1)}), bf16[16,2048]{1,0:T(8,128)(2,1)}) %reduce-scatter.26.cloned.1.call-update) | async-done | bytes 65552 | tf_op jit(solution)/shard_map/reduce_scatter | solution.py:387
  1382.3 103.4 %reduce-scatter.24.cloned.1.call-done = bf16[128,2048]{1,0:T(8,128)(2,1)} async-done(((bf16[2048,2048]{1,0:T(8,128)(2,1)}), bf16[128,2048]{1,0:T(8,128)(2,1)}) %reduce-scatter.24.cloned.1.call-update) | async-done | bytes 524304 | tf_op jit(solution)/shard_map/reduce_scatter | solution.py:318
  1487.2 64.9 %all-reduce.10 = (f32[2048]{0:T(1024)}, f32[2048]{0:T(1024)}, f32[2048]{0:T(1024)}) all-reduce(f32[2048]{0:T(1024)S(1)} %get-tuple-element.406, f32[2048]{0:T(1024)S(1)} %get-tuple-element.404, f32[2048]{0:T(1024)S(1)} %copy-done.42), channel_id=1, replica_groups=mesh['dp'=8,'head'=16] {'dp','head'}, use_global_device_ids=true, to_apply=%region_22.23 | all-reduce | flops 6144 | bytes 49152 | tf_op jit(solution)/shard_map/psum | solution.py:403
  (308 shorter events, 191.7 us)
Async XLA Ops:
  8.0 84.7 %all-gather.12.cloned.1.call-start = ((), (), s32[]{:S(2)}) async-start(), calls=%async_computation.9 | async-start | bytes 8912896 | tf_op jit(solution)/shard_map/all_gather | solution.py:272
  11.4 209.4 %reduce-scatter.14.cloned.1.call-start = ((), (), s32[]{:S(2)}) async-start(), calls=%async_computation.10 | async-start | bytes 8912896 | tf_op jit(solution)/shard_map/reduce_scatter | solution.py:262
  121.1 103.3 %copy-start.41 = (bf16[16,2048]{1,0:T(8,128)(2,1)S(1)}, bf16[16,2048]{1,0:T(8,128)(2,1)}, u32[]{:S(2)}) copy-start(bf16[16,2048]{1,0:T(8,128)(2,1)} %param.24) | copy-start | bytes 196612
  121.1 136.4 %all-gather.16.cloned.1.call-start = ((), (), s32[]{:S(2)}) async-start(), calls=%async_computation.12 | async-start | bytes 1769472 | tf_op jit(solution)/shard_map/all_gather | solution.py:253
  121.7 175.5 %all-gather.14.cloned.1.call-start = ((), (), s32[]{:S(2)}) async-start(), calls=%async_computation.11 | async-start | bytes 8912896 | tf_op jit(solution)/shard_map/all_gather | solution.py:272
  224.2 195.5 %reduce-scatter.16.cloned.1.call-start = ((), (), s32[]{:S(2)}) async-start(), calls=%async_computation.13 | async-start | bytes 8912896 | tf_op jit(solution)/shard_map/reduce_scatter | solution.py:262
  319.7 101.3 %copy-start.37 = (f32[2048]{0:T(1024)S(1)}, f32[2048]{0:T(1024)}, u32[]{:S(2)}) copy-start(f32[2048]{0:T(1024)} %param.25) | copy-start | bytes 24580
  319.7 103.5 %copy-start.45 = (s32[1,3]{1,0:T(1,128)S(1)}, s32[1,3]{1,0:T(1,128)}, u32[]{:S(2)}) copy-start(s32[1,3]{1,0:T(1,128)} %param.18) | copy-start | bytes 40
  319.7 106.1 %copy-start.7 = (bf16[128,2048]{1,0:T(8,128)(2,1)S(1)}, bf16[128,2048]{1,0:T(8,128)(2,1)}, u32[]{:S(2)}) copy-start(bf16[128,2048]{1,0:T(8,128)(2,1)} %param.17) | copy-start | bytes 1572868
  319.8 140.8 %all-gather.28.cloned.1.call-start = ((), (), s32[]{:S(2)}) async-start(), calls=%async_computation.26 | async-start | bytes 1769472 | tf_op jit(solution)/shard_map/all_gather | solution.py:256
  320.5 184.2 %all-gather.20.cloned.1.call-start = ((), (), s32[]{:S(2)}) async-start(), calls=%async_computation.15 | async-start | bytes 3244032 | tf_op jit(solution)/shard_map/all_gather | solution.py:255
  321.2 258.7 %all-gather.18.cloned.1.call-start = ((), (), s32[]{:S(2)}) async-start(), calls=%async_computation.14 | async-start | bytes 8912896 | tf_op jit(solution)/shard_map/all_gather | solution.py:272
  423.2 229.7 %all-gather.22.cloned.1.call-start = ((), (), s32[]{:S(2)}) async-start(), calls=%async_computation.17 | async-start | bytes 8912896 | tf_op jit(solution)/shard_map/all_gather | solution.py:315
  426.9 347.9 %reduce-scatter.20.cloned.1.call-start = ((), (), s32[]{:S(2)}) async-start(), calls=%async_computation.18 | async-start | bytes 8912896 | tf_op jit(solution)/shard_map/reduce_scatter | solution.py:318
  674.6 177.0 %all-gather.24.cloned.1.call-start = ((), (), s32[]{:S(2)}) async-start(), calls=%async_computation.19 | async-start | bytes 8912896 | tf_op jit(solution)/shard_map/all_gather | solution.py:315
  779.5 202.1 %reduce-scatter.22.cloned.1.call-start = ((), (), s32[]{:S(2)}) async-start(), calls=%async_computation.20 | async-start | bytes 8912896 | tf_op jit(solution)/shard_map/reduce_scatter | solution.py:318
  881.3 205.6 %reduce-scatter.18.cloned.1.call-start = ((), (), s32[]{:S(2)}) async-start(), calls=%async_computation.16 | async-start | bytes 8912896 | tf_op jit(solution)/shard_map/reduce_scatter | solution.py:262
  891.9 195.1 %copy-start.8 = (bf16[128,2048]{1,0:T(8,128)(2,1)S(1)}, bf16[128,2048]{1,0:T(8,128)(2,1)}, u32[]{:S(2)}) copy-start(bf16[128,2048]{1,0:T(8,128)(2,1)} %param.17) | copy-start | bytes 1572868
  891.9 195.1 %copy-start.9 = (bf16[128,2048]{1,0:T(8,128)(2,1)S(1)}, bf16[128,2048]{1,0:T(8,128)(2,1)}, u32[]{:S(2)}) copy-start(bf16[128,2048]{1,0:T(8,128)(2,1)} %reduce-scatter.20.cloned.1.call-done) | copy-start | bytes 1572868
  891.9 270.2 %all-gather.26.cloned.1.call-start = ((), (), s32[]{:S(2)}) async-start(), calls=%async_computation.21 | async-start | bytes 8912896 | tf_op jit(solution)/shard_map/all_gather | solution.py:315
  1090.4 188.2 %all-reduce.14.cloned.1.call-start = ((), (), s32[]{:S(2)}) async-start(), calls=%async_computation.27 | async-start | bytes 5767168
  1104.4 195.3 %reduce-scatter.30.cloned.1.call-start = ((), (), s32[]{:S(2)}) async-start(), calls=%async_computation.25 | async-start | bytes 589824 | tf_op jit(solution)/shard_map/reduce_scatter | solution.py:393
  1110.3 231.3 %reduce-scatter.28.cloned.1.call-start = ((), (), s32[]{:S(2)}) async-start(), calls=%async_computation.24 | async-start | bytes 1769472 | tf_op jit(solution)/shard_map/reduce_scatter | solution.py:390
  1118.8 261.9 %reduce-scatter.26.cloned.1.call-start = ((), (), s32[]{:S(2)}) async-start(), calls=%async_computation.23 | async-start | bytes 589824 | tf_op jit(solution)/shard_map/reduce_scatter | solution.py:387
  1212.8 272.9 %reduce-scatter.24.cloned.1.call-start = ((), (), s32[]{:S(2)}) async-start(), calls=%async_computation.22 | async-start | bytes 8912896 | tf_op jit(solution)/shard_map/reduce_scatter | solution.py:318
  1234.2 251.6 %copy-start.39 = (f32[2048]{0:T(1024)S(1)}, f32[2048]{0:T(1024)}, u32[]{:S(2)}) copy-start(f32[2048]{0:T(1024)} %param.19) | copy-start | bytes 24580
  1273.3 212.4 %copy-start.44 = (f32[128]{0:T(128)S(1)}, f32[128]{0:T(128)}, u32[]{:S(2)}) copy-start(f32[128]{0:T(128)} %copy-done.43) | copy-start | bytes 1540
  1273.3 213.9 %copy-start.42 = (f32[2048]{0:T(1024)S(1)}, f32[2048]{0:T(1024)}, u32[]{:S(2)}) copy-start(f32[2048]{0:T(1024)} %get-tuple-element.402) | copy-start | bytes 24580
  1273.3 278.7 %copy-start.10 = (f32[128,2048]{1,0:T(8,128)S(1)}, f32[128,2048]{1,0:T(8,128)}, u32[]{:S(2)}) copy-start(f32[128,2048]{1,0:T(8,128)} %get-tuple-element.456) | copy-start | bytes 3145732
  1273.4 71.2 %collective-permute-start = (bf16[2048,24]{0,1:T(8,128)(2,1)S(1)}, bf16[2048,24]{0,1:T(8,128)(2,1)S(1)}, u32[]{:S(2)}, u32[]{:S(2)}) collective-permute-start(bf16[2048,24]{0,1:T(8,128)(2,1)S(1)} %get-tuple-element.451), channel_id=1, source_target_pairs={{0,16},{16,32},{32,48},{48,64},{64,80},{80,96},{96,112},{1,17},{17... | collective-permute-start | bytes 294920
  1276.6 68.0 %collective-permute-start.1 = (bf16[2048,4]{0,1:T(4,128)(2,1)S(1)}, bf16[2048,4]{0,1:T(4,128)(2,1)S(1)}, u32[]{:S(2)}, u32[]{:S(2)}) collective-permute-start(bf16[2048,4]{0,1:T(4,128)(2,1)S(1)} %slice.149), channel_id=1, source_target_pairs={{0,32},{16,48},{32,64},{48,80},{64,96},{80,112},{1,33},{17,49},{33... | collective-permute-start | bytes 49160
  1343.2 3.8 collective-permute-start.2
  (43 other events, 789.4 us)
Sparse Core Ops, SparseCore 0:
  11.9 80.7 all-gather.11
  121.2 99.5 reduce-scatter.13
  674.7 100.0 reduce-scatter.19
  779.6 71.8 all-gather.23
  881.5 100.1 reduce-scatter.21
  985.7 101.1 reduce-scatter.17
Sparse Core Ops, SparseCore 1:
  123.2 47.8 all-gather.15
  224.3 72.8 all-gather.13
  319.8 99.8 reduce-scatter.15
  421.3 39.2 all-gather.27
  462.2 42.4 all-gather.19
  507.8 72.1 all-gather.17
  582.3 70.5 all-gather.21
  1090.5 71.6 all-gather.25
  1164.6 92.0 all-reduce.13
  1259.0 40.6 reduce-scatter.29
  1302.1 39.3 reduce-scatter.27
  1344.0 36.7 reduce-scatter.25
  1384.9 100.8 reduce-scatter.23
where the time goes:
time: 1570 us; the launch traced here: 1560 us
  waiting for transfers between devices  1070 us (68%)
  blocking collectives  198 us (13%)
  matrix products  165 us (11%)
  other arithmetic  61.1 us (4%)
  local copies, waits for them, and re-layouts  26.7 us (2%)
  between operations  18.4 us (1%)
    reduce_scatter x3, waiting for transfers between devices, project_out(): lax.psum_scatter(jnp.dot(left_side, right_side, preferred_element_type=jn...  301 us
    reduce_scatter x3, waiting for transfers between devices, gather_back(): lax.psum_scatter(contract_cols(left_side, right_side).astype(jnp.bfloat16...  293 us
    all_gather x3, waiting for transfers between devices, spread(): lax.all_gather(grad_local.astype(jnp.bfloat16), 'head', axis=0, tiled=True)  177 us
    all_gather x3, waiting for transfers between devices, share_rows(): return lax.all_gather(rows_local, 'head', axis=0, tiled=True)  129 us
    psum x1, blocking collectives, body(): lax.psum((gain_a_grad, gain_b_grad, gain_c_grad), ('dp', 'head'))  64.9 us
    dot_general x6, matrix products, contract_cols(): lax.dot_general(left_side, right_side, (((1,), (1,)), ((), ())), preferre...  43.9 us
    all_gather x1, waiting for transfers between devices, body(): lax.all_gather(mlp_in, 'dp', axis=2, tiled=True)  41.7 us
    dot_general x6, matrix products, contract_rows(): lax.dot_general(left_side, right_side, (((0,), (0,)), ((), ())), preferre...  40.9 us
  transfers between devices with their start and end apart: 22, of which 18 were waited for; matrix products, arithmetic and copies ran while one was open for 11% of the time, Pallas kernels for 0%

commit v1 on v0

v1 whole, which is shorter than its diff:
```python
import functools
import math

import jax
import jax.numpy as jnp
import numpy as np
from jax import lax
from jax.experimental import pallas as pl
from jax.experimental.pallas import tpu as pltpu
from jax.sharding import Mesh
from jax.sharding import PartitionSpec as P

FEAT = 16
HEAD_V = 128
WINDOW = 64
EPSILON = 1e-05
D = 2048
TOK = 128
HALF_TOK = 1024
EDGE = 64
UNIT_PAD = 48
BIN_PAD = 32
STATE = 256
PLANE = ("xh", "xl", "y")
RING = ("z", "c")
ALL = ("xl", "y", "xh", "z", "c")
MESH = pl.DeviceIdType.MESH
BF = jnp.bfloat16
F32 = jnp.float32
VM = pl.BlockSpec(memory_space=pltpu.VMEM)
ANY = pl.BlockSpec(memory_space=pl.ANY)


def dnn(a, b):
    return lax.dot_general(a, b, (((1,), (0,)), ((), ())), preferred_element_type=F32)


def dnt(a, b):
    return lax.dot_general(a, b, (((1,), (1,)), ((), ())), preferred_element_type=F32)


def dtn(a, b):
    return lax.dot_general(a, b, (((0,), (0,)), ((), ())), preferred_element_type=F32)


def remote(src, dst, send_sem, recv_sem, device):
    copy = pltpu.make_async_remote_copy(
        src_ref=src,
        dst_ref=dst,
        send_sem=send_sem,
        recv_sem=recv_sem,
        device_id=device,
        device_id_type=MESH,
    )
    copy.start()
    return copy


def greet(devices):
    barrier = pltpu.get_barrier_semaphore()
    for device in devices:
        pl.semaphore_signal(barrier, inc=1, device_id=device, device_id_type=MESH)
    pl.semaphore_wait(barrier, len(devices))


class Ring:
    def __init__(self):
        self.z = lax.axis_index("z")
        self.c = lax.axis_index("c")
        self.oc = 1 - self.c
        self.zp = lax.rem(self.z + 1, 4)
        self.zm = lax.rem(self.z + 3, 4)
        self.zz = lax.rem(self.z + 2, 4)
        self.up = {"z": self.zp}
        self.dn = {"z": self.zm}
        self.sib = {"c": self.oc}

    def greet(self):
        greet((self.up, self.dn, self.sib))


def gather_rows(ring, buf, out_ref, ss, rs, ls, base=0):
    half = TOK // 2
    me = ring.z * 2 + ring.c
    below, above, far = ring.zm * 2 + ring.c, ring.zp * 2 + ring.c, ring.zz * 2 + ring.c

    def send(slot, part, device, index):
        piece = buf.at[slot, pl.ds(part * half, half), :]
        return remote(piece, piece, ss.at[base + index], rs.at[base + index], device)

    local = []

    def keep(slot):
        copy = pltpu.make_async_copy(
            buf.at[slot],
            out_ref.at[pl.ds(pl.multiple_of(slot * TOK, TOK), TOK), :],
            ls.at[len(local)],
        )
        copy.start()
        local.append(copy)

    up, dn, sib = ring.up, ring.dn, ring.sib
    cp = {}
    cp[0] = send(me, 0, up, 0)
    cp[1] = send(me, 1, dn, 1)
    cp[2] = send(me, 1, up, 2)
    cp[3] = send(me, 0, dn, 3)
    cp[4] = send(me, 0, sib, 4)
    cp[5] = send(me, 1, sib, 5)
    keep(me)
    cp[0].wait_recv()
    cp[6] = send(below, 0, up, 6)
    cp[8] = send(below, 0, sib, 8)
    cp[1].wait_recv()
    cp[7] = send(above, 1, dn, 7)
    cp[9] = send(above, 1, sib, 9)
    cp[2].wait_recv()
    cp[10] = send(below, 1, sib, 10)
    keep(below)
    cp[3].wait_recv()
    cp[11] = send(above, 0, sib, 11)
    keep(above)
    cp[4].wait_recv()
    cp[5].wait_recv()
    keep(ring.z * 2 + ring.oc)
    cp[8].wait_recv()
    cp[10].wait_recv()
    keep(ring.zm * 2 + ring.oc)
    cp[9].wait_recv()
    cp[11].wait_recv()
    keep(ring.zp * 2 + ring.oc)
    cp[6].wait_recv()
    cp[12] = send(far, 0, sib, 12)
    cp[7].wait_recv()
    cp[13] = send(far, 1, sib, 13)
    keep(far)
    cp[12].wait_recv()
    cp[13].wait_recv()
    keep(ring.zz * 2 + ring.oc)
    for index in range(14):
        cp[index].wait_send()
    for copy in local:
        copy.wait()


def scatter_sum(ring, a_ref, w_ref, part, sib_in, far_in, end_in, ss, rs, base=0):
    half = TOK // 2
    c, oc = ring.c, ring.oc
    up, dn, sib = ring.up, ring.dn, ring.sib
    order = (ring.zz, ring.zp, ring.zm, ring.z)
    step = 512

    def multiply(index):
        row = pl.multiple_of(order[index] * (2 * TOK), 2 * TOK)

        def one(n, carry):
            col = pl.ds(pl.multiple_of(n * step, step), step)
            res = dnn(a_ref[pl.ds(row, 2 * TOK), :], w_ref[:, col]).astype(BF)
            part[index, 0, :, col] = res[:TOK]
            part[index, 1, :, col] = res[TOK:]
            return carry

        lax.fori_loop(0, D // step, one, 0)
        return remote(
            part.at[index, oc], sib_in.at[index], ss.at[base + index], rs.at[base + index], sib
        )

    def add(index, rows_start, rows, other):
        def one(i, carry):
            at = pl.ds(pl.multiple_of(rows_start + i * 16, 16), 16)
            part[index, c, at, :] = (part[index, c, at, :].astype(F32) + other(i, at)).astype(BF)
            return carry

        lax.fori_loop(0, rows // 16, one, 0)

    def add_sib(index):
        add(index, 0, TOK, lambda i, at: sib_in[index, at, :].astype(F32))

    def send(src, dst, device, index):
        return remote(src, dst, ss.at[base + index], rs.at[base + index], device)

    low, high = pl.ds(0, half), pl.ds(half, half)
    cp = {}
    cp[0] = multiply(0)
    cp[1] = multiply(1)
    cp[0].wait_recv()
    add_sib(0)
    cp[4] = send(part.at[0, c, low, :], far_in.at[0], up, 4)
    cp[5] = send(part.at[0, c, high, :], far_in.at[1], dn, 5)
    cp[2] = multiply(2)
    cp[1].wait_recv()
    add_sib(1)
    cp[6] = send(part.at[1, c, high, :], end_in.at[0, high, :], up, 6)
    cp[3] = multiply(3)
    cp[2].wait_recv()
    add_sib(2)
    cp[7] = send(part.at[2, c, low, :], end_in.at[1, low, :], dn, 7)
    cp[4].wait_recv()
    add(1, 0, half, lambda i, at: far_in[0, pl.ds(pl.multiple_of(i * 16, 16), 16), :].astype(F32))
    cp[8] = send(part.at[1, c, low, :], end_in.at[0, low, :], up, 8)
    cp[5].wait_recv()
    add(2, half, half, lambda i, at: far_in[1, pl.ds(pl.multiple_of(i * 16, 16), 16), :].astype(F32))
    cp[9] = send(part.at[2, c, high, :], end_in.at[1, high, :], dn, 9)
    cp[3].wait_recv()
    add_sib(3)
    cp[6].wait_recv()
    cp[7].wait_recv()
    cp[8].wait_recv()
    cp[9].wait_recv()
    return cp


SCATTER_SCRATCH = [
    pltpu.VMEM((4, 2, TOK, D), BF),
    pltpu.VMEM((4, TOK, D), BF),
    pltpu.VMEM((2, TOK // 2, D), BF),
    pltpu.VMEM((2, TOK, D), BF),
]


def params(collective_id, limit=48):
    return pltpu.CompilerParams(
        collective_id=collective_id, has_side_effects=True, vmem_limit_bytes=limit << 20
    )


def scale_of(rows):
    return lax.rsqrt(jnp.mean(rows * rows, axis=-1, keepdims=True) + EPSILON)


def first_kernel(x_ref, gain_ref, out_ref, buf, ss, rs, ls):
    ring = Ring()
    me = ring.z * 2 + ring.c

    def one(i, carry):
        at = pl.ds(pl.multiple_of(i * 16, 16), 16)
        rows = x_ref[at, :].astype(F32)
        buf[me, at, :] = (rows * scale_of(rows) * gain_ref[...]).astype(BF)
        return carry

    lax.fori_loop(0, TOK // 16, one, 0)
    ring.greet()
    gather_rows(ring, buf, out_ref, ss, rs, ls)


def first_gather(x, gain):
    return pl.pallas_call(
        first_kernel,
        out_shape=jax.ShapeDtypeStruct((HALF_TOK, D), BF),
        in_specs=[VM, VM],
        out_specs=ANY,
        scratch_shapes=[
            pltpu.VMEM((8, TOK, D), BF),
            pltpu.SemaphoreType.DMA((14,)),
            pltpu.SemaphoreType.DMA((14,)),
            pltpu.SemaphoreType.DMA((8,)),
        ],
        compiler_params=params(1),
    )(x, gain)


def total_rows(part, end_in, c, at):
    return (
        part[3, c, at, :].astype(F32)
        + end_in[0, at, :].astype(F32)
        + end_in[1, at, :].astype(F32)
    )


def forward_kernel(
    a_ref, w_ref, x_ref, gain_ref, x_out, h_out, part, sib_in, far_in, end_in, buf, ss, rs, ls
):
    ring = Ring()
    me = ring.z * 2 + ring.c
    ring.greet()
    cp = scatter_sum(ring, a_ref, w_ref, part, sib_in, far_in, end_in, ss, rs)

    def one(i, carry):
        at = pl.ds(pl.multiple_of(i * 16, 16), 16)
        rows = x_ref[at, :].astype(F32) + total_rows(part, end_in, ring.c, at)
        x_out[at, :] = rows
        buf[me, at, :] = (rows * scale_of(rows) * gain_ref[...]).astype(BF)
        return carry

    lax.fori_loop(0, TOK // 16, one, 0)
    gather_rows(ring, buf, h_out, ss, rs, ls, base=10)
    for index in range(10):
        cp[index].wait_send()


def forward_step(a, w, x, gain, collective_id):
    return pl.pallas_call(
        forward_kernel,
        out_shape=(
            jax.ShapeDtypeStruct((TOK, D), F32),
            jax.ShapeDtypeStruct((HALF_TOK, D), BF),
        ),
        in_specs=[VM] * 4,
        out_specs=(VM, ANY),
        scratch_shapes=SCATTER_SCRATCH
        + [
            pltpu.VMEM((8, TOK, D), BF),
            pltpu.SemaphoreType.DMA((24,)),
            pltpu.SemaphoreType.DMA((24,)),
            pltpu.SemaphoreType.DMA((8,)),
        ],
        compiler_params=params(collective_id),
    )(a, w, x, gain)


def norm_back_rows(v_ref, gain_ref, grads, at, gain_acc):
    rows = v_ref[at, :].astype(F32)
    scale = scale_of(rows)
    unit = rows * scale
    gain_acc[...] += grads * unit
    scaled = grads * gain_ref[...]
    return scale * (scaled - unit * jnp.mean(scaled * unit, axis=-1, keepdims=True))


def backward_kernel(
    a_ref,
    w_ref,
    v_ref,
    gain_ref,
    d_ref,
    d_out,
    gain_out,
    e_out,
    part,
    sib_in,
    far_in,
    end_in,
    gain_acc,
    buf,
    ss,
    rs,
    ls,
):
    ring = Ring()
    me = ring.z * 2 + ring.c
    ring.greet()
    gain_acc[...] = jnp.zeros_like(gain_acc)
    cp = scatter_sum(ring, a_ref, w_ref, part, sib_in, far_in, end_in, ss, rs)

    def one(i, carry):
        at = pl.ds(pl.multiple_of(i * 16, 16), 16)
        grads = total_rows(part, end_in, ring.c, at)
        rows = d_ref[at, :] + norm_back_rows(v_ref, gain_ref, grads, at, gain_acc)
        d_out[at, :] = rows
        buf[me, at, :] = rows.astype(BF)
        return carry

    lax.fori_loop(0, TOK // 16, one, 0)
    gain_out[...] = jnp.sum(gain_acc[...], axis=0, keepdims=True)
    gather_rows(ring, buf, e_out, ss, rs, ls, base=10)
    for index in range(10):
        cp[index].wait_send()


def backward_step(a, w, v, gain, d, collective_id):
    return pl.pallas_call(
        backward_kernel,
        out_shape=(
            jax.ShapeDtypeStruct((TOK, D), F32),
            jax.ShapeDtypeStruct((1, D), F32),
            jax.ShapeDtypeStruct((HALF_TOK, D), BF),
        ),
        in_specs=[VM] * 5,
        out_specs=(VM, VM, ANY),
        scratch_shapes=SCATTER_SCRATCH
        + [
            pltpu.VMEM((16, D), F32),
            pltpu.VMEM((8, TOK, D), BF),
            pltpu.SemaphoreType.DMA((24,)),
            pltpu.SemaphoreType.DMA((24,)),
            pltpu.SemaphoreType.DMA((8,)),
        ],
        compiler_params=params(collective_id),
    )(a, w, v, gain, d)


def last_kernel(
    a_ref, w_ref, v_ref, gain_ref, d_ref, d_out, gain_out, part, sib_in, far_in, end_in, gain_acc, ss, rs
):
    ring = Ring()
    ring.greet()
    gain_acc[...] = jnp.zeros_like(gain_acc)
    cp = scatter_sum(ring, a_ref, w_ref, part, sib_in, far_in, end_in, ss, rs)

    def one(i, carry):
        at = pl.ds(pl.multiple_of(i * 16, 16), 16)
        grads = total_rows(part, end_in, ring.c, at)
        d_out[at, :] = d_ref[at, :] + norm_back_rows(v_ref, gain_ref, grads, at, gain_acc)
        return carry

    lax.fori_loop(0, TOK // 16, one, 0)
    gain_out[...] = jnp.sum(gain_acc[...], axis=0, keepdims=True)
    for index in range(10):
        cp[index].wait_send()


def last_step(a, w, v, gain, d):
    return pl.pallas_call(
        last_kernel,
        out_shape=(jax.ShapeDtypeStruct((TOK, D), F32), jax.ShapeDtypeStruct((1, D), F32)),
        in_specs=[VM] * 5,
        out_specs=(VM, VM),
        scratch_shapes=SCATTER_SCRATCH
        + [
            pltpu.VMEM((16, D), F32),
            pltpu.SemaphoreType.DMA((10,)),
            pltpu.SemaphoreType.DMA((10,)),
        ],
        compiler_params=params(6),
    )(a, w, v, gain, d)


def state_tables():
    first = np.zeros((128, STATE), np.float32)
    second = np.zeros((128, STATE), np.float32)
    bias = np.zeros((8, STATE), np.float32)
    coef = np.zeros((8, STATE), np.float32)
    bias[0, 0] = bias[1, 0] = 1.0
    coef[0, 0] = 1.0
    at = 1
    for i in range(FEAT):
        first[i, at] = 1.0
        bias[1, at] = 1.0
        coef[0, at] = 1.0 / math.sqrt(FEAT)
        at += 1
    for i in range(FEAT):
        for j in range(i, FEAT):
            first[i, at] = 1.0
            second[j, at] = 1.0
            coef[0, at] = (0.5 if i == j else 1.0) / FEAT
            at += 1
    picks = np.zeros((4, 128, 128), np.float32)
    for which in range(4):
        for i in range(FEAT):
            picks[which, which * FEAT + i, i] = 1.0
    return (
        np.stack([first, second]),
        np.concatenate([bias[:2], coef[:1], np.zeros((5, STATE), np.float32)]),
        picks,
    )


def causal_mask(row_start, col_start, rows, cols, edge):
    t = row_start + lax.broadcasted_iota(jnp.int32, (rows, cols), 0)
    u = col_start + lax.broadcasted_iota(jnp.int32, (rows, cols), 1)
    return (u <= t) & ((t >= edge) == (u >= edge))


BLK = 256
NBLK = HALF_TOK // BLK
INV_ROOT = 1.0 / math.sqrt(FEAT)


def linear_forward_kernel(
    p_ref, e_ref, t_ref, pick_ref, y_ref, sv_ref, sn_ref, qs, ks, num, den, sv_s, sn_s, sv_r, sn_r, ss, rs
):
    xh = lax.axis_index("xh")
    partner = {"xh": 1 - xh}
    edge = jnp.where(xh == 0, EDGE, HALF_TOK - EDGE)
    bias1, bias2, coef = t_ref[0:1, :], t_ref[1:2, :], t_ref[2:3, :]
    small = p_ref[:, 2 * HEAD_V :]
    for j in range(2):
        qs[j] = dnn(small, pick_ref[2 * j]).astype(BF)
        ks[j] = dnn(small, pick_ref[2 * j + 1]).astype(BF)

    def rows_of(r):
        return slice(r * BLK, (r + 1) * BLK)

    def phi_of(vecs):
        return (dnn(vecs, e_ref[0]) + bias1) * (dnn(vecs, e_ref[1]) + bias2)

    for j in range(2):
        sv = jnp.zeros((HEAD_V, STATE), F32)
        sn = jnp.zeros((1, STATE), F32)
        for r in range(NBLK):
            phi = phi_of(ks[j, rows_of(r), :])
            if r == 0:
                slot = lax.broadcasted_iota(jnp.int32, (BLK, STATE), 0)
                phi = jnp.where(slot >= EDGE, phi, 0.0)
            sv = sv + dtn(p_ref[rows_of(r), j * HEAD_V : (j + 1) * HEAD_V], phi.astype(BF))
            sn = sn + jnp.sum(phi, axis=0, keepdims=True)
        sv_s[j] = (sv * coef).astype(BF)
        sn_s[j] = jnp.broadcast_to(sn * coef, (8, STATE))
    greet((partner,))
    copies = (
        remote(sv_s, sv_r, ss.at[0], rs.at[0], partner),
        remote(sn_s, sn_r, ss.at[1], rs.at[1], partner),
    )
    for j in range(2):
        for r in range(NBLK):
            queries = qs[j, rows_of(r), :]
            rows_num = jnp.zeros((BLK, HEAD_V), F32)
            rows_den = jnp.zeros((BLK, 1), F32)
            for s in range(r + 1):
                scores = dnt(queries, ks[j, rows_of(s), :]) * INV_ROOT
                mask = causal_mask(r * BLK, s * BLK, BLK, BLK, edge)
                kernel = jnp.where(mask, 1.0 + scores + 0.5 * scores * scores, 0.0)
                rows_den = rows_den + jnp.sum(kernel, axis=-1, keepdims=True)
                rows_num = rows_num + dnn(
                    kernel.astype(BF), p_ref[rows_of(s), j * HEAD_V : (j + 1) * HEAD_V]
                )
            num[j, rows_of(r), :] = rows_num
            den[j, rows_of(r), :] = jnp.broadcast_to(rows_den, (BLK, HEAD_V))
    for copy in copies:
        copy.wait_recv()
    sv_ref[...] = sv_r[...]
    sn_ref[...] = sn_r[...]
    for j in range(2):
        for r in range(NBLK):
            phi = phi_of(qs[j, rows_of(r), :])
            cross_den = jnp.sum(phi * sn_r[j, 0:1, :], axis=-1, keepdims=True)
            cross_num = dnt(phi.astype(BF), sv_r[j])
            slot = r * BLK + lax.broadcasted_iota(jnp.int32, (BLK, HEAD_V), 0)
            seen = (slot < HALF_TOK - EDGE) & (xh == 1)
            top = num[j, rows_of(r), :] + jnp.where(seen, cross_num, 0.0)
            bottom = den[j, rows_of(r), :] + jnp.where(seen, cross_den, 0.0)
            y_ref[rows_of(r), j * HEAD_V : (j + 1) * HEAD_V] = (top / bottom).astype(BF)
    for copy in copies:
        copy.wait_send()


def linear_forward(p1, tables):
    return pl.pallas_call(
        linear_forward_kernel,
        out_shape=(
            jax.ShapeDtypeStruct((HALF_TOK, 2 * HEAD_V), BF),
            jax.ShapeDtypeStruct((2, HEAD_V, STATE), BF),
            jax.ShapeDtypeStruct((2, 8, STATE), F32),
        ),
        in_specs=[VM] * 4,
        out_specs=(VM, VM, VM),
        scratch_shapes=[
            pltpu.VMEM((2, HALF_TOK, 128), BF),
            pltpu.VMEM((2, HALF_TOK, 128), BF),
            pltpu.VMEM((2, HALF_TOK, HEAD_V), F32),
            pltpu.VMEM((2, HALF_TOK, HEAD_V), F32),
            pltpu.VMEM((2, HEAD_V, STATE), BF),
            pltpu.VMEM((2, 8, STATE), F32),
            pltpu.VMEM((2, HEAD_V, STATE), BF),
            pltpu.VMEM((2, 8, STATE), F32),
            pltpu.SemaphoreType.DMA((2,)),
            pltpu.SemaphoreType.DMA((2,)),
        ],
        compiler_params=params(7),
    )(p1, *tables)


def linear_backward_kernel(
    p_ref,
    dy_ref,
    sv_ref,
    sn_ref,
    e_ref,
    t_ref,
    pick_ref,
    dp_ref,
    qs,
    ks,
    dq,
    dk,
    dv,
    tv_s,
    tn_s,
    tv_r,
    tn_r,
    ss,
    rs,
):
    xh = lax.axis_index("xh")
    partner = {"xh": 1 - xh}
    edge = jnp.where(xh == 0, EDGE, HALF_TOK - EDGE)
    bias1, bias2, coef = t_ref[0:1, :], t_ref[1:2, :], t_ref[2:3, :]
    small = p_ref[:, 2 * HEAD_V :]
    for j in range(2):
        qs[j] = dnn(small, pick_ref[2 * j]).astype(BF)
        ks[j] = dnn(small, pick_ref[2 * j + 1]).astype(BF)
    dk[...] = jnp.zeros_like(dk)
    dv[...] = jnp.zeros_like(dv)

    def rows_of(r):
        return slice(r * BLK, (r + 1) * BLK)

    def factors_of(vecs):
        return (dnn(vecs, e_ref[0]) + bias1, dnn(vecs, e_ref[1]) + bias2)

    def factors_back(phi_grad, one, two):
        return dnt((phi_grad * two).astype(BF), e_ref[0]) + dnt(
            (phi_grad * one).astype(BF), e_ref[1]
        )

    for j in range(2):
        head = slice(j * HEAD_V, (j + 1) * HEAD_V)
        tv = jnp.zeros((HEAD_V, STATE), F32)
        tn = jnp.zeros((1, STATE), F32)
        for r in range(NBLK):
            queries = qs[j, rows_of(r), :]
            grads = dy_ref[rows_of(r), head]
            one, two = factors_of(queries)
            phi = one * two
            slot = r * BLK + lax.broadcasted_iota(jnp.int32, (BLK, 1), 0)
            seen = (slot < HALF_TOK - EDGE) & (xh == 1)
            cross_den = jnp.sum(phi * sn_ref[j, 0:1, :], axis=-1, keepdims=True)
            cross_num = dnt(phi.astype(BF), sv_ref[j])
            total = jnp.where(seen, cross_den, 0.0)
            dot = jnp.where(
                seen, jnp.sum(cross_num * grads.astype(F32), axis=-1, keepdims=True), 0.0
            )
            kept = []
            for s in range(r + 1):
                scores = dnt(queries, ks[j, rows_of(s), :]) * INV_ROOT
                mask = causal_mask(r * BLK, s * BLK, BLK, BLK, edge)
                kernel = jnp.where(mask, 1.0 + scores + 0.5 * scores * scores, 0.0)
                weight_grad = dnt(grads, p_ref[rows_of(s), head])
                total = total + jnp.sum(kernel, axis=-1, keepdims=True)
                dot = dot + jnp.sum(kernel * weight_grad, axis=-1, keepdims=True)
                kept.append((scores, mask, kernel, weight_grad))
            inverse = 1.0 / total
            mean = dot * inverse
            grads_n = (grads.astype(F32) * inverse).astype(BF)
            query_grad = jnp.zeros((BLK, 128), F32)
            for s in range(r + 1):
                scores, mask, kernel, weight_grad = kept[s]
                score_grad = jnp.where(
                    mask, (weight_grad - mean) * inverse * (1.0 + scores), 0.0
                ).astype(BF)
                query_grad = query_grad + dnn(score_grad, ks[j, rows_of(s), :])
                dk[j, rows_of(s), :] += dtn(score_grad, queries)
                dv[j, rows_of(s), :] += dtn(kernel.astype(BF), grads_n)
            shift = jnp.where(seen, -(mean * inverse), 0.0)
            cross_g = jnp.where(seen, grads_n, jnp.zeros_like(grads_n))
            phi_grad = dnn(cross_g, sv_ref[j]) + shift * sn_ref[j, 0:1, :]
            dq[j, rows_of(r), :] = query_grad * INV_ROOT + factors_back(phi_grad, one, two)
            tv = tv + dtn(cross_g, phi.astype(BF))
            tn = tn + jnp.sum(shift * phi, axis=0, keepdims=True)
        tv_s[j] = (tv * coef).astype(BF)
        tn_s[j] = jnp.broadcast_to(tn * coef, (8, STATE))
    greet((partner,))
    copies = (
        remote(tv_s, tv_r, ss.at[0], rs.at[0], partner),
        remote(tn_s, tn_r, ss.at[1], rs.at[1], partner),
    )
    for copy in copies:
        copy.wait_recv()
    for r in range(NBLK):
        placed = jnp.zeros((BLK, 128), F32)
        for j in range(2):
            head = slice(j * HEAD_V, (j + 1) * HEAD_V)
            one, two = factors_of(ks[j, rows_of(r), :])
            phi = one * two
            if r == 0:
                slot = lax.broadcasted_iota(jnp.int32, (BLK, STATE), 0)
                open_rows = slot >= EDGE
                phi = jnp.where(open_rows, phi, 0.0)
            phi_grad = dnn(p_ref[rows_of(r), head], tv_r[j]) + tn_r[j, 0:1, :]
            if r == 0:
                phi_grad = jnp.where(open_rows, phi_grad, 0.0)
            key_grad = dk[j, rows_of(r), :] * INV_ROOT + factors_back(phi_grad, one, two)
            value_grad = dv[j, rows_of(r), :] + dnt(phi.astype(BF), tv_r[j])
            dp_ref[rows_of(r), head] = value_grad.astype(BF)
            placed = placed + dnt(dq[j, rows_of(r), :].astype(BF), pick_ref[2 * j])
            placed = placed + dnt(key_grad.astype(BF), pick_ref[2 * j + 1])
        dp_ref[rows_of(r), 2 * HEAD_V :] = placed.astype(BF)
    for copy in copies:
        copy.wait_send()


def linear_backward(p1, dy, sv, sn, tables):
    return pl.pallas_call(
        linear_backward_kernel,
        out_shape=jax.ShapeDtypeStruct((HALF_TOK, 3 * HEAD_V), BF),
        in_specs=[VM] * 7,
        out_specs=VM,
        scratch_shapes=[
            pltpu.VMEM((2, HALF_TOK, 128), BF),
            pltpu.VMEM((2, HALF_TOK, 128), BF),
            pltpu.VMEM((2, HALF_TOK, 128), F32),
            pltpu.VMEM((2, HALF_TOK, 128), F32),
            pltpu.VMEM((2, HALF_TOK, HEAD_V), F32),
            pltpu.VMEM((2, HEAD_V, STATE), BF),
            pltpu.VMEM((2, 8, STATE), F32),
            pltpu.VMEM((2, HEAD_V, STATE), BF),
            pltpu.VMEM((2, 8, STATE), F32),
            pltpu.SemaphoreType.DMA((2,)),
            pltpu.SemaphoreType.DMA((2,)),
        ],
        compiler_params=params(8),
    )(p1, dy, sv, sn, *tables)


WBLK = 128
WKEYS = WBLK + WINDOW
INV_ROOT_V = 1.0 / math.sqrt(HEAD_V)


def window_mask(r, edge, lowest):
    t = r * WBLK + lax.broadcasted_iota(jnp.int32, (WBLK, WKEYS), 0)
    u = r * WBLK - WINDOW + lax.broadcasted_iota(jnp.int32, (WBLK, WKEYS), 1)
    return (u <= t) & (t - u < WINDOW) & ((t >= edge) == (u >= edge)) & (u >= lowest)


def window_forward_kernel(p_ref, cos_ref, sin_ref, y_ref, q_ref, kv_ref, ss, rs):
    xh = lax.axis_index("xh")
    partner = {"xh": 1 - xh}
    edge = jnp.where(xh == 0, EDGE, HALF_TOK - EDGE)
    lowest = jnp.where(xh == 0, 0, -WINDOW)

    def turned(r, part):
        rows = slice(r * WBLK, (r + 1) * WBLK)
        vecs = p_ref[rows, part * 128 : (part + 1) * 128]
        return (
            vecs * cos_ref[rows, :] + pltpu.roll(vecs, HEAD_V // 2, 1) * sin_ref[rows, :]
        ).astype(BF)

    blocks = HALF_TOK // WBLK
    for r in (blocks - 1,) + tuple(range(blocks - 1)):
        rows = slice(r * WBLK, (r + 1) * WBLK)
        shifted = slice(WINDOW + r * WBLK, WINDOW + (r + 1) * WBLK)
        for j in range(2):
            q_ref[rows, j * 128 : (j + 1) * 128] = turned(r, 3 * j)
            kv_ref[shifted, j * 128 : (j + 1) * 128] = turned(r, 3 * j + 1)
            kv_ref[shifted, (2 + j) * 128 : (3 + j) * 128] = p_ref[
                rows, (3 * j + 2) * 128 : (3 * j + 3) * 128
            ].astype(BF)
        if r == blocks - 1:
            greet((partner,))
            copy = remote(
                kv_ref.at[pl.ds(HALF_TOK, WINDOW), :],
                kv_ref.at[pl.ds(0, WINDOW), :],
                ss,
                rs,
                partner,
            )
    for r in tuple(range(1, blocks)) + (0,):
        if r == 0:
            copy.wait_recv()
        rows = slice(r * WBLK, (r + 1) * WBLK)
        keys = slice(r * WBLK, r * WBLK + WKEYS)
        mask = window_mask(r, edge, lowest)
        for j in range(2):
            head = slice(j * 128, (j + 1) * 128)
            scores = dnt(q_ref[rows, head], kv_ref[keys, head]) * INV_ROOT_V
            scores = jnp.where(mask, scores, -1e30)
            exps = jnp.exp(scores - jnp.max(scores, axis=-1, keepdims=True))
            probs = exps / jnp.sum(exps, axis=-1, keepdims=True)
            y_ref[rows, head] = dnn(
                probs.astype(BF), kv_ref[keys, (2 + j) * 128 : (3 + j) * 128]
            ).astype(BF)
    copy.wait_send()


def window_forward(p2, cosine, sine):
    return pl.pallas_call(
        window_forward_kernel,
        out_shape=(
            jax.ShapeDtypeStruct((HALF_TOK, 256), BF),
            jax.ShapeDtypeStruct((HALF_TOK, 256), BF),
            jax.ShapeDtypeStruct((HALF_TOK + WINDOW, 512), BF),
        ),
        in_specs=[VM] * 3,
        out_specs=(VM, VM, VM),
        scratch_shapes=[pltpu.SemaphoreType.DMA, pltpu.SemaphoreType.DMA],
        compiler_params=params(9),
    )(p2, cosine, sine)


def window_backward_kernel(
    q_ref, kv_ref, dy_ref, cos_ref, sin_ref, dp_ref, dkv, halo, ss, rs
):
    xh = lax.axis_index("xh")
    partner = {"xh": 1 - xh}
    edge = jnp.where(xh == 0, EDGE, HALF_TOK - EDGE)
    lowest = jnp.where(xh == 0, 0, -WINDOW)
    dkv[...] = jnp.zeros_like(dkv)
    blocks = HALF_TOK // WBLK

    def turned_back(r, grads):
        rows = slice(r * WBLK, (r + 1) * WBLK)
        return (
            grads * cos_ref[rows, :] + pltpu.roll(grads * sin_ref[rows, :], HEAD_V // 2, 1)
        ).astype(BF)

    for r in range(blocks):
        rows = slice(r * WBLK, (r + 1) * WBLK)
        keys = slice(r * WBLK, r * WBLK + WKEYS)
        mask = window_mask(r, edge, lowest)
        for j in range(2):
            head = slice(j * 128, (j + 1) * 128)
            vals = slice((2 + j) * 128, (3 + j) * 128)
            queries, grads = q_ref[rows, head], dy_ref[rows, head]
            scores = dnt(queries, kv_ref[keys, head]) * INV_ROOT_V
            scores = jnp.where(mask, scores, -1e30)
            exps = jnp.exp(scores - jnp.max(scores, axis=-1, keepdims=True))
            probs = exps / jnp.sum(exps, axis=-1, keepdims=True)
            prob_grad = dnt(grads, kv_ref[keys, vals])
            score_grad = (
                probs * (prob_grad - jnp.sum(prob_grad * probs, axis=-1, keepdims=True))
            ).astype(BF)
            dp_ref[rows, 3 * j * 128 : (3 * j + 1) * 128] = turned_back(
                r, dnn(score_grad, kv_ref[keys, head]) * INV_ROOT_V
            )
            dkv[keys, head] += dtn(score_grad, queries) * INV_ROOT_V
            dkv[keys, vals] += dtn(probs.astype(BF), grads)
        if r == 0:
            greet((partner,))
            copy = remote(dkv.at[pl.ds(0, WINDOW), :], halo, ss, rs, partner)
    for r in range(blocks):
        rows = slice(r * WBLK, (r + 1) * WBLK)
        shifted = slice(WINDOW + r * WBLK, WINDOW + (r + 1) * WBLK)
        if r == blocks - 1:
            copy.wait_recv()
            dkv[HALF_TOK : HALF_TOK + WINDOW, :] += halo[...]
        for j in range(2):
            dp_ref[rows, (3 * j + 1) * 128 : (3 * j + 2) * 128] = turned_back(
                r, dkv[shifted, j * 128 : (j + 1) * 128]
            )
            dp_ref[rows, (3 * j + 2) * 128 : (3 * j + 3) * 128] = dkv[
                shifted, (2 + j) * 128 : (3 + j) * 128
            ].astype(BF)
    copy.wait_send()


def window_backward(q, kv, dy, cosine, sine):
    return pl.pallas_call(
        window_backward_kernel,
        out_shape=jax.ShapeDtypeStruct((HALF_TOK, 768), BF),
        in_specs=[VM] * 5,
        out_specs=VM,
        scratch_shapes=[
            pltpu.VMEM((HALF_TOK + WINDOW, 512), F32),
            pltpu.VMEM((WINDOW, 512), F32),
            pltpu.SemaphoreType.DMA,
            pltpu.SemaphoreType.DMA,
        ],
        compiler_params=params(10),
    )(q, kv, dy, cosine, sine)


def plane_gather(rows):
    return lax.all_gather(rows, PLANE, axis=0, tiled=True)


def plane_reduce(rows):
    return lax.psum_scatter(rows.astype(BF), PLANE, scatter_dimension=0, tiled=True).astype(F32)


def padded(rows, count):
    return jnp.pad(rows, ((0, count - rows.shape[0]), (0, 0)))


def place():
    slot = lax.axis_index("xh") * HALF_TOK + jnp.arange(HALF_TOK, dtype=jnp.int32)
    last = 2 * HALF_TOK - EDGE
    segment = (slot >= EDGE).astype(jnp.int32) + (slot >= last).astype(jnp.int32)
    start = jnp.where(segment == 0, 0, jnp.where(segment == 1, EDGE, last)).astype(jnp.int32)
    return segment, slot - start


def body(
    block_input,
    cotangent,
    lengths,
    gain_a,
    based_in,
    based_out,
    gain_b,
    swa_in,
    swa_out,
    gain_c,
    mlp_in,
    mlp_down,
):
    gains = [gain.reshape(1, D) for gain in (gain_a, gain_b, gain_c)]
    units = mlp_down.shape[0]
    wide = based_in.shape[1]
    segment, position = place()
    first = (lax.axis_index("z") * 2 + lax.axis_index("c")) * TOK
    my_segment = lax.dynamic_slice_in_dim(segment, first, TOK)
    my_position = lax.dynamic_slice_in_dim(position, first, TOK)
    chosen = jnp.where(
        my_segment == 0,
        lengths[0, 0],
        jnp.where(my_segment == 1, lengths[0, 1], lengths[0, 2]),
    )
    valid = (my_position < chosen).astype(F32)
    cot_local = cotangent.astype(F32) * valid[:, None]
    frequency = jnp.exp(
        -math.log(10000.0) * jnp.arange(HEAD_V // 2, dtype=F32) * 2.0 / HEAD_V
    )
    angles = position.astype(F32)[:, None] * frequency[None, :]
    cosine, sine = jnp.cos(angles), jnp.sin(angles)
    cosine = jnp.concatenate([cosine, cosine], axis=1)
    sine = jnp.concatenate([-sine, sine], axis=1)

    lin_all = plane_gather(jnp.concatenate([padded(based_in.T, BIN_PAD), based_out], axis=0))
    win_all = plane_gather(jnp.concatenate([swa_in.T, swa_out], axis=0))
    ff_all = plane_gather(
        jnp.concatenate(
            [padded(part, UNIT_PAD) for part in (mlp_in[:, 0, :].T, mlp_in[:, 1, :].T, mlp_down)],
            axis=0,
        )
    )

    def pieces(rows, *counts):
        rows = rows.reshape(16, sum(counts), D)
        ends = np.cumsum((0,) + counts)
        return [
            rows[:, ends[i] : ends[i + 1]].reshape(16 * counts[i], D) for i in range(len(counts))
        ]

    lin_rows, lin_out = pieces(lin_all, BIN_PAD, 16)
    win_in, win_out = pieces(win_all, 48, 16)
    ff_gate, ff_up, ff_out = pieces(ff_all, UNIT_PAD, UNIT_PAD, UNIT_PAD)
    lin_heads = lin_rows.reshape(16, BIN_PAD, D)[:, :wide].reshape(2, 8 * wide, D)
    lin_in = jnp.concatenate(
        [
            lin_heads[:, 2 * FEAT :].reshape(2 * HEAD_V, D),
            lin_heads[:, : 2 * FEAT].reshape(4 * FEAT, D),
            jnp.zeros((128 - 4 * FEAT, D), BF),
        ],
        axis=0,
    )
    table_e, table_t, table_p = state_tables()
    tables = (jnp.asarray(table_e, BF), jnp.asarray(table_t, F32), jnp.asarray(table_p, BF))

    h1 = first_gather(block_input, gains[0])
    cot_all = lax.all_gather(cot_local.astype(BF), RING, axis=0, tiled=True)
    p1 = dnt(h1, lin_in).astype(BF)
    y1, state_v, state_n = linear_forward(p1, tables)
    x2, h2 = forward_step(y1, lin_out, block_input, gains[1], 2)
    p2 = dnt(h2, win_in)
    y2, queries, key_vals = window_forward(p2, cosine, sine)
    x3, h3 = forward_step(y2, win_out, x2, gains[2], 3)
    gate = dnt(h3, ff_gate)
    up = dnt(h3, ff_up)
    sig = jax.nn.sigmoid(gate)
    act = (gate * sig * up).astype(BF)
    out_sum = lax.psum_scatter(dnn(act, ff_out).astype(BF), RING, scatter_dimension=0, tiled=True)
    block_output = (x3 + out_sum.astype(F32)).astype(BF)

    d_act = dnt(cot_all, ff_out)
    d_gate = (d_act * up * sig * (1.0 + gate * (1.0 - sig))).astype(BF)
    d_up = (d_act * gate * sig).astype(BF)
    d_gu = jnp.concatenate([d_gate, d_up], axis=1)
    ff_in = jnp.concatenate([ff_gate, ff_up], axis=0)

    def reduce_together(*grads):
        rows = [grad.astype(BF).reshape(16, -1, D) for grad in grads]
        ends = np.cumsum([0] + [part.shape[1] for part in rows])
        total = plane_reduce(jnp.concatenate(rows, axis=1).reshape(-1, D))
        return [total[ends[i] : ends[i + 1]] for i in range(len(rows))]

    grad_down, grad_gate, grad_up = reduce_together(
        dtn(act, cot_all), dtn(d_gate, h3), dtn(d_up, h3)
    )
    dx3, grad_c, e3 = backward_step(d_gu, ff_in, x3, gains[2], cot_local, 4)
    d_y2 = dnt(e3, win_out).astype(BF)
    grad_win_out = dtn(y2, e3)
    d_p2 = window_backward(queries, key_vals, d_y2, cosine, sine)
    grad_win_in = dtn(d_p2, h2)
    dx2, grad_b, e2 = backward_step(d_p2, win_in, x2, gains[1], dx3, 5)
    d_y1 = dnt(e2, lin_out).astype(BF)
    grad_lin_out = dtn(y1, e2)
    d_p1 = linear_backward(p1, d_y1, state_v, state_n, tables)
    lin_grad = dtn(d_p1, h1).astype(BF)
    lin_grad = jnp.concatenate(
        [
            lin_grad[2 * HEAD_V : 2 * HEAD_V + 4 * FEAT].reshape(2, 2 * FEAT, D),
            lin_grad[: 2 * HEAD_V].reshape(2, HEAD_V, D),
        ],
        axis=1,
    ).reshape(16, wide, D)
    lin_grad = jnp.pad(lin_grad, ((0, 0), (0, BIN_PAD - wide), (0, 0))).reshape(16 * BIN_PAD, D)
    grad_win_in, grad_win_out, grad_lin_in, grad_lin_out = reduce_together(
        grad_win_in, grad_win_out, lin_grad, grad_lin_out
    )
    input_grad, grad_a = last_step(d_p1, lin_in, block_input, gains[0], dx2)
    gain_sums = lax.psum(jnp.concatenate([grad_a, grad_b, grad_c], axis=0), ALL)
    return (
        block_output,
        input_grad,
        gain_sums[0],
        grad_lin_in[:wide].T,
        grad_lin_out,
        gain_sums[1],
        grad_win_in.T,
        grad_win_out,
        gain_sums[2],
        jnp.stack([grad_gate[:units].T, grad_up[:units].T], axis=1),
        grad_down[:units],
    )


def solution(mesh):
    grid = Mesh(mesh.devices.reshape(2, 4, 2, 4, 2), ALL)
    tokens = P(ALL, None)
    weight = ("xh", "z", "c", "xl", "y")
    rows, cols = P(weight, None), P(None, weight)
    return jax.shard_map(
        body,
        mesh=grid,
        in_specs=(
            tokens,
            tokens,
            P(("xl", "y"), None),
            P(),
            cols,
            rows,
            P(),
            cols,
            rows,
            P(),
            P(None, None, weight),
            rows,
        ),
        out_specs=(
            tokens,
            tokens,
            P(),
            cols,
            rows,
            P(),
            cols,
            rows,
            P(),
            P(None, None, weight),
            rows,
        ),
        check_vma=False,
    )
```

time: 1570 us -> 626 us (0.40)
  waiting for transfers between devices: 1070 us -> 73.1 us
  Pallas kernels: 0 us -> 311 us
  blocking collectives: 198 us -> 65.6 us
  matrix products: 165 us -> 74.9 us
  other arithmetic: 61.1 us -> 32.4 us
  local copies, waits for them, and re-layouts: 26.7 us -> 49.2 us
    reduce_scatter x9 -> x3, waiting for transfers between devices: 686 us -> 50.8 us  [the longest x2 50.8 us: plane_reduce(): lax.psum_scatter(rows.astype(BF), PLANE, scatter_dimension=0, tiled=True)]
    all_gather x9 -> x4, waiting for transfers between devices: 381 us -> 22.2 us  [the longest x3 16.1 us: plane_gather(): return lax.all_gather(rows, PLANE, axis=0, tiled=True)]
    pallas_call x0 -> x10, Pallas kernels: none -> 311 us  [the longest x2 111 us: backward_step(): pl.pallas_call(backward_kernel, out_shape=(jax.ShapeDtypeStruct((TOK, D),...]
    all_gather x3 -> x0, blocking collectives: 93.7 us -> none  [the longest x1 32 us: body(): lax.all_gather(based_in, 'dp', axis=1, tiled=True)]
    dot_general x52 -> x15, matrix products: 165 us -> 74.9 us  [the longest x7 45.6 us: dnt(): lax.dot_general(a, b, (((1,), (1,)), ((), ())), preferred_element_type=F32)]
    unnamed x1 -> x0, blocking collectives: 39.1 us -> none
    convert_element_type x20 -> x5, other arithmetic: 36.8 us -> 6.34 us  [the longest x2 2.36 us: plane_reduce(): lax.psum_scatter(rows.astype(BF), PLANE, scatter_dimension=0, tiled=True)]
    concatenate x5 -> x11, other arithmetic: 0.83 us -> 23.1 us  [the longest x2 7.9 us: reduce_together(): total = plane_reduce(jnp.concatenate(rows, axis=1).reshape(-1, D))]
  transfers between devices with their start and end apart: 22 -> 7, of which waited for: 18 -> 3; matrix products, arithmetic and copies ran while one was open for 11% -> 17% of each run, Pallas kernels for 0% -> 50%
where the time goes in v1:
time: 626 us; the launch traced here: 622 us
  Pallas kernels  311 us (50%)
  matrix products  74.9 us (12%)
  waiting for transfers between devices  73.1 us (12%)
  blocking collectives  65.6 us (10%)
  local copies, waits for them, and re-layouts  49.2 us (8%)
  other arithmetic  32.4 us (5%)
  between operations  15.2 us (2%)
    pallas_call x2, Pallas kernels, backward_step(): pl.pallas_call(backward_kernel, out_shape=(jax.ShapeDtypeStruct((TOK, D),...  111 us
    pallas_call x2, Pallas kernels, forward_step(): pl.pallas_call(forward_kernel, out_shape=(jax.ShapeDtypeStruct((TOK, D),...  93.3 us
    psum x1, blocking collectives, body(): gain_sums = lax.psum(jnp.concatenate([grad_a, grad_b, grad_c], axis=0), ALL)  65.6 us
    reduce_scatter x2, waiting for transfers between devices, plane_reduce(): lax.psum_scatter(rows.astype(BF), PLANE, scatter_dimension=0, tiled=True)  50.8 us
    dot_general x7, matrix products, dnt(): lax.dot_general(a, b, (((1,), (1,)), ((), ())), preferred_element_type=F32)  45.6 us
    pallas_call x1, Pallas kernels, last_step(): pl.pallas_call(last_kernel, out_shape=(jax.ShapeDtypeStruct((TOK, D), F32...  26.4 us
    pallas_call x1, Pallas kernels, first_gather(): pl.pallas_call(first_kernel, out_shape=jax.ShapeDtypeStruct((HALF_TOK, D)...  25.2 us
    dot_general x7, matrix products, dtn(): lax.dot_general(a, b, (((0,), (0,)), ((), ())), preferred_element_type=F32)  24.3 us
  transfers between devices with their start and end apart: 7, of which 3 were waited for; matrix products, arithmetic and copies ran while one was open for 17% of the time, Pallas kernels for 50%

profile of v1, /device:TPU:0, one launch (start us, length us, event | category | flops | bytes accessed | tf_op | source)
XLA Modules:
  0.0 621.7 jit_solution(3863600324524369464)
XLA Ops:
  17.5 25.2 %shard_map.230 = bf16[1024,2048]{1,0:T(8,128)(2,1)S(1)} custom-call(bf16[128,2048]{1,0:T(8,128)(2,1)S(1)} %copy-done, f32[1,2048]{1,0:T(1,128)S(1)} %bitcast.89), custom_call_target="tpu_custom_call" | custom-call | tf_op jit(solution)/shard_map/pallas_call | solution.py:247
  45.1 16.1 %all-gather.5.cloned.1.call-done = bf16[768,2048]{1,0:T(8,128)(2,1)} async-done(((bf16[48,2048]{1,0:T(8,128)(2,1)}), bf16[768,2048]{1,0:T(8,128)(2,1)}) %all-gather.5.cloned.1.call-update) | async-done | bytes 3145744 | tf_op jit(solution)/shard_map/all_gather | solution.py:844
  72.9 4.8 convolution_convert_fusion.8.p_ref
  77.7 11.6 %shard_map.231 = (bf16[1024,256]{1,0:T(8,128)(2,1)S(1)}, bf16[2,128,256]{2,1,0:T(8,128)(2,1)S(1)}, f32[2,8,256]{2,1,0:T(8,128)S(1)}) custom-call(bf16[1024,384]{1,0:T(8,128)(2,1)S(1)} %convolution_convert_fusion.8.p_ref, bf16[2,128,256]{2,1,0:T(8,128)(2,1)S(1)} %copy-done.28, f32[8,256]{1,0:T(8,128)S(1)} %copy-done.32, bf16[4,128,128]{2,1,0:T(8,128)(2,1)S(1)} %copy-done.27), custom_call_target="tpu_custom_call" | custom-call | tf_op jit(solution)/shard_map/pallas_call | solution.py:528
  90.0 48.7 %shard_map.232 = (f32[128,2048]{1,0:T(8,128)S(1)}, bf16[1024,2048]{1,0:T(8,128)(2,1)}) custom-call(bf16[1024,256]{1,0:T(8,128)(2,1)S(1)} %get-tuple-element.29.a_ref, bf16[256,2048]{1,0:T(8,128)(2,1)S(1)} %bitcast.81, bf16[128,2048]{1,0:T(8,128)(2,1)S(1)} %copy-done, f32[1,2048]{1,0:T(1,128)S(1)} %bitcast.87), custom_call_target="tpu_custom_call" | custom-call | tf_op jit(solution)/shard_map/pallas_call | solution.py:292
  144.6 5.1 fusion.22.p_ref
  149.7 10.5 %shard_map.233 = (bf16[1024,256]{1,0:T(8,128)(2,1)S(1)}, bf16[1024,256]{1,0:T(8,128)(2,1)S(1)}, bf16[1088,512]{1,0:T(8,128)(2,1)S(1)}) custom-call(f32[1024,768]{1,0:T(8,128)} %fusion.22.p_ref, f32[1024,128]{1,0:T(8,128)S(1)} %get-tuple-element.94.cos_ref, f32[1024,128]{1,0:T(8,128)S(1)} %get-tuple-element.95.sin_ref), custom_call_target="tpu_custom_call" | custom-call | tf_op jit(solution)/shard_map/pallas_call | solution.py:757
  162.0 44.5 %shard_map.234 = (f32[128,2048]{1,0:T(8,128)S(1)}, bf16[1024,2048]{1,0:T(8,128)(2,1)}) custom-call(bf16[1024,256]{1,0:T(8,128)(2,1)S(1)} %get-tuple-element.31.a_ref, bf16[256,2048]{1,0:T(8,128)(2,1)S(1)} %bitcast.83, f32[128,2048]{1,0:T(8,128)S(1)} %copy-done.11, f32[1,2048]{1,0:T(1,128)S(1)} %bitcast.85), custom_call_target="tpu_custom_call" | custom-call | tf_op jit(solution)/shard_map/pallas_call | solution.py:292
  208.4 6.4 %fusion.17 = (bf16[16,48,2048]{2,1,0:T(8,128)(2,1)}, bf16[16,48,2048]{2,1,0:T(8,128)(2,1)S(1)}, bf16[16,48,2048]{2,1,0:T(8,128)(2,1)}) fusion(bf16[16,144,2048]{2,1,0:T(8,128)(2,1)} %bitcast.99), kind=kLoop, calls=%fused_computation.66 | loop fusion | bytes 18874368 | tf_op jit(solution)/shard_map/slice | solution.py:912
  216.3 5.1 fusion.23
  221.5 6.1 all-gather.11.cloned.1.call-done
  227.6 17.2 %fusion.24 = f32[1024,768]{1,0:T(8,128)S(1)} fusion(bf16[1024,2048]{1,0:T(8,128)(2,1)} %all-gather.11.cloned.1.call-done, bf16[768,2048]{1,0:T(8,128)(2,1)} %bitcast.105), kind=kOutput, calls=%fused_computation.73 | convolution fusion | flops 3221225472 | bytes 10485760 | tf_op jit(solution)/shard_map/dot_general | solution.py:39
  244.9 6.1 multiply_convert_fusion.1
  252.1 5.0 convolution_convert_fusion
  257.2 4.0 pad_maximum_fusion.2.a_ref
  262.1 3.7 pad_maximum_fusion.1.w_ref
  265.9 60.5 %shard_map.235 = (f32[128,2048]{1,0:T(8,128)S(1)}, f32[1,2048]{1,0:T(1,128)S(1)}, bf16[1024,2048]{1,0:T(8,128)(2,1)}) custom-call(bf16[1024,1536]{1,0:T(8,128)(2,1)} %pad_maximum_fusion.2.a_ref, bf16[1536,2048]{1,0:T(8,128)(2,1)} %pad_maximum_fusion.1.w_ref, f32[128,2048]{1,0:T(8,128)S(1)} %copy-done.2, f32[1,2048]{1,0:T(1,128)S(1)} %bitcast.86, ...), custom_call_target="tpu_custom_call" | custom-call | tf_op jit(solution)/shard_map/pallas_call | solution.py:361
  326.4 3.6 convolution_convert_fusion.10.dy_ref
  330.1 11.6 %shard_map.236.a_ref = bf16[1024,768]{1,0:T(8,128)(2,1)S(1)} custom-call(bf16[1024,256]{1,0:T(8,128)(2,1)S(1)} %copy-done.24, bf16[1088,512]{1,0:T(8,128)(2,1)S(1)} %copy-done.16, bf16[1024,256]{1,0:T(8,128)(2,1)S(1)} %convolution_convert_fusion.10.dy_ref, f32[1024,128]{1,0:T(8,128)S(1)} %get-tuple-element.94.cos_ref, f32[1024,128]{1,0:T(8,128)S(1)} %get-tuple-element.95.sin_ref), custom_call_target="tpu_custom_call" | custom-call | tf_op jit(solution)/shard_map/pallas_call | solution.py:828
  341.7 50.8 %shard_map.237 = (f32[128,2048]{1,0:T(8,128)S(1)}, f32[1,2048]{1,0:T(1,128)S(1)}, bf16[1024,2048]{1,0:T(8,128)(2,1)}) custom-call(bf16[1024,768]{1,0:T(8,128)(2,1)S(1)} %shard_map.236.a_ref, bf16[768,2048]{1,0:T(8,128)(2,1)} %bitcast.98, f32[128,2048]{1,0:T(8,128)S(1)} %copy-done.12, f32[1,2048]{1,0:T(1,128)S(1)} %bitcast.88, ...), custom_call_target="tpu_custom_call" | custom-call | tf_op jit(solution)/shard_map/pallas_call | solution.py:361
  394.2 3.6 convolution_convert_fusion.9.dy_ref
  397.8 21.1 %shard_map.238.a_ref = bf16[1024,384]{1,0:T(8,128)(2,1)S(1)} custom-call(bf16[1024,384]{1,0:T(8,128)(2,1)S(1)} %copy-done.14, bf16[1024,256]{1,0:T(8,128)(2,1)S(1)} %convolution_convert_fusion.9.dy_ref, bf16[2,128,256]{2,1,0:T(8,128)(2,1)S(1)} %get-tuple-element.40.sv_ref, f32[2,8,256]{2,1,0:T(8,128)S(1)} %copy-done.35, bf16[2,128,256]{2,1,0:T(8,128)(2,1)S(1)} %copy-done.28, ...), custom_call_target="tpu_custom_call" | custom-call | tf_op jit(solution)/shard_map/pallas_call | solution.py:673
  425.3 3.6 convolution_convert_fusion.6
  431.1 3.7 convolution_convert_fusion.4
  434.8 3.6 fusion.3
  438.5 6.3 %convolution_convert_fusion.2 = bf16[768,2048]{1,0:T(8,128)(2,1)S(1)} fusion(bf16[1024,768]{1,0:T(8,128)(2,1)} %get-tuple-element.72, bf16[1024,2048]{1,0:T(8,128)(2,1)} %get-tuple-element.34), kind=kOutput, calls=%fused_computation.10 | convolution fusion | flops 3222798336 | bytes 8912896 | tf_op jit(solution)/shard_map/dot_general | solution.py:43
  444.9 3.9 convolution_convert_fusion.1
  448.8 3.7 convolution_convert_fusion.3
  452.5 4.3 pad_maximum_fusion
  459.5 26.4 %shard_map.239 = (f32[128,2048]{1,0:T(8,128)S(1)}, f32[1,2048]{1,0:T(1,128)S(1)}) custom-call(bf16[1024,384]{1,0:T(8,128)(2,1)S(1)} %shard_map.238.a_ref, bf16[384,2048]{1,0:T(8,128)(2,1)S(1)} %maximum_maximum_fusion.w_ref, bf16[128,2048]{1,0:T(8,128)(2,1)S(1)} %copy-done, f32[1,2048]{1,0:T(1,128)S(1)} %bitcast.90, f32[128,2048]{1,0:T(8,128)S(1)} %copy-done.20), custom_call_target="tpu_custom_call" | custom-call | tf_op jit(solution)/shard_map/pallas_call | solution.py:403
  486.9 65.6 %psum.7 = f32[3,2048]{1,0:T(4,128)S(1)} all-reduce(f32[3,2048]{1,0:T(4,128)S(1)} %pad_maximum_fusion.8), channel_id=1, replica_groups=mesh['xl'=2,'y'=4,'xh'=2,'z'=4,'c'=2] {'xl','y','xh','z','c'}, use_global_device_ids=true, to_apply=%region_1.2 | all-reduce | flops 6144 | bytes 49152 | tf_op jit(solution)/shard_map/psum | solution.py:982
  559.3 50.8 %reduce-scatter.8.cloned.1.call-done = bf16[144,2048]{1,0:T(8,128)(2,1)} async-done(((bf16[2304,2048]{1,0:T(8,128)(2,1)}), bf16[144,2048]{1,0:T(8,128)(2,1)}) %reduce-scatter.8.cloned.1.call-update) | async-done | bytes 589840 | tf_op jit(solution)/shard_map/reduce_scatter | solution.py:848
  (194 shorter events, 63.2 us)
Async XLA Ops:
  7.2 6.5 %copy-start.54 = (s32[1,3]{1,0:T(1,128)S(1)}, s32[1,3]{1,0:T(1,128)}, u32[]{:S(2)}) copy-start(s32[1,3]{1,0:T(1,128)} %param.17) | copy-start | bytes 40
  7.2 9.1 %copy-start.52 = (bf16[128,2048]{1,0:T(8,128)(2,1)S(1)}, bf16[128,2048]{1,0:T(8,128)(2,1)}, u32[]{:S(2)}) copy-start(bf16[128,2048]{1,0:T(8,128)(2,1)} %param.16) | copy-start | bytes 1572868
  7.2 53.9 %all-gather.5.cloned.1.call-start = ((), (), s32[]{:S(2)}) async-start(), calls=%async_computation.3 | async-start | bytes 3342336 | tf_op jit(solution)/shard_map/all_gather | solution.py:844
  9.0 130.8 %all-gather.7.cloned.1.call-start = ((), (), s32[]{:S(2)}) async-start(), calls=%async_computation.4 | async-start | bytes 4456448 | tf_op jit(solution)/shard_map/all_gather | solution.py:844
  10.7 197.6 %all-gather.9.cloned.1.call-start = ((), (), s32[]{:S(2)}) async-start(), calls=%async_computation.5 | async-start | bytes 10027008 | tf_op jit(solution)/shard_map/all_gather | solution.py:844
  13.6 213.9 %all-gather.11.cloned.1.call-start = ((), (), s32[]{:S(2)}) async-start(), calls=%async_computation.7 | async-start | bytes 4718592 | tf_op jit(solution)/shard_map/all_gather | solution.py:931
  17.3 535.8 %reduce-scatter.4.cloned.1.call-start = ((), (), s32[]{:S(2)}) async-start(), calls=%async_computation.6 | async-start | bytes 4718592 | tf_op jit(solution)/shard_map/reduce_scatter | solution.py:942
  17.5 54.5 %copy-start.55 = (bf16[384]{0:T(512)(128)(2,1)}, bf16[384]{0:T(512)(128)(2,1)S(1)}, u32[]{:S(2)}) copy-start(bf16[384]{0:T(512)(128)(2,1)S(1)} %pad.52.clone) | copy-start | bytes 2308
  72.9 17.1 %copy-start.6 = (bf16[16,16,2048]{2,1,0:T(8,128)(2,1)S(1)}, bf16[16,16,2048]{2,1,0:T(8,128)(2,1)}, u32[]{:S(2)}) copy-start(bf16[16,16,2048]{2,1,0:T(8,128)(2,1)} %slice.117) | copy-start | bytes 3145732
  72.9 17.1 %copy-start.30 = (f32[2048]{0:T(1024)S(1)}, f32[2048]{0:T(1024)}, u32[]{:S(2)}) copy-start(f32[2048]{0:T(1024)} %param.21) | copy-start | bytes 24580
  77.7 12.2 %copy-start.13 = (bf16[1024,384]{1,0:T(8,128)(2,1)}, bf16[1024,384]{1,0:T(8,128)(2,1)S(1)}, u32[]{:S(2)}) copy-start(bf16[1024,384]{1,0:T(8,128)(2,1)S(1)} %convolution_convert_fusion.8.p_ref) | copy-start | bytes 2359300
  90.0 53.6 %copy-start.25 = (bf16[1024,256]{1,0:T(8,128)(2,1)}, bf16[1024,256]{1,0:T(8,128)(2,1)S(1)}, u32[]{:S(2)}) copy-start(bf16[1024,256]{1,0:T(8,128)(2,1)S(1)} %get-tuple-element.29.a_ref) | copy-start | bytes 1572868
  141.0 21.0 %copy-start.8 = (bf16[16,16,2048]{2,1,0:T(8,128)(2,1)}, bf16[16,16,2048]{2,1,0:T(8,128)(2,1)S(1)}, u32[]{:S(2)}) copy-start(bf16[16,16,2048]{2,1,0:T(8,128)(2,1)S(1)} %slice.119) | copy-start | bytes 3145732
  143.6 6.1 copy-start.44
  149.7 12.3 %copy-start.11 = (f32[128,2048]{1,0:T(8,128)S(1)}, f32[128,2048]{1,0:T(8,128)}, u32[]{:S(2)}) copy-start(f32[128,2048]{1,0:T(8,128)} %copy-done.10) | copy-start | bytes 3145732
  149.7 12.3 %copy-start.29 = (f32[2048]{0:T(1024)S(1)}, f32[2048]{0:T(1024)}, u32[]{:S(2)}) copy-start(f32[2048]{0:T(1024)} %param.24) | copy-start | bytes 24580
  208.4 8.0 %copy-start.58 = (bf16[1024,2048]{1,0:T(8,128)(2,1)S(1)}, bf16[1024,2048]{1,0:T(8,128)(2,1)}, u32[]{:S(2)}) copy-start(bf16[1024,2048]{1,0:T(8,128)(2,1)} %get-tuple-element.34) | copy-start | bytes 12582916
  227.6 17.3 %copy-start.42 = (bf16[16,48,2048]{2,1,0:T(8,128)(2,1)S(1)}, bf16[16,48,2048]{2,1,0:T(8,128)(2,1)}, u32[]{:S(2)}) copy-start(bf16[16,48,2048]{2,1,0:T(8,128)(2,1)} %get-tuple-element.71) | copy-start | bytes 9437188
  227.6 17.3 %copy-start.59 = (bf16[1024,2048]{1,0:T(8,128)(2,1)S(1)}, bf16[1024,2048]{1,0:T(8,128)(2,1)}, u32[]{:S(2)}) copy-start(bf16[1024,2048]{1,0:T(8,128)(2,1)} %get-tuple-element.34) | copy-start | bytes 12582916
  227.6 17.3 %copy-start.66 = (f32[1024,768]{1,0:T(8,128)S(1)}, f32[1024,768]{1,0:T(8,128)}, u32[]{:S(2)}) copy-start(f32[1024,768]{1,0:T(8,128)} %fusion.23) | copy-start | bytes 9437188
  244.9 7.3 %copy-start.47 = (bf16[16,48,2048]{2,1,0:T(8,128)(2,1)S(1)}, bf16[16,48,2048]{2,1,0:T(8,128)(2,1)}, u32[]{:S(2)}) copy-start(bf16[16,48,2048]{2,1,0:T(8,128)(2,1)} %get-tuple-element.69) | copy-start | bytes 9437188
  257.1 297.9 %reduce-scatter.6.cloned.1.call-start = ((), (), s32[]{:S(2)}) async-start(), calls=%async_computation.8 | async-start | bytes 7798784 | tf_op jit(solution)/shard_map/reduce_scatter | solution.py:848
  265.9 60.5 %copy-start.9 = (bf16[16,16,2048]{2,1,0:T(8,128)(2,1)S(1)}, bf16[16,16,2048]{2,1,0:T(8,128)(2,1)}, u32[]{:S(2)}) copy-start(bf16[16,16,2048]{2,1,0:T(8,128)(2,1)} %copy-done.8) | copy-start | bytes 3145732
  330.0 11.7 %copy-start.12 = (f32[128,2048]{1,0:T(8,128)S(1)}, f32[128,2048]{1,0:T(8,128)}, u32[]{:S(2)}) copy-start(f32[128,2048]{1,0:T(8,128)} %copy-done.10) | copy-start | bytes 3145732
  341.7 52.4 %copy-start.7 = (bf16[16,16,2048]{2,1,0:T(8,128)(2,1)S(1)}, bf16[16,16,2048]{2,1,0:T(8,128)(2,1)}, u32[]{:S(2)}) copy-start(bf16[16,16,2048]{2,1,0:T(8,128)(2,1)} %slice.117) | copy-start | bytes 3145732
  394.2 24.8 %copy-start.5 = (bf16[1024,2048]{1,0:T(8,128)(2,1)S(1)}, bf16[1024,2048]{1,0:T(8,128)(2,1)}, u32[]{:S(2)}) copy-start(bf16[1024,2048]{1,0:T(8,128)(2,1)} %copy-done.4) | copy-start | bytes 12582916
  438.5 6.4 %copy-start.49 = (bf16[1024,768]{1,0:T(8,128)(2,1)S(1)}, bf16[1024,768]{1,0:T(8,128)(2,1)}, u32[]{:S(2)}) copy-start(bf16[1024,768]{1,0:T(8,128)(2,1)} %get-tuple-element.74) | copy-start | bytes 4718596
  438.5 171.5 %reduce-scatter.8.cloned.1.call-start = ((), (), s32[]{:S(2)}) async-start(), calls=%async_computation.9 | async-start | bytes 10027008 | tf_op jit(solution)/shard_map/reduce_scatter | solution.py:848
  438.5 6.3 %copy-start.60 = (bf16[1024,2048]{1,0:T(8,128)(2,1)S(1)}, bf16[1024,2048]{1,0:T(8,128)(2,1)}, u32[]{:S(2)}) copy-start(bf16[1024,2048]{1,0:T(8,128)(2,1)} %get-tuple-element.34) | copy-start | bytes 12582916
  457.7 29.1 %copy-start.37 = (f32[1,2048]{1,0:T(1,128)S(1)}, f32[1,2048]{1,0:T(1,128)}, u32[]{:S(2)}) copy-start(f32[1,2048]{1,0:T(1,128)} %copy-done.36) | copy-start | bytes 24580
  457.7 29.1 %copy-start.39 = (f32[1,2048]{1,0:T(1,128)S(1)}, f32[1,2048]{1,0:T(1,128)}, u32[]{:S(2)}) copy-start(f32[1,2048]{1,0:T(1,128)} %copy-done.38) | copy-start | bytes 24580
  457.7 95.4 %copy-start.3 = (f32[128,2048]{1,0:T(8,128)S(1)}, f32[128,2048]{1,0:T(8,128)}, u32[]{:S(2)}) copy-start(f32[128,2048]{1,0:T(8,128)} %copy-done.1) | copy-start | bytes 3145732
  (42 other events, 117.3 us)
Sparse Core Ops, SparseCore 0:
  10.8 50.2 all-gather.4
  63.8 51.3 all-gather.6
  118.0 76.6 all-gather.8
  196.9 30.6 all-gather.10
  257.3 51.5 reduce-scatter.3
  438.6 80.2 reduce-scatter.5
  522.8 87.2 reduce-scatter.7

commit v2 on v1

--- a/solution.py
+++ b/solution.py
@@ -79,8 +79,45 @@
         greet((self.up, self.dn, self.sib))
 
 
-def gather_rows(ring, buf, out_ref, ss, rs, ls, base=0):
-    half = TOK // 2
+class Plane:
+    def __init__(self):
+        self.x = lax.axis_index("xh") * 2 + lax.axis_index("xl")
+        self.y = lax.axis_index("y")
+
+    def at_x(self, x):
+        return {"xh": lax.div(x, 2), "xl": lax.rem(x, 2)}
+
+    def at_y(self, y):
+        return {"y": y}
+
+    def ring(self, along_x):
+        me = self.x if along_x else self.y
+        plus, minus, far = lax.rem(me + 1, 4), lax.rem(me + 3, 4), lax.rem(me + 2, 4)
+        to = self.at_x if along_x else self.at_y
+        return me, plus, minus, far, to(plus), to(minus)
+
+    def neighbours(self):
+        xs, ys = self.ring(True), self.ring(False)
+        return (xs[4], xs[5], ys[4], ys[5])
+
+
+def finish(steps):
+    for _ in steps:
+        pass
+
+
+def advance(steps):
+    next(steps, None)
+
+
+def weave(main, *others):
+    for _ in main:
+        for other in others:
+            advance(other)
+
+
+def gather_steps(ring, buf, out_ref, ss, rs, ls, rows, base=0, ready=None):
+    half = rows // 2
     me = ring.z * 2 + ring.c
     below, above, far = ring.zm * 2 + ring.c, ring.zp * 2 + ring.c, ring.zz * 2 + ring.c
 
@@ -91,13 +128,13 @@
     local = []
 
     def keep(slot):
-        copy = pltpu.make_async_copy(
-            buf.at[slot],
-            out_ref.at[pl.ds(pl.multiple_of(slot * TOK, TOK), TOK), :],
-            ls.at[len(local)],
-        )
+        copy = pltpu.make_async_copy(buf.at[slot], out_ref.at[slot], ls.at[len(local)])
         copy.start()
         local.append(copy)
+
+    def done(chip):
+        if ready is not None:
+            ready(chip)
 
     up, dn, sib = ring.up, ring.dn, ring.sib
     cp = {}
@@ -108,42 +145,54 @@
     cp[4] = send(me, 0, sib, 4)
     cp[5] = send(me, 1, sib, 5)
     keep(me)
+    yield
     cp[0].wait_recv()
     cp[6] = send(below, 0, up, 6)
     cp[8] = send(below, 0, sib, 8)
+    yield
     cp[1].wait_recv()
     cp[7] = send(above, 1, dn, 7)
     cp[9] = send(above, 1, sib, 9)
+    yield
     cp[2].wait_recv()
     cp[10] = send(below, 1, sib, 10)
     keep(below)
     cp[3].wait_recv()
     cp[11] = send(above, 0, sib, 11)
     keep(above)
+    yield
     cp[4].wait_recv()
     cp[5].wait_recv()
     keep(ring.z * 2 + ring.oc)
+    done(ring.z)
+    yield
     cp[8].wait_recv()
     cp[10].wait_recv()
     keep(ring.zm * 2 + ring.oc)
-    cp[9].wait_recv()
-    cp[11].wait_recv()
-    keep(ring.zp * 2 + ring.oc)
+    done(ring.zm)
+    yield
     cp[6].wait_recv()
     cp[12] = send(far, 0, sib, 12)
     cp[7].wait_recv()
     cp[13] = send(far, 1, sib, 13)
     keep(far)
+    yield
+    cp[9].wait_recv()
+    cp[11].wait_recv()
+    keep(ring.zp * 2 + ring.oc)
+    done(ring.zp)
+    yield
     cp[12].wait_recv()
     cp[13].wait_recv()
     keep(ring.zz * 2 + ring.oc)
+    done(ring.zz)
     for index in range(14):
         cp[index].wait_send()
     for copy in local:
         copy.wait()
 
 
-def scatter_sum(ring, a_ref, w_ref, part, sib_in, far_in, end_in, ss, rs, base=0):
+def scatter_steps(ring, product, part, sib_in, far_in, end_in, ss, rs):
     half = TOK // 2
     c, oc = ring.c, ring.oc
     up, dn, sib = ring.up, ring.dn, ring.sib
@@ -155,15 +204,13 @@
 
         def one(n, carry):
             col = pl.ds(pl.multiple_of(n * step, step), step)
-            res = dnn(a_ref[pl.ds(row, 2 * TOK), :], w_ref[:, col]).astype(BF)
+            res = product(pl.ds(row, 2 * TOK), col).astype(BF)
             part[index, 0, :, col] = res[:TOK]
             part[index, 1, :, col] = res[TOK:]
             return carry
 
         lax.fori_loop(0, D // step, one, 0)
-        return remote(
-            part.at[index, oc], sib_in.at[index], ss.at[base + index], rs.at[base + index], sib
-        )
+        return remote(part.at[index, oc], sib_in.at[index], ss.at[index], rs.at[index], sib)
 
     def add(index, rows_start, rows, other):
         def one(i, carry):
@@ -176,8 +223,16 @@
     def add_sib(index):
         add(index, 0, TOK, lambda i, at: sib_in[index, at, :].astype(F32))
 
+    def add_far(index, which):
+        add(
+            index,
+            which * half,
+            half,
+            lambda i, at: far_in[which, pl.ds(pl.multiple_of(i * 16, 16), 16), :].astype(F32),
+        )
+
     def send(src, dst, device, index):
-        return remote(src, dst, ss.at[base + index], rs.at[base + index], device)
+        return remote(src, dst, ss.at[index], rs.at[index], device)
 
     low, high = pl.ds(0, half), pl.ds(half, half)
     cp = {}
@@ -195,19 +250,23 @@
     cp[2].wait_recv()
     add_sib(2)
     cp[7] = send(part.at[2, c, low, :], end_in.at[1, low, :], dn, 7)
+    yield
     cp[4].wait_recv()
-    add(1, 0, half, lambda i, at: far_in[0, pl.ds(pl.multiple_of(i * 16, 16), 16), :].astype(F32))
+    add_far(1, 0)
     cp[8] = send(part.at[1, c, low, :], end_in.at[0, low, :], up, 8)
     cp[5].wait_recv()
-    add(2, half, half, lambda i, at: far_in[1, pl.ds(pl.multiple_of(i * 16, 16), 16), :].astype(F32))
+    add_far(2, 1)
     cp[9] = send(part.at[2, c, high, :], end_in.at[1, high, :], dn, 9)
     cp[3].wait_recv()
     add_sib(3)
+    yield
     cp[6].wait_recv()
     cp[7].wait_recv()
+    yield
     cp[8].wait_recv()
     cp[9].wait_recv()
-    return cp
+    for index in range(10):
+        cp[index].wait_send()
 
 
 SCATTER_SCRATCH = [
@@ -215,48 +274,160 @@
     pltpu.VMEM((4, TOK, D), BF),
     pltpu.VMEM((2, TOK // 2, D), BF),
     pltpu.VMEM((2, TOK, D), BF),
+    pltpu.SemaphoreType.DMA((10,)),
+    pltpu.SemaphoreType.DMA((10,)),
 ]
-
-
-def params(collective_id, limit=48):
+GATHER_SCRATCH = [
+    pltpu.VMEM((8, TOK, D), BF),
+    pltpu.SemaphoreType.DMA((14,)),
+    pltpu.SemaphoreType.DMA((14,)),
+    pltpu.SemaphoreType.DMA((8,)),
+]
+HALF_SCRATCH = [pltpu.VMEM((8, TOK // 2, D), BF)] + GATHER_SCRATCH[1:]
+
+
+def plane_view(plane, ref, half, stage, place, part):
+    cols = pl.ds(half * (D // 2) + (part or 0) * (D // 4), D // 2 if part is None else D // 4)
+    if stage == 0:
+        return ref.at[place, plane.y, :, cols] if half == 0 else ref.at[plane.x, place, :, cols]
+    return ref.at[:, place, :, cols] if half == 0 else ref.at[place, :, :, cols]
+
+
+def plane_gather_steps(plane, buf, ss, rs):
+    copies = []
+
+    def send(view, device):
+        copies.append(remote(view, view, ss.at[len(copies)], rs.at[len(copies)], device))
+        return copies[-1]
+
+    for stage in (0, 1):
+        rings = [plane.ring(half == stage) for half in (0, 1)]
+        near, far = [], []
+        for half in (0, 1):
+            me, plus, minus, _, to_plus, to_minus = rings[half]
+            view = plane_view(plane, buf, half, stage, me, None)
+            near.append((send(view, to_plus), send(view, to_minus)))
+        yield
+        for half in (0, 1):
+            me, plus, minus, _, to_plus, to_minus = rings[half]
+            near[half][0].wait_recv()
+            far.append(send(plane_view(plane, buf, half, stage, minus, 0), to_plus))
+            near[half][1].wait_recv()
+            far.append(send(plane_view(plane, buf, half, stage, plus, 1), to_minus))
+        yield
+        for copy in far:
+            copy.wait_recv()
+    for copy in copies:
+        copy.wait_send()
+
+
+def plane_reduce_scratch(rows):
+    return [
+        pltpu.VMEM((4, 4, rows, D), BF),
+        pltpu.VMEM((2, 2, 4, rows, D // 4), BF),
+        pltpu.VMEM((2, 2, 4, rows, D // 2), BF),
+        pltpu.VMEM((2, 2, rows, D // 4), BF),
+        pltpu.VMEM((2, 2, rows, D // 2), BF),
+        pltpu.SemaphoreType.DMA((24,)),
+        pltpu.SemaphoreType.DMA((24,)),
+    ]
+
+
+def plane_reduce_steps(plane, grads, far_a, end_a, far_b, end_b, ss, rs, out_ref):
+    copies = []
+    rows = grads.shape[2]
+
+    def send(src, dst, device):
+        copies.append(remote(src, dst, ss.at[len(copies)], rs.at[len(copies)], device))
+        return copies[-1]
+
+    def add(view, other):
+        def one(i, carry):
+            at = pl.ds(pl.multiple_of(i * 16, 16), 16)
+            piece = view.at[..., at, :]
+            piece[...] = (piece[...].astype(F32) + other.at[..., at, :][...].astype(F32)).astype(BF)
+            return carry
+
+        lax.fori_loop(0, rows // 16, one, 0)
+
+    for stage in (0, 1):
+        rings = [plane.ring(half != stage) for half in (0, 1)]
+        far_in, end_in = (far_a, end_a) if stage == 0 else (far_b, end_b)
+
+        def view(half, place, part):
+            return plane_view(plane, grads, half, 1 - stage, place, part)
+
+        def ends(half, side, part):
+            if part is None:
+                return end_in.at[half, side]
+            return end_in.at[half, side, ..., pl.ds(part * (D // 4), D // 4)]
+
+        first, last = [], []
+        for half in (0, 1):
+            me, plus, minus, far, to_plus, to_minus = rings[half]
+            first.append(
+                (
+                    send(view(half, far, 0), far_in.at[half, 0], to_plus),
+                    send(view(half, far, 1), far_in.at[half, 1], to_minus),
+                )
+            )
+            last.append(send(view(half, plus, 1), ends(half, 0, 1), to_plus))
+            last.append(send(view(half, minus, 0), ends(half, 1, 0), to_minus))
+        yield
+        for half in (0, 1):
+            me, plus, minus, far, to_plus, to_minus = rings[half]
+            first[half][0].wait_recv()
+            add(view(half, plus, 0), far_in.at[half, 0])
+            last.append(send(view(half, plus, 0), ends(half, 0, 0), to_plus))
+            first[half][1].wait_recv()
+            add(view(half, minus, 1), far_in.at[half, 1])
+            last.append(send(view(half, minus, 1), ends(half, 1, 1), to_minus))
+        yield
+        for copy in last:
+            copy.wait_recv()
+        for half in (0, 1):
+            me = rings[half][0]
+            if stage == 0:
+                for side in (0, 1):
+                    add(view(half, me, None), ends(half, side, None))
+            else:
+                cols = pl.ds(half * (D // 2), D // 2)
+                out_ref[:, cols] = (
+                    view(half, me, None)[...].astype(F32)
+                    + end_in[half, 0].astype(F32)
+                    + end_in[half, 1].astype(F32)
+                )
+        yield
+    for copy in copies:
+        copy.wait_send()
+
+
+def load(src, dst, sem):
+    copy = pltpu.make_async_copy(src, dst, sem)
+    copy.start()
+    return copy
+
+
+def params(collective_id, limit=58):
     return pltpu.CompilerParams(
         collective_id=collective_id, has_side_effects=True, vmem_limit_bytes=limit << 20
     )
 
 
+def sds(shape, dtype=BF):
+    return jax.ShapeDtypeStruct(shape, dtype)
+
+
 def scale_of(rows):
     return lax.rsqrt(jnp.mean(rows * rows, axis=-1, keepdims=True) + EPSILON)
 
 
-def first_kernel(x_ref, gain_ref, out_ref, buf, ss, rs, ls):
-    ring = Ring()
-    me = ring.z * 2 + ring.c
-
-    def one(i, carry):
-        at = pl.ds(pl.multiple_of(i * 16, 16), 16)
-        rows = x_ref[at, :].astype(F32)
-        buf[me, at, :] = (rows * scale_of(rows) * gain_ref[...]).astype(BF)
+def by_rows(one):
+    def step(i, carry):
+        one(pl.ds(pl.multiple_of(i * 16, 16), 16))
         return carry
 
-    lax.fori_loop(0, TOK // 16, one, 0)
-    ring.greet()
-    gather_rows(ring, buf, out_ref, ss, rs, ls)
-
-
-def first_gather(x, gain):
-    return pl.pallas_call(
-        first_kernel,
-        out_shape=jax.ShapeDtypeStruct((HALF_TOK, D), BF),
-        in_specs=[VM, VM],
-        out_specs=ANY,
-        scratch_shapes=[
-            pltpu.VMEM((8, TOK, D), BF),
-            pltpu.SemaphoreType.DMA((14,)),
-            pltpu.SemaphoreType.DMA((14,)),
-            pltpu.SemaphoreType.DMA((8,)),
-        ],
-        compiler_params=params(1),
-    )(x, gain)
+    lax.fori_loop(0, TOK // 16, step, 0)
 
 
 def total_rows(part, end_in, c, at):
@@ -267,43 +438,116 @@
     )
 
 
+def chip_rows(chip):
+    return pl.ds(pl.multiple_of(chip * (2 * TOK), 2 * TOK), 2 * TOK)
+
+
+def first_kernel(
+    x_ref, gain_ref, shard_ref, h_out, w_out, p_ref, wide, wss, wrs, buf, ss, rs, ls, wls
+):
+    ring, plane = Ring(), Plane()
+    me = ring.z * 2 + ring.c
+    barrier = pltpu.get_barrier_semaphore()
+    partners = (ring.up, ring.dn, ring.sib) + plane.neighbours()
+    for device in partners:
+        pl.semaphore_signal(barrier, inc=1, device_id=device, device_id_type=MESH)
+    wide[plane.x, plane.y] = shard_ref[...]
+
+    def one(at):
+        rows = x_ref[at, :].astype(F32)
+        buf[me, at, :] = (rows * scale_of(rows) * gain_ref[...]).astype(BF)
+
+    by_rows(one)
+    pl.semaphore_wait(barrier, len(partners))
+    weights = plane_gather_steps(plane, wide, wss, wrs)
+    advance(weights)
+    rows = gather_steps(ring, buf, h_out, ss, rs, ls, TOK)
+    weave(rows, weights)
+    finish(weights)
+    keep = load(wide, w_out, wls)
+
+    def project(i, carry):
+        at = pl.ds(pl.multiple_of(i * 256, 256), 256)
+        h = buf[pl.ds(2 * i, 2)].reshape(256, D)
+        w = wide[:, :, :BIN_PAD, :].reshape(16 * BIN_PAD, D)
+        p_ref[at, :] = dnt(h, w).astype(BF)
+        return carry
+
+    lax.fori_loop(0, 4, project, 0)
+    keep.wait()
+
+
+def first_step(x, gain, shard):
+    return pl.pallas_call(
+        first_kernel,
+        out_shape=(
+            sds((8, TOK, D)),
+            sds((4, 4, BIN_PAD + 16, D)),
+            sds((HALF_TOK, 16 * BIN_PAD)),
+        ),
+        in_specs=[VM] * 3,
+        out_specs=(ANY, ANY, VM),
+        scratch_shapes=[
+            pltpu.VMEM((4, 4, BIN_PAD + 16, D), BF),
+            pltpu.SemaphoreType.DMA((16,)),
+            pltpu.SemaphoreType.DMA((16,)),
+        ]
+        + GATHER_SCRATCH
+        + [pltpu.SemaphoreType.DMA],
+        compiler_params=params(1),
+    )(x, gain, shard)
+
+
 def forward_kernel(
-    a_ref, w_ref, x_ref, gain_ref, x_out, h_out, part, sib_in, far_in, end_in, buf, ss, rs, ls
+    off,
+    a_ref,
+    w_ref,
+    x_ref,
+    gain_ref,
+    x_out,
+    h_out,
+    w,
+    wls,
+    part,
+    sib_in,
+    far_in,
+    end_in,
+    sss,
+    srs,
+    buf,
+    ss,
+    rs,
+    ls,
 ):
     ring = Ring()
     me = ring.z * 2 + ring.c
+    loading = load(w_ref.at[:, :, pl.ds(off, 16), :], w, wls)
     ring.greet()
-    cp = scatter_sum(ring, a_ref, w_ref, part, sib_in, far_in, end_in, ss, rs)
-
-    def one(i, carry):
-        at = pl.ds(pl.multiple_of(i * 16, 16), 16)
+    loading.wait()
+
+    def product(rows, col):
+        return dnn(a_ref[rows, :], w[:, :, :, col].reshape(256, -1))
+
+    finish(scatter_steps(ring, product, part, sib_in, far_in, end_in, sss, srs))
+
+    def one(at):
         rows = x_ref[at, :].astype(F32) + total_rows(part, end_in, ring.c, at)
         x_out[at, :] = rows
         buf[me, at, :] = (rows * scale_of(rows) * gain_ref[...]).astype(BF)
-        return carry
-
-    lax.fori_loop(0, TOK // 16, one, 0)
-    gather_rows(ring, buf, h_out, ss, rs, ls, base=10)
-    for index in range(10):
-        cp[index].wait_send()
-
-
-def forward_step(a, w, x, gain, collective_id):
+
+    by_rows(one)
+    finish(gather_steps(ring, buf, h_out, ss, rs, ls, TOK))
+
+
+def forward_step(a, w, off, x, gain, collective_id):
     return pl.pallas_call(
-        forward_kernel,
-        out_shape=(
-            jax.ShapeDtypeStruct((TOK, D), F32),
-            jax.ShapeDtypeStruct((HALF_TOK, D), BF),
-        ),
-        in_specs=[VM] * 4,
+        functools.partial(forward_kernel, off),
+        out_shape=(sds((TOK, D), F32), sds((8, TOK, D))),
+        in_specs=[VM, ANY, VM, VM],
         out_specs=(VM, ANY),
-        scratch_shapes=SCATTER_SCRATCH
-        + [
-            pltpu.VMEM((8, TOK, D), BF),
-            pltpu.SemaphoreType.DMA((24,)),
-            pltpu.SemaphoreType.DMA((24,)),
-            pltpu.SemaphoreType.DMA((8,)),
-        ],
+        scratch_shapes=[pltpu.VMEM((4, 4, 16, D), BF), pltpu.SemaphoreType.DMA]
+        + SCATTER_SCRATCH
+        + GATHER_SCRATCH,
         compiler_params=params(collective_id),
     )(a, w, x, gain)
 
@@ -317,20 +561,138 @@
     return scale * (scaled - unit * jnp.mean(scaled * unit, axis=-1, keepdims=True))
 
 
-def backward_kernel(
-    a_ref,
+CHUNK = 8 * UNIT_PAD
+
+
+def mlp_kernel(
+    h_ref, lo_ref, hi_ref, w_ref, act_ref, d_ref, down_ref, h, cot, gate_w, up_w, down_w, sems
+):
+    copies = {}
+    copies["h"] = load(h_ref, h, sems.at[0])
+    names = (("gate", gate_w), ("up", up_w), ("down", down_w))
+    for n, (name, ref) in enumerate(names):
+        for i in range(2):
+            copies[name, i] = load(
+                w_ref.at[pl.ds(8 * i, 8), pl.ds(n * UNIT_PAD, UNIT_PAD), :],
+                ref.at[pl.ds(8 * i, 8)],
+                sems.at[3 + 2 * n + i],
+            )
+        if n == 0:
+            copies["lo"] = load(lo_ref, cot.at[:, pl.ds(0, TOK // 2), :], sems.at[1])
+            copies["hi"] = load(hi_ref, cot.at[:, pl.ds(TOK // 2, TOK // 2), :], sems.at[2])
+    copies["h"].wait()
+    copies["lo"].wait()
+    copies["hi"].wait()
+    for i in range(2):
+        for name, _ in names:
+            copies[name, i].wait()
+        units = slice(8 * i, 8 * i + 8)
+
+        def one(n, carry):
+            at = chip_rows(n)
+            tokens = pl.ds(2 * n, 2)
+            rows = h[tokens].reshape(2 * TOK, D)
+            gate = dnt(rows, gate_w[units].reshape(CHUNK, D))
+            up = dnt(rows, up_w[units].reshape(CHUNK, D))
+            d_act = dnt(cot[tokens].reshape(2 * TOK, D), down_w[units].reshape(CHUNK, D))
+            sig = 1.0 / (1.0 + jnp.exp(-gate))
+            silu = gate * sig
+            act_ref[at, i * CHUNK : (i + 1) * CHUNK] = (silu * up).astype(BF)
+            d_ref[at, i * CHUNK : (i + 1) * CHUNK] = (
+                d_act * up * (sig * (1.0 + gate * (1.0 - sig)))
+            ).astype(BF)
+            d_ref[at, (2 + i) * CHUNK : (3 + i) * CHUNK] = (d_act * silu).astype(BF)
+            return carry
+
+        lax.fori_loop(0, 4, one, 0)
+
+    def last(n, carry):
+        at = chip_rows(n)
+        for col in range(0, D, 512):
+            down_ref[at, col : col + 512] = dnn(
+                act_ref[at, :], down_w[:, :, col : col + 512].reshape(2 * CHUNK, 512)
+            ).astype(BF)
+        return carry
+
+    lax.fori_loop(0, 4, last, 0)
+
+
+def mlp_step(h, lo, hi, w):
+    return pl.pallas_call(
+        mlp_kernel,
+        out_shape=(
+            sds((HALF_TOK, 2 * CHUNK)),
+            sds((HALF_TOK, 4 * CHUNK)),
+            sds((HALF_TOK, D)),
+        ),
+        in_specs=[ANY] * 4,
+        out_specs=(VM, VM, VM),
+        scratch_shapes=[
+            pltpu.VMEM((8, TOK, D), BF),
+            pltpu.VMEM((8, TOK, D), BF),
+        ]
+        + [pltpu.VMEM((16, UNIT_PAD, D), BF)] * 3
+        + [pltpu.SemaphoreType.DMA((9,))],
+        compiler_params=pltpu.CompilerParams(vmem_limit_bytes=58 << 20),
+    )(h, lo, hi, w)
+
+
+def mlp_grad_steps(jobs, stage, out_ref, sems):
+    copies = []
+    for n, (lhs, col, rhs, off, half) in enumerate(jobs):
+        slot = n % 2
+        if n >= 2:
+            copies[n - 2].wait()
+
+        def one(k, carry):
+            cols = pl.ds(pl.multiple_of(k * 512, 512), 512)
+            res = dtn(lhs[:, col : col + CHUNK], rhs[:, :, cols].reshape(HALF_TOK, 512))
+            stage[slot, :, :, cols] = res.astype(BF).reshape(8, UNIT_PAD, 512)
+            return carry
+
+        lax.fori_loop(0, 4, one, 0)
+        copies.append(
+            load(
+                stage.at[slot],
+                out_ref.at[pl.ds(8 * half, 8), pl.ds(off, UNIT_PAD), :],
+                sems.at[n],
+            )
+        )
+        yield
+    copies[-2].wait()
+    copies[-1].wait()
+
+
+def mlp_back_kernel(
+    d_ref,
+    act_ref,
     w_ref,
+    wo_ref,
+    h_ref,
+    lo_ref,
+    hi_ref,
     v_ref,
     gain_ref,
-    d_ref,
+    res_ref,
     d_out,
     gain_out,
     e_out,
+    dy_out,
+    g_out,
+    w,
+    wo,
+    h,
+    cot,
+    stage,
+    sems,
+    gsems,
+    gain_acc,
     part,
     sib_in,
     far_in,
     end_in,
-    gain_acc,
+    sss,
+    srs,
     buf,
     ss,
     rs,
@@ -338,81 +700,373 @@
 ):
     ring = Ring()
     me = ring.z * 2 + ring.c
+    loads = [
+        load(w_ref.at[:, pl.ds(0, UNIT_PAD), :], w.at[0], sems.at[0]),
+        load(w_ref.at[:, pl.ds(UNIT_PAD, UNIT_PAD), :], w.at[1], sems.at[1]),
+    ]
+    late = [
+        load(h_ref, h, sems.at[2]),
+        load(lo_ref, cot.at[:, pl.ds(0, TOK // 2), :], sems.at[3]),
+        load(hi_ref, cot.at[:, pl.ds(TOK // 2, TOK // 2), :], sems.at[4]),
+        load(wo_ref.at[:, :, pl.ds(48, 16), :], wo, sems.at[5]),
+    ]
     ring.greet()
     gain_acc[...] = jnp.zeros_like(gain_acc)
-    cp = scatter_sum(ring, a_ref, w_ref, part, sib_in, far_in, end_in, ss, rs)
-
-    def one(i, carry):
-        at = pl.ds(pl.multiple_of(i * 16, 16), 16)
-        grads = total_rows(part, end_in, ring.c, at)
-        rows = d_ref[at, :] + norm_back_rows(v_ref, gain_ref, grads, at, gain_acc)
+    for copy in loads:
+        copy.wait()
+
+    def product(rows, col):
+        return dnn(d_ref[rows, :], w[:, :, :, col].reshape(4 * CHUNK, -1))
+
+    def grads():
+        for copy in late:
+            copy.wait()
+        jobs = [(d_ref, n * CHUNK, h, (n // 2) * UNIT_PAD, n % 2) for n in range(4)]
+        jobs += [(act_ref, n * CHUNK, cot, 2 * UNIT_PAD, n) for n in range(2)]
+        yield from mlp_grad_steps(jobs, stage, g_out, gsems)
+
+    weight_grads = grads()
+    weave(
+        scatter_steps(ring, product, part, sib_in, far_in, end_in, sss, srs),
+        weight_grads,
+    )
+
+    def one(at):
+        grad = total_rows(part, end_in, ring.c, at)
+        rows = res_ref[at, :] + norm_back_rows(v_ref, gain_ref, grad, at, gain_acc)
         d_out[at, :] = rows
         buf[me, at, :] = rows.astype(BF)
-        return carry
-
-    lax.fori_loop(0, TOK // 16, one, 0)
+
+    by_rows(one)
+
+    def ready(chip):
+        dy_out[chip_rows(chip), :] = dnt(
+            buf[pl.ds(2 * chip, 2)].reshape(2 * TOK, D), wo[...].reshape(256, D)
+        ).astype(BF)
+
+    weave(gather_steps(ring, buf, e_out, ss, rs, ls, TOK, ready=ready), weight_grads)
+    finish(weight_grads)
     gain_out[...] = jnp.sum(gain_acc[...], axis=0, keepdims=True)
-    gather_rows(ring, buf, e_out, ss, rs, ls, base=10)
-    for index in range(10):
-        cp[index].wait_send()
-
-
-def backward_step(a, w, v, gain, d, collective_id):
+
+
+def mlp_back_step(d, act, w, wo, h, lo, hi, v, gain, res):
     return pl.pallas_call(
-        backward_kernel,
+        mlp_back_kernel,
         out_shape=(
-            jax.ShapeDtypeStruct((TOK, D), F32),
-            jax.ShapeDtypeStruct((1, D), F32),
-            jax.ShapeDtypeStruct((HALF_TOK, D), BF),
+            sds((TOK, D), F32),
+            sds((1, D), F32),
+            sds((8, TOK, D)),
+            sds((HALF_TOK, 256)),
+            sds((16, 3 * UNIT_PAD, D)),
         ),
-        in_specs=[VM] * 5,
-        out_specs=(VM, VM, ANY),
-        scratch_shapes=SCATTER_SCRATCH
-        + [
+        in_specs=[VM, VM, ANY, ANY, ANY, ANY, ANY, VM, VM, VM],
+        out_specs=(VM, VM, ANY, VM, ANY),
+        scratch_shapes=[
+            pltpu.VMEM((2, 16, UNIT_PAD, D), BF),
+            pltpu.VMEM((4, 4, 16, D), BF),
+            pltpu.VMEM((8, TOK, D), BF),
+            pltpu.VMEM((8, TOK, D), BF),
+            pltpu.VMEM((2, 8, UNIT_PAD, D), BF),
+            pltpu.SemaphoreType.DMA((6,)),
+            pltpu.SemaphoreType.DMA((6,)),
             pltpu.VMEM((16, D), F32),
+        ]
+        + SCATTER_SCRATCH
+        + GATHER_SCRATCH,
+        compiler_params=params(4),
+    )(d, act, w, wo, h, lo, hi, v, gain, res)
+
+
+def window_back_out_kernel(
+    d_ref,
+    w_ref,
+    wo_ref,
+    h_ref,
+    y_ref,
+    e_ref,
+    v_ref,
+    gain_ref,
+    res_ref,
+    d_out,
+    gain_out,
+    e_out,
+    dy_out,
+    g_out,
+    w,
+    wo,
+    h,
+    e,
+    sems,
+    gain_acc,
+    grads,
+    far_a,
+    end_a,
+    far_b,
+    end_b,
+    gss,
+    grs,
+    part,
+    sib_in,
+    far_in,
+    end_in,
+    sss,
+    srs,
+    buf,
+    ss,
+    rs,
+    ls,
+):
+    ring, plane = Ring(), Plane()
+    me = ring.z * 2 + ring.c
+    first = load(w_ref.at[:, :, pl.ds(0, 48), :], w, sems.at[0])
+    late = [
+        load(h_ref, h, sems.at[1]),
+        load(e_ref, e, sems.at[2]),
+        load(wo_ref.at[:, :, pl.ds(BIN_PAD, 16), :], wo, sems.at[3]),
+    ]
+    greet((ring.up, ring.dn, ring.sib) + plane.neighbours())
+    gain_acc[...] = jnp.zeros_like(gain_acc)
+    first.wait()
+
+    def product(rows, col):
+        return dnn(d_ref[rows, :], w[:, :, :, col].reshape(768, -1))
+
+    def weights():
+        for copy in late:
+            copy.wait()
+
+        def one(k, carry):
+            cols = pl.ds(pl.multiple_of(k * 512, 512), 512)
+            rows = h[:, :, cols].reshape(HALF_TOK, 512)
+            for i in range(2):
+                res = dtn(d_ref[:, i * 384 : (i + 1) * 384], rows).astype(BF)
+                grads[2 * i : 2 * i + 2, :, :48, cols] = res.reshape(2, 4, 48, 512)
+            res = dtn(y_ref[...], e[:, :, cols].reshape(HALF_TOK, 512)).astype(BF)
+            grads[:, :, 48:, cols] = res.reshape(4, 4, 16, 512)
+            return carry
+
+        lax.fori_loop(0, 4, one, 0)
+        yield from plane_reduce_steps(
+            plane, grads, far_a, end_a, far_b, end_b, gss, grs, g_out
+        )
+
+    weight_grads = weights()
+    weave(
+        scatter_steps(ring, product, part, sib_in, far_in, end_in, sss, srs),
+        weight_grads,
+    )
+
+    def one(at):
+        grad = total_rows(part, end_in, ring.c, at)
+        rows = res_ref[at, :] + norm_back_rows(v_ref, gain_ref, grad, at, gain_acc)
+        d_out[at, :] = rows
+        buf[me, at, :] = rows.astype(BF)
+
+    by_rows(one)
+
+    def ready(chip):
+        dy_out[chip_rows(chip), :] = dnt(
+            buf[pl.ds(2 * chip, 2)].reshape(2 * TOK, D), wo[...].reshape(256, D)
+        ).astype(BF)
+
+    weave(gather_steps(ring, buf, e_out, ss, rs, ls, TOK, ready=ready), weight_grads)
+    finish(weight_grads)
+    gain_out[...] = jnp.sum(gain_acc[...], axis=0, keepdims=True)
+
+
+def window_back_out_step(d, w, wo, h, y, e, v, gain, res):
+    return pl.pallas_call(
+        window_back_out_kernel,
+        out_shape=(
+            sds((TOK, D), F32),
+            sds((1, D), F32),
+            sds((8, TOK, D)),
+            sds((HALF_TOK, 256)),
+            sds((64, D), F32),
+        ),
+        in_specs=[VM, ANY, ANY, ANY, VM, ANY, VM, VM, VM],
+        out_specs=(VM, VM, ANY, VM, VM),
+        scratch_shapes=[
+            pltpu.VMEM((4, 4, 48, D), BF),
+            pltpu.VMEM((4, 4, 16, D), BF),
             pltpu.VMEM((8, TOK, D), BF),
-            pltpu.SemaphoreType.DMA((24,)),
-            pltpu.SemaphoreType.DMA((24,)),
-            pltpu.SemaphoreType.DMA((8,)),
-        ],
-        compiler_params=params(collective_id),
-    )(a, w, v, gain, d)
+            pltpu.VMEM((8, TOK, D), BF),
+            pltpu.SemaphoreType.DMA((4,)),
+            pltpu.VMEM((16, D), F32),
+        ]
+        + plane_reduce_scratch(64)
+        + SCATTER_SCRATCH
+        + GATHER_SCRATCH,
+        compiler_params=params(5),
+    )(d, w, wo, h, y, e, v, gain, res)
+
+
+def sum_everywhere(ring, plane, pack, ring_in, x_in, y_in, ss, rs):
+    copies = []
+    me = ring.z * 2 + ring.c
+
+    def exchange(value, dst, own, count, device_of):
+        pack[...] = value
+        dst[own] = value
+        sent = []
+        for o in range(1, count):
+            n = len(copies)
+            sent.append(
+                remote(
+                    pack,
+                    dst.at[own],
+                    ss.at[n],
+                    rs.at[n],
+                    device_of(lax.rem(own + o, count)),
+                )
+            )
+            copies.append(sent[-1])
+        for copy in sent:
+            copy.wait_recv()
+        for copy in sent:
+            copy.wait_send()
+        total = dst[0]
+        for k in range(1, count):
+            total = total + dst[k]
+        return total
+
+    total = exchange(
+        pack[...], ring_in, me, 8, lambda t: {"z": lax.div(t, 2), "c": lax.rem(t, 2)}
+    )
+    total = exchange(total, x_in, plane.x, 4, plane.at_x)
+    return exchange(total, y_in, plane.y, 4, plane.at_y)
 
 
 def last_kernel(
-    a_ref, w_ref, v_ref, gain_ref, d_ref, d_out, gain_out, part, sib_in, far_in, end_in, gain_acc, ss, rs
+    d_ref,
+    w_ref,
+    h_ref,
+    y_ref,
+    e_ref,
+    v_ref,
+    gain_ref,
+    res_ref,
+    gb_ref,
+    gc_ref,
+    d_out,
+    ga_out,
+    gb_out,
+    gc_out,
+    g_out,
+    w,
+    h,
+    e,
+    sems,
+    gain_acc,
+    pack,
+    ring_in,
+    x_in,
+    y_in,
+    pss,
+    prs,
+    grads,
+    far_a,
+    end_a,
+    far_b,
+    end_b,
+    gss,
+    grs,
+    part,
+    sib_in,
+    far_in,
+    end_in,
+    sss,
+    srs,
 ):
-    ring = Ring()
-    ring.greet()
+    ring, plane = Ring(), Plane()
+    first = load(w_ref.at[:, :, pl.ds(0, BIN_PAD), :], w, sems.at[0])
+    late = [load(h_ref, h, sems.at[1]), load(e_ref, e, sems.at[2])]
+    me = ring.z * 2 + ring.c
+    partners = []
+    for o in range(1, 8):
+        to = lax.rem(me + o, 8)
+        partners.append({"z": lax.div(to, 2), "c": lax.rem(to, 2)})
+    for o in range(1, 4):
+        partners.append(plane.at_x(lax.rem(plane.x + o, 4)))
+        partners.append(plane.at_y(lax.rem(plane.y + o, 4)))
+    greet(partners)
     gain_acc[...] = jnp.zeros_like(gain_acc)
-    cp = scatter_sum(ring, a_ref, w_ref, part, sib_in, far_in, end_in, ss, rs)
-
-    def one(i, carry):
-        at = pl.ds(pl.multiple_of(i * 16, 16), 16)
-        grads = total_rows(part, end_in, ring.c, at)
-        d_out[at, :] = d_ref[at, :] + norm_back_rows(v_ref, gain_ref, grads, at, gain_acc)
-        return carry
-
-    lax.fori_loop(0, TOK // 16, one, 0)
-    gain_out[...] = jnp.sum(gain_acc[...], axis=0, keepdims=True)
-    for index in range(10):
-        cp[index].wait_send()
-
-
-def last_step(a, w, v, gain, d):
+    first.wait()
+
+    def product(rows, col):
+        return dnn(d_ref[rows, :], w[:, :, :, col].reshape(16 * BIN_PAD, -1))
+
+    def weights():
+        for copy in late:
+            copy.wait()
+
+        def one(k, carry):
+            cols = pl.ds(pl.multiple_of(k * 512, 512), 512)
+            res = dtn(d_ref[...], h[:, :, cols].reshape(HALF_TOK, 512)).astype(BF)
+            grads[:, :, :BIN_PAD, cols] = res.reshape(4, 4, BIN_PAD, 512)
+            res = dtn(y_ref[...], e[:, :, cols].reshape(HALF_TOK, 512)).astype(BF)
+            grads[:, :, BIN_PAD:, cols] = res.reshape(4, 4, 16, 512)
+            return carry
+
+        lax.fori_loop(0, 4, one, 0)
+        yield from plane_reduce_steps(
+            plane, grads, far_a, end_a, far_b, end_b, gss, grs, g_out
+        )
+
+    weight_grads = weights()
+    weave(
+        scatter_steps(ring, product, part, sib_in, far_in, end_in, sss, srs),
+        weight_grads,
+    )
+
+    def one(at):
+        grad = total_rows(part, end_in, ring.c, at)
+        d_out[at, :] = res_ref[at, :] + norm_back_rows(v_ref, gain_ref, grad, at, gain_acc)
+
+    by_rows(one)
+    wide = D // 8
+    gains = (jnp.sum(gain_acc[...], axis=0, keepdims=True), gb_ref[...], gc_ref[...])
+    for n, gain in enumerate(gains):
+        for r in range(8):
+            pack[r : r + 1, n * wide : (n + 1) * wide] = gain[:, r * wide : (r + 1) * wide]
+    total = sum_everywhere(ring, plane, pack, ring_in, x_in, y_in, pss, prs)
+    pack[...] = total
+    for n, out in enumerate((ga_out, gb_out, gc_out)):
+        for r in range(8):
+            out[:, r * wide : (r + 1) * wide] = pack[r : r + 1, n * wide : (n + 1) * wide]
+    finish(weight_grads)
+
+
+def last_step(d, w, h, y, e, v, gain, res, grad_b, grad_c):
+    small = (8, 3 * D // 8)
     return pl.pallas_call(
         last_kernel,
-        out_shape=(jax.ShapeDtypeStruct((TOK, D), F32), jax.ShapeDtypeStruct((1, D), F32)),
-        in_specs=[VM] * 5,
-        out_specs=(VM, VM),
-        scratch_shapes=SCATTER_SCRATCH
-        + [
+        out_shape=(
+            sds((TOK, D), F32),
+            sds((1, D), F32),
+            sds((1, D), F32),
+            sds((1, D), F32),
+            sds((BIN_PAD + 16, D), F32),
+        ),
+        in_specs=[VM, ANY, ANY, VM, ANY, VM, VM, VM, VM, VM],
+        out_specs=(VM,) * 5,
+        scratch_shapes=[
+            pltpu.VMEM((4, 4, BIN_PAD, D), BF),
+            pltpu.VMEM((8, TOK, D), BF),
+            pltpu.VMEM((8, TOK, D), BF),
+            pltpu.SemaphoreType.DMA((3,)),
             pltpu.VMEM((16, D), F32),
-            pltpu.SemaphoreType.DMA((10,)),
-            pltpu.SemaphoreType.DMA((10,)),
-        ],
+            pltpu.VMEM(small, F32),
+            pltpu.VMEM((8,) + small, F32),
+            pltpu.VMEM((4,) + small, F32),
+            pltpu.VMEM((4,) + small, F32),
+            pltpu.SemaphoreType.DMA((13,)),
+            pltpu.SemaphoreType.DMA((13,)),
+        ]
+        + plane_reduce_scratch(BIN_PAD + 16)
+        + SCATTER_SCRATCH,
         compiler_params=params(6),
-    )(a, w, v, gain, d)
+    )(d, w, h, y, e, v, gain, res, grad_b, grad_c)
 
 
 def state_tables():
@@ -456,20 +1110,65 @@
 INV_ROOT = 1.0 / math.sqrt(FEAT)
 
 
+def select_table(width):
+    table = np.zeros((16 * BIN_PAD, 3 * HEAD_V), np.float32)
+    for shard in range(16):
+        for i in range(width):
+            head, col = shard // 8, (shard % 8) * width + i
+            to = 2 * HEAD_V + 2 * FEAT * head + col if col < 2 * FEAT else head * HEAD_V + col - 2 * FEAT
+            table[shard * BIN_PAD + i, to] = 1.0
+    return table
+
+
 def linear_forward_kernel(
-    p_ref, e_ref, t_ref, pick_ref, y_ref, sv_ref, sn_ref, qs, ks, num, den, sv_s, sn_s, sv_r, sn_r, ss, rs
+    raw_ref,
+    sel_ref,
+    e_ref,
+    t_ref,
+    pick_ref,
+    cot_ref,
+    y_ref,
+    p_ref,
+    sv_ref,
+    sn_ref,
+    lo_ref,
+    qs,
+    ks,
+    num,
+    den,
+    sv_s,
+    sn_s,
+    sv_r,
+    sn_r,
+    xss,
+    xrs,
+    buf,
+    ss,
+    rs,
+    ls,
 ):
+    ring = Ring()
     xh = lax.axis_index("xh")
     partner = {"xh": 1 - xh}
     edge = jnp.where(xh == 0, EDGE, HALF_TOK - EDGE)
     bias1, bias2, coef = t_ref[0:1, :], t_ref[1:2, :], t_ref[2:3, :]
+    barrier = pltpu.get_barrier_semaphore()
+    for device in (ring.up, ring.dn, ring.sib, partner):
+        pl.semaphore_signal(barrier, inc=1, device_id=device, device_id_type=MESH)
+    buf[ring.z * 2 + ring.c] = cot_ref[: TOK // 2, :]
+
+    def rows_of(r):
+        return slice(r * BLK, (r + 1) * BLK)
+
+    for r in range(NBLK):
+        p_ref[rows_of(r), :] = dnn(raw_ref[rows_of(r), :], sel_ref[...]).astype(BF)
+    pl.semaphore_wait(barrier, 4)
+    cots = gather_steps(ring, buf, lo_ref, ss, rs, ls, TOK // 2)
+    advance(cots)
     small = p_ref[:, 2 * HEAD_V :]
     for j in range(2):
         qs[j] = dnn(small, pick_ref[2 * j]).astype(BF)
         ks[j] = dnn(small, pick_ref[2 * j + 1]).astype(BF)
-
-    def rows_of(r):
-        return slice(r * BLK, (r + 1) * BLK)
 
     def phi_of(vecs):
         return (dnn(vecs, e_ref[0]) + bias1) * (dnn(vecs, e_ref[1]) + bias2)
@@ -486,13 +1185,13 @@
             sn = sn + jnp.sum(phi, axis=0, keepdims=True)
         sv_s[j] = (sv * coef).astype(BF)
         sn_s[j] = jnp.broadcast_to(sn * coef, (8, STATE))
-    greet((partner,))
     copies = (
-        remote(sv_s, sv_r, ss.at[0], rs.at[0], partner),
-        remote(sn_s, sn_r, ss.at[1], rs.at[1], partner),
+        remote(sv_s, sv_r, xss.at[0], xrs.at[0], partner),
+        remote(sn_s, sn_r, xss.at[1], xrs.at[1], partner),
     )
     for j in range(2):
         for r in range(NBLK):
+            advance(cots)
             queries = qs[j, rows_of(r), :]
             rows_num = jnp.zeros((BLK, HEAD_V), F32)
             rows_den = jnp.zeros((BLK, 1), F32)
@@ -522,18 +1221,21 @@
             y_ref[rows_of(r), j * HEAD_V : (j + 1) * HEAD_V] = (top / bottom).astype(BF)
     for copy in copies:
         copy.wait_send()
-
-
-def linear_forward(p1, tables):
+    finish(cots)
+
+
+def linear_forward(raw, select, tables, cot):
     return pl.pallas_call(
         linear_forward_kernel,
         out_shape=(
-            jax.ShapeDtypeStruct((HALF_TOK, 2 * HEAD_V), BF),
-            jax.ShapeDtypeStruct((2, HEAD_V, STATE), BF),
-            jax.ShapeDtypeStruct((2, 8, STATE), F32),
+            sds((HALF_TOK, 2 * HEAD_V)),
+            sds((HALF_TOK, 3 * HEAD_V)),
+            sds((2, HEAD_V, STATE)),
+            sds((2, 8, STATE), F32),
+            sds((8, TOK // 2, D)),
         ),
-        in_specs=[VM] * 4,
-        out_specs=(VM, VM, VM),
+        in_specs=[VM] * 6,
+        out_specs=(VM, VM, VM, VM, ANY),
         scratch_shapes=[
             pltpu.VMEM((2, HALF_TOK, 128), BF),
             pltpu.VMEM((2, HALF_TOK, 128), BF),
@@ -545,9 +1247,10 @@
             pltpu.VMEM((2, 8, STATE), F32),
             pltpu.SemaphoreType.DMA((2,)),
             pltpu.SemaphoreType.DMA((2,)),
-        ],
+        ]
+        + HALF_SCRATCH,
         compiler_params=params(7),
-    )(p1, *tables)
+    )(raw, select, *tables, cot)
 
 
 def linear_backward_kernel(
@@ -555,9 +1258,11 @@
     dy_ref,
     sv_ref,
     sn_ref,
+    sel_ref,
     e_ref,
     t_ref,
     pick_ref,
+    raw_ref,
     dp_ref,
     qs,
     ks,
@@ -575,6 +1280,8 @@
     partner = {"xh": 1 - xh}
     edge = jnp.where(xh == 0, EDGE, HALF_TOK - EDGE)
     bias1, bias2, coef = t_ref[0:1, :], t_ref[1:2, :], t_ref[2:3, :]
+    barrier = pltpu.get_barrier_semaphore()
+    pl.semaphore_signal(barrier, inc=1, device_id=partner, device_id_type=MESH)
     small = p_ref[:, 2 * HEAD_V :]
     for j in range(2):
         qs[j] = dnn(small, pick_ref[2 * j]).astype(BF)
@@ -639,7 +1346,7 @@
             tn = tn + jnp.sum(shift * phi, axis=0, keepdims=True)
         tv_s[j] = (tv * coef).astype(BF)
         tn_s[j] = jnp.broadcast_to(tn * coef, (8, STATE))
-    greet((partner,))
+    pl.semaphore_wait(barrier, 1)
     copies = (
         remote(tv_s, tv_r, ss.at[0], rs.at[0], partner),
         remote(tn_s, tn_r, ss.at[1], rs.at[1], partner),
@@ -665,17 +1372,19 @@
             placed = placed + dnt(dq[j, rows_of(r), :].astype(BF), pick_ref[2 * j])
             placed = placed + dnt(key_grad.astype(BF), pick_ref[2 * j + 1])
         dp_ref[rows_of(r), 2 * HEAD_V :] = placed.astype(BF)
+        raw_ref[rows_of(r), :] = dnt(dp_ref[rows_of(r), :], sel_ref[...]).astype(BF)
     for copy in copies:
         copy.wait_send()
 
 
-def linear_backward(p1, dy, sv, sn, tables):
+def linear_backward(p1, dy, sv, sn, select, tables):
     return pl.pallas_call(
         linear_backward_kernel,
-        out_shape=jax.ShapeDtypeStruct((HALF_TOK, 3 * HEAD_V), BF),
-        in_specs=[VM] * 7,
+        out_shape=sds((HALF_TOK, 16 * BIN_PAD)),
+        in_specs=[VM] * 8,
         out_specs=VM,
         scratch_shapes=[
+            pltpu.VMEM((HALF_TOK, 3 * HEAD_V), BF),
             pltpu.VMEM((2, HALF_TOK, 128), BF),
             pltpu.VMEM((2, HALF_TOK, 128), BF),
             pltpu.VMEM((2, HALF_TOK, 128), F32),
@@ -689,7 +1398,7 @@
             pltpu.SemaphoreType.DMA((2,)),
         ],
         compiler_params=params(8),
-    )(p1, dy, sv, sn, *tables)
+    )(p1, dy, sv, sn, select, *tables)
 
 
 WBLK = 128
@@ -703,39 +1412,72 @@
     return (u <= t) & (t - u < WINDOW) & ((t >= edge) == (u >= edge)) & (u >= lowest)
 
 
-def window_forward_kernel(p_ref, cos_ref, sin_ref, y_ref, q_ref, kv_ref, ss, rs):
+def window_forward_kernel(
+    h_ref,
+    w_ref,
+    cos_ref,
+    sin_ref,
+    cot_ref,
+    y_ref,
+    q_ref,
+    kv_ref,
+    hi_ref,
+    h,
+    w,
+    sems,
+    xss,
+    xrs,
+    buf,
+    ss,
+    rs,
+    ls,
+):
+    ring = Ring()
     xh = lax.axis_index("xh")
     partner = {"xh": 1 - xh}
     edge = jnp.where(xh == 0, EDGE, HALF_TOK - EDGE)
     lowest = jnp.where(xh == 0, 0, -WINDOW)
-
-    def turned(r, part):
-        rows = slice(r * WBLK, (r + 1) * WBLK)
-        vecs = p_ref[rows, part * 128 : (part + 1) * 128]
+    loads = (
+        load(w_ref.at[:, :, pl.ds(0, 48), :], w, sems.at[0]),
+        load(h_ref, h, sems.at[1]),
+    )
+    barrier = pltpu.get_barrier_semaphore()
+    for device in (ring.up, ring.dn, ring.sib, partner):
+        pl.semaphore_signal(barrier, inc=1, device_id=device, device_id_type=MESH)
+    buf[ring.z * 2 + ring.c] = cot_ref[TOK // 2 :, :]
+    pl.semaphore_wait(barrier, 4)
+    cots = gather_steps(ring, buf, hi_ref, ss, rs, ls, TOK // 2)
+    advance(cots)
+    for copy in loads:
+        copy.wait()
+    size = 2 * TOK
+    blocks = HALF_TOK // size
+
+    def turned(vecs, rows):
         return (
             vecs * cos_ref[rows, :] + pltpu.roll(vecs, HEAD_V // 2, 1) * sin_ref[rows, :]
         ).astype(BF)
 
-    blocks = HALF_TOK // WBLK
     for r in (blocks - 1,) + tuple(range(blocks - 1)):
-        rows = slice(r * WBLK, (r + 1) * WBLK)
-        shifted = slice(WINDOW + r * WBLK, WINDOW + (r + 1) * WBLK)
+        rows = slice(r * size, (r + 1) * size)
+        shifted = slice(WINDOW + r * size, WINDOW + (r + 1) * size)
+        tokens = h[2 * r : 2 * r + 2].reshape(size, D)
         for j in range(2):
-            q_ref[rows, j * 128 : (j + 1) * 128] = turned(r, 3 * j)
-            kv_ref[shifted, j * 128 : (j + 1) * 128] = turned(r, 3 * j + 1)
-            kv_ref[shifted, (2 + j) * 128 : (3 + j) * 128] = p_ref[
-                rows, (3 * j + 2) * 128 : (3 * j + 3) * 128
-            ].astype(BF)
+            mat = w[2 * j : 2 * j + 2].reshape(384, D)
+            proj = dnt(tokens, mat)
+            q_ref[rows, j * 128 : (j + 1) * 128] = turned(proj[:, :128], rows)
+            kv_ref[shifted, j * 128 : (j + 1) * 128] = turned(proj[:, 128:256], rows)
+            kv_ref[shifted, (2 + j) * 128 : (3 + j) * 128] = proj[:, 256:].astype(BF)
         if r == blocks - 1:
-            greet((partner,))
             copy = remote(
                 kv_ref.at[pl.ds(HALF_TOK, WINDOW), :],
                 kv_ref.at[pl.ds(0, WINDOW), :],
-                ss,
-                rs,
+                xss,
+                xrs,
                 partner,
             )
-    for r in tuple(range(1, blocks)) + (0,):
+        advance(cots)
+    for r in tuple(range(1, HALF_TOK // WBLK)) + (0,):
         if r == 0:
             copy.wait_recv()
         rows = slice(r * WBLK, (r + 1) * WBLK)
@@ -750,22 +1492,32 @@
             y_ref[rows, head] = dnn(
                 probs.astype(BF), kv_ref[keys, (2 + j) * 128 : (3 + j) * 128]
             ).astype(BF)
+        advance(cots)
     copy.wait_send()
-
-
-def window_forward(p2, cosine, sine):
+    finish(cots)
+
+
+def window_forward(h, w, cosine, sine, cot):
     return pl.pallas_call(
         window_forward_kernel,
         out_shape=(
-            jax.ShapeDtypeStruct((HALF_TOK, 256), BF),
-            jax.ShapeDtypeStruct((HALF_TOK, 256), BF),
-            jax.ShapeDtypeStruct((HALF_TOK + WINDOW, 512), BF),
+            sds((HALF_TOK, 256)),
+            sds((HALF_TOK, 256)),
+            sds((HALF_TOK + WINDOW, 512)),
+            sds((8, TOK // 2, D)),
         ),
-        in_specs=[VM] * 3,
-        out_specs=(VM, VM, VM),
-        scratch_shapes=[pltpu.SemaphoreType.DMA, pltpu.SemaphoreType.DMA],
+        in_specs=[ANY, ANY, VM, VM, VM],
+        out_specs=(VM, VM, VM, ANY),
+        scratch_shapes=[
+            pltpu.VMEM((8, TOK, D), BF),
+            pltpu.VMEM((4, 4, 48, D), BF),
+            pltpu.SemaphoreType.DMA((2,)),
+            pltpu.SemaphoreType.DMA,
+            pltpu.SemaphoreType.DMA,
+        ]
+        + HALF_SCRATCH,
         compiler_params=params(9),
-    )(p2, cosine, sine)
+    )(h, w, cosine, sine, cot)
 
 
 def window_backward_kernel(
@@ -775,6 +1527,8 @@
     partner = {"xh": 1 - xh}
     edge = jnp.where(xh == 0, EDGE, HALF_TOK - EDGE)
     lowest = jnp.where(xh == 0, 0, -WINDOW)
+    barrier = pltpu.get_barrier_semaphore()
+    pl.semaphore_signal(barrier, inc=1, device_id=partner, device_id_type=MESH)
     dkv[...] = jnp.zeros_like(dkv)
     blocks = HALF_TOK // WBLK
 
@@ -806,7 +1560,7 @@
             dkv[keys, head] += dtn(score_grad, queries) * INV_ROOT_V
             dkv[keys, vals] += dtn(probs.astype(BF), grads)
         if r == 0:
-            greet((partner,))
+            pl.semaphore_wait(barrier, 1)
             copy = remote(dkv.at[pl.ds(0, WINDOW), :], halo, ss, rs, partner)
     for r in range(blocks):
         rows = slice(r * WBLK, (r + 1) * WBLK)
@@ -838,14 +1592,6 @@
         ],
         compiler_params=params(10),
     )(q, kv, dy, cosine, sine)
-
-
-def plane_gather(rows):
-    return lax.all_gather(rows, PLANE, axis=0, tiled=True)
-
-
-def plane_reduce(rows):
-    return lax.psum_scatter(rows.astype(BF), PLANE, scatter_dimension=0, tiled=True).astype(F32)
 
 
 def padded(rows, count):
@@ -877,6 +1623,18 @@
     gains = [gain.reshape(1, D) for gain in (gain_a, gain_b, gain_c)]
     units = mlp_down.shape[0]
     wide = based_in.shape[1]
+    win_all = lax.all_gather(
+        jnp.concatenate([swa_in.T, swa_out], axis=0), PLANE, axis=0, tiled=True
+    ).reshape(4, 4, 64, D)
+    ff_all = lax.all_gather(
+        jnp.concatenate(
+            [padded(part, UNIT_PAD) for part in (mlp_in[:, 0, :].T, mlp_in[:, 1, :].T, mlp_down)],
+            axis=0,
+        ),
+        PLANE,
+        axis=0,
+        tiled=True,
+    ).reshape(16, 3 * UNIT_PAD, D)
     segment, position = place()
     first = (lax.axis_index("z") * 2 + lax.axis_index("c")) * TOK
     my_segment = lax.dynamic_slice_in_dim(segment, first, TOK)
@@ -886,8 +1644,9 @@
         lengths[0, 0],
         jnp.where(my_segment == 1, lengths[0, 1], lengths[0, 2]),
     )
-    valid = (my_position < chosen).astype(F32)
-    cot_local = cotangent.astype(F32) * valid[:, None]
+    valid = (my_position < chosen)[:, None]
+    cot_low = jnp.where(valid, cotangent, jnp.zeros_like(cotangent))
+    cot_local = cot_low.astype(F32)
     frequency = jnp.exp(
         -math.log(10000.0) * jnp.arange(HEAD_V // 2, dtype=F32) * 2.0 / HEAD_V
     )
@@ -895,103 +1654,48 @@
     cosine, sine = jnp.cos(angles), jnp.sin(angles)
     cosine = jnp.concatenate([cosine, cosine], axis=1)
     sine = jnp.concatenate([-sine, sine], axis=1)
-
-    lin_all = plane_gather(jnp.concatenate([padded(based_in.T, BIN_PAD), based_out], axis=0))
-    win_all = plane_gather(jnp.concatenate([swa_in.T, swa_out], axis=0))
-    ff_all = plane_gather(
-        jnp.concatenate(
-            [padded(part, UNIT_PAD) for part in (mlp_in[:, 0, :].T, mlp_in[:, 1, :].T, mlp_down)],
-            axis=0,
-        )
-    )
-
-    def pieces(rows, *counts):
-        rows = rows.reshape(16, sum(counts), D)
-        ends = np.cumsum((0,) + counts)
-        return [
-            rows[:, ends[i] : ends[i + 1]].reshape(16 * counts[i], D) for i in range(len(counts))
-        ]
-
-    lin_rows, lin_out = pieces(lin_all, BIN_PAD, 16)
-    win_in, win_out = pieces(win_all, 48, 16)
-    ff_gate, ff_up, ff_out = pieces(ff_all, UNIT_PAD, UNIT_PAD, UNIT_PAD)
-    lin_heads = lin_rows.reshape(16, BIN_PAD, D)[:, :wide].reshape(2, 8 * wide, D)
-    lin_in = jnp.concatenate(
-        [
-            lin_heads[:, 2 * FEAT :].reshape(2 * HEAD_V, D),
-            lin_heads[:, : 2 * FEAT].reshape(4 * FEAT, D),
-            jnp.zeros((128 - 4 * FEAT, D), BF),
-        ],
-        axis=0,
-    )
-    table_e, table_t, table_p = state_tables()
-    tables = (jnp.asarray(table_e, BF), jnp.asarray(table_t, F32), jnp.asarray(table_p, BF))
-
-    h1 = first_gather(block_input, gains[0])
-    cot_all = lax.all_gather(cot_local.astype(BF), RING, axis=0, tiled=True)
-    p1 = dnt(h1, lin_in).astype(BF)
-    y1, state_v, state_n = linear_forward(p1, tables)
-    x2, h2 = forward_step(y1, lin_out, block_input, gains[1], 2)
-    p2 = dnt(h2, win_in)
-    y2, queries, key_vals = window_forward(p2, cosine, sine)
-    x3, h3 = forward_step(y2, win_out, x2, gains[2], 3)
-    gate = dnt(h3, ff_gate)
-    up = dnt(h3, ff_up)
-    sig = jax.nn.sigmoid(gate)
-    act = (gate * sig * up).astype(BF)
-    out_sum = lax.psum_scatter(dnn(act, ff_out).astype(BF), RING, scatter_dimension=0, tiled=True)
+    tables = tuple(
+        jnp.asarray(table, kind) for table, kind in zip(state_tables(), (BF, F32, BF))
+    )
+    select = jnp.asarray(select_table(wide), BF)
+
+    shard = jnp.concatenate([padded(based_in.T, BIN_PAD), based_out], axis=0)
+    h1, lin_all, raw = first_step(block_input, gains[0], shard)
+    y1, p1, state_v, state_n, cot_lo = linear_forward(raw, select, tables, cot_low)
+    x2, h2 = forward_step(y1, lin_all, BIN_PAD, block_input, gains[1], 2)
+    y2, queries, key_vals, cot_hi = window_forward(h2, win_all, cosine, sine, cot_low)
+    x3, h3 = forward_step(y2, win_all, 48, x2, gains[2], 3)
+    act, d_gu, down = mlp_step(h3, cot_lo, cot_hi, ff_all)
+    out_sum = lax.psum_scatter(down, RING, scatter_dimension=0, tiled=True)
+    dx3, grad_c, e3, d_y2, ff_grads = mlp_back_step(
+        d_gu, act, ff_all, win_all, h3, cot_lo, cot_hi, x3, gains[2], cot_local
+    )
+    ff_grads = lax.psum_scatter(
+        ff_grads.reshape(-1, D), PLANE, scatter_dimension=0, tiled=True
+    ).astype(F32)
+    d_p2 = window_backward(queries, key_vals, d_y2, cosine, sine)
+    dx2, grad_b, e2, d_y1, win_grads = window_back_out_step(
+        d_p2, win_all, lin_all, h2, y2, e3, x2, gains[1], dx3
+    )
+    d_p1 = linear_backward(p1, d_y1, state_v, state_n, select, tables)
+    input_grad, grad_a, grad_b, grad_c, lin_grads = last_step(
+        d_p1, lin_all, h1, y1, e2, block_input, gains[0], dx2, grad_b, grad_c
+    )
     block_output = (x3 + out_sum.astype(F32)).astype(BF)
-
-    d_act = dnt(cot_all, ff_out)
-    d_gate = (d_act * up * sig * (1.0 + gate * (1.0 - sig))).astype(BF)
-    d_up = (d_act * gate * sig).astype(BF)
-    d_gu = jnp.concatenate([d_gate, d_up], axis=1)
-    ff_in = jnp.concatenate([ff_gate, ff_up], axis=0)
-
-    def reduce_together(*grads):
-        rows = [grad.astype(BF).reshape(16, -1, D) for grad in grads]
-        ends = np.cumsum([0] + [part.shape[1] for part in rows])
-        total = plane_reduce(jnp.concatenate(rows, axis=1).reshape(-1, D))
-        return [total[ends[i] : ends[i + 1]] for i in range(len(rows))]
-
-    grad_down, grad_gate, grad_up = reduce_together(
-        dtn(act, cot_all), dtn(d_gate, h3), dtn(d_up, h3)
-    )
-    dx3, grad_c, e3 = backward_step(d_gu, ff_in, x3, gains[2], cot_local, 4)
-    d_y2 = dnt(e3, win_out).astype(BF)
-    grad_win_out = dtn(y2, e3)
-    d_p2 = window_backward(queries, key_vals, d_y2, cosine, sine)
-    grad_win_in = dtn(d_p2, h2)
-    dx2, grad_b, e2 = backward_step(d_p2, win_in, x2, gains[1], dx3, 5)
-    d_y1 = dnt(e2, lin_out).astype(BF)
-    grad_lin_out = dtn(y1, e2)
-    d_p1 = linear_backward(p1, d_y1, state_v, state_n, tables)
-    lin_grad = dtn(d_p1, h1).astype(BF)
-    lin_grad = jnp.concatenate(
-        [
-            lin_grad[2 * HEAD_V : 2 * HEAD_V + 4 * FEAT].reshape(2, 2 * FEAT, D),
-            lin_grad[: 2 * HEAD_V].reshape(2, HEAD_V, D),
-        ],
-        axis=1,
-    ).reshape(16, wide, D)
-    lin_grad = jnp.pad(lin_grad, ((0, 0), (0, BIN_PAD - wide), (0, 0))).reshape(16 * BIN_PAD, D)
-    grad_win_in, grad_win_out, grad_lin_in, grad_lin_out = reduce_together(
-        grad_win_in, grad_win_out, lin_grad, grad_lin_out
-    )
-    input_grad, grad_a = last_step(d_p1, lin_in, block_input, gains[0], dx2)
-    gain_sums = lax.psum(jnp.concatenate([grad_a, grad_b, grad_c], axis=0), ALL)
+    gate_grad = ff_grads[:units]
+    up_grad = ff_grads[UNIT_PAD : UNIT_PAD + units]
     return (
         block_output,
         input_grad,
-        gain_sums[0],
-        grad_lin_in[:wide].T,
-        grad_lin_out,
-        gain_sums[1],
-        grad_win_in.T,
-        grad_win_out,
-        gain_sums[2],
-        jnp.stack([grad_gate[:units].T, grad_up[:units].T], axis=1),
-        grad_down[:units],
+        grad_a.reshape(D),
+        lin_grads[:wide].T,
+        lin_grads[BIN_PAD:],
+        grad_b.reshape(D),
+        win_grads[:48].T,
+        win_grads[48:],
+        grad_c.reshape(D),
+        jnp.stack([gate_grad.T, up_grad.T], axis=1),
+        ff_grads[2 * UNIT_PAD : 2 * UNIT_PAD + units],
     )
 
 

time: 626 us -> 497 us (0.79)
  Pallas kernels: 311 us -> 449 us
  matrix products: 74.9 us -> 0 us
  waiting for transfers between devices: 73.1 us -> 0.09 us
  blocking collectives: 65.6 us -> 0 us
  local copies, waits for them, and re-layouts: 49.2 us -> 12.3 us
  other arithmetic: 32.4 us -> 13.1 us
    pallas_call x9 -> x10, Pallas kernels: 299 us -> 437 us  [the longest x2 99 us: forward_step(): pl.pallas_call(functools.partial(forward_kernel, off), out_shape=(sds((TO...]
    dot_general x15 -> x0, matrix products: 74.9 us -> none  [the longest x7 45.6 us: dnt(): lax.dot_general(a, b, (((1,), (1,)), ((), ())), preferred_element_type=F32)]
    psum x1 -> x0, blocking collectives: 65.6 us -> none  [body(): gain_sums = lax.psum(jnp.concatenate([grad_a, grad_b, grad_c], axis=0), ALL)]
    reduce_scatter x3 -> x2, waiting for transfers between devices: 50.8 us -> 0.01 us  [the longest x1 0.01 us: body(): out_sum = lax.psum_scatter(down, RING, scatter_dimension=0, tiled=True)]
    all_gather x4 -> x2, waiting for transfers between devices: 22.2 us -> 0.02 us  [the longest x1 0.02 us: body(): lax.all_gather(jnp.concatenate([padded(part, UNIT_PAD) for part in (mlp_i...]
    concatenate x9 -> x2, other arithmetic: 21.9 us -> 2.41 us  [the longest x1 1.72 us: body(): jnp.concatenate([swa_in.T, swa_out], axis=0)]
    slice x12 -> x3, local copies, waits for them, and re-layouts: 20.7 us -> 3.1 us  [the longest x1 1.66 us: body(): lin_grads[BIN_PAD:]]
    unnamed x136 -> x29, local copies, waits for them, and re-layouts: 17.9 us -> 4.24 us
  transfers between devices with their start and end apart: 7 -> 4, of which waited for: 3 -> 0; matrix products, arithmetic and copies ran while one was open for 17% -> 4% of each run, Pallas kernels for 50% -> 86%
where the time goes in v2:
time: 497 us; the launch traced here: 489 us
  Pallas kernels  449 us (90%)
  between operations  14.5 us (3%)
  other arithmetic  13.1 us (3%)
  local copies, waits for them, and re-layouts  12.3 us (2%)
    pallas_call x2, Pallas kernels, forward_step(): pl.pallas_call(functools.partial(forward_kernel, off), out_shape=(sds((TO...  99 us
    pallas_call x1, Pallas kernels, window_back_out_step(): pl.pallas_call(window_back_out_kernel, out_shape=(sds((TOK, D), F32), sds...  77.3 us
    pallas_call x1, Pallas kernels, mlp_back_step(): pl.pallas_call(mlp_back_kernel, out_shape=(sds((TOK, D), F32), sds((1, D)...  73.6 us
    pallas_call x1, Pallas kernels, last_step(): pl.pallas_call(last_kernel, out_shape=(sds((TOK, D), F32), sds((1, D), F3...  53.8 us
    pallas_call x1, Pallas kernels, first_step(): pl.pallas_call(first_kernel, out_shape=(sds((8, TOK, D)), sds((4, 4, BIN_...  39.7 us
    pallas_call x1, Pallas kernels, mlp_step(): pl.pallas_call(mlp_kernel, out_shape=(sds((HALF_TOK, 2 * CHUNK)), sds((HA...  26.8 us
    pallas_call x1, Pallas kernels, linear_backward(): pl.pallas_call(linear_backward_kernel, out_shape=sds((HALF_TOK, 16 * BIN_...  23 us
    pallas_call x1, Pallas kernels, window_forward(): pl.pallas_call(window_forward_kernel, out_shape=(sds((HALF_TOK, 256)), sd...  22.2 us
  transfers between devices with their start and end apart: 4, of which 0 were waited for; matrix products, arithmetic and copies ran while one was open for 4% of the time, Pallas kernels for 86%

profile of v2, /device:TPU:0, one launch (start us, length us, event | category | flops | bytes accessed | tf_op | source)
XLA Modules:
  0.0 489.2 jit_solution(5280803346402343514)
XLA Ops:
  7.2 1.7 pad_maximum_fusion.3
  9.0 1.7 fusion.14
  11.0 0.9 fusion.5
  12.0 0.7 fusion.7.shard_ref
  12.7 39.7 %shard_map.239 = (bf16[8,128,2048]{2,1,0:T(8,128)(2,1)}, bf16[4,4,48,2048]{3,2,1,0:T(8,128)(2,1)}, bf16[1024,512]{1,0:T(8,128)(2,1)}) custom-call(bf16[128,2048]{1,0:T(8,128)(2,1)} %v_ref.1, f32[1,2048]{1,0:T(1,128)} %bitcast.45, bf16[48,2048]{1,0:T(8,128)(2,1)} %fusion.7.shard_ref), custom_call_target="tpu_custom_call" | custom-call | tf_op jit(solution)/shard_map/pallas_call | solution.py:481
  52.4 0.6 fusion.15
  53.0 2.0 fusion.12
  55.0 1.3 fusion.13
  56.3 21.5 %shard_map.240 = (bf16[1024,256]{1,0:T(8,128)(2,1)}, bf16[1024,384]{1,0:T(8,128)(2,1)}, bf16[2,128,256]{2,1,0:T(8,128)(2,1)}, f32[2,8,256]{2,1,0:T(8,128)}, bf16[8,64,2048]{2,1,0:T(8,128)(2,1)}) custom-call(bf16[1024,512]{1,0:T(8,128)(2,1)} %get-tuple-element.45.raw_ref, bf16[512,384]{1,0:T(8,128)(2,1)} %constant.51.clone.sel_ref, ...), custom_call_target="tpu_custom_call" | custom-call | tf_op jit(solution)/shard_map/pallas_call | solution.py:1228
  77.9 49.3 %shard_map.241 = (f32[128,2048]{1,0:T(8,128)}, bf16[8,128,2048]{2,1,0:T(8,128)(2,1)}) custom-call(bf16[1024,256]{1,0:T(8,128)(2,1)} %get-tuple-element.46.a_ref.y_ref, bf16[4,4,48,2048]{3,2,1,0:T(8,128)(2,1)} %get-tuple-element.47.w_ref.wo_ref, bf16[128,2048]{1,0:T(8,128)(2,1)} %v_ref.1, f32[1,2048]{1,0:T(1,128)} %bitcast.43), custom_call_target="tpu_custom_call" | custom-call | tf_op jit(solution)/shard_map/pallas_call | solution.py:543
  127.2 1.9 fusion.8
  129.1 1.3 pad_maximum_fusion.1
  130.5 22.2 %shard_map.242 = (bf16[1024,256]{1,0:T(8,128)(2,1)}, bf16[1024,256]{1,0:T(8,128)(2,1)}, bf16[1088,512]{1,0:T(8,128)(2,1)}, bf16[8,64,2048]{2,1,0:T(8,128)(2,1)}) custom-call(bf16[8,128,2048]{2,1,0:T(8,128)(2,1)} %get-tuple-element.48.h_ref, bf16[4,4,64,2048]{3,2,1,0:T(8,128)(2,1)} %bitcast.34, f32[1024,128]{1,0:T(8,128)} %get-tuple-element.104.cos_ref, ...), custom_call_target="tpu_custom_call" | custom-call | tf_op jit(solution)/shard_map/pallas_call | solution.py:1501
  152.7 49.7 %shard_map.243 = (f32[128,2048]{1,0:T(8,128)}, bf16[8,128,2048]{2,1,0:T(8,128)(2,1)}) custom-call(bf16[1024,256]{1,0:T(8,128)(2,1)} %get-tuple-element.49.a_ref.y_ref, bf16[4,4,64,2048]{3,2,1,0:T(8,128)(2,1)} %bitcast.35, f32[128,2048]{1,0:T(8,128)} %get-tuple-element.50.x_ref.v_ref, f32[1,2048]{1,0:T(1,128)} %bitcast.47), custom_call_target="tpu_custom_call" | custom-call | tf_op jit(solution)/shard_map/pallas_call | solution.py:543
  202.4 26.8 %shard_map.244 = (bf16[1024,768]{1,0:T(8,128)(2,1)}, bf16[1024,1536]{1,0:T(8,128)(2,1)}, bf16[1024,2048]{1,0:T(8,128)(2,1)}) custom-call(bf16[8,128,2048]{2,1,0:T(8,128)(2,1)} %get-tuple-element.52.h_ref, bf16[8,64,2048]{2,1,0:T(8,128)(2,1)} %get-tuple-element.53.lo_ref, bf16[8,64,2048]{2,1,0:T(8,128)(2,1)} %get-tuple-element.54.hi_ref, ...), custom_call_target="tpu_custom_call" | custom-call | tf_op jit(solution)/shard_map/pallas_call | solution.py:621
  229.3 73.6 %shard_map.245 = (f32[128,2048]{1,0:T(8,128)}, f32[1,2048]{1,0:T(1,128)}, bf16[8,128,2048]{2,1,0:T(8,128)(2,1)}, bf16[1024,256]{1,0:T(8,128)(2,1)}, bf16[16,144,2048]{2,1,0:T(8,128)(2,1)}) custom-call(bf16[1024,1536]{1,0:T(8,128)(2,1)} %get-tuple-element.59.d_ref, bf16[1024,768]{1,0:T(8,128)(2,1)} %get-tuple-element.60.act_ref, ...), custom_call_target="tpu_custom_call" | custom-call | tf_op jit(solution)/shard_map/pallas_call | solution.py:753
  302.9 12.1 %shard_map.246.d_ref = bf16[1024,768]{1,0:T(8,128)(2,1)} custom-call(bf16[1024,256]{1,0:T(8,128)(2,1)} %get-tuple-element.57.q_ref, bf16[1088,512]{1,0:T(8,128)(2,1)} %get-tuple-element.58.kv_ref, bf16[1024,256]{1,0:T(8,128)(2,1)} %get-tuple-element.61.dy_ref, f32[1024,128]{1,0:T(8,128)} %get-tuple-element.104.cos_ref, f32[1024,128]{1,0:T(8,128)} %get-tuple-element.105.sin_ref), custom_call_target="tpu_custom_call" | custom-call | tf_op jit(solution)/shard_map/pallas_call | solution.py:1582
  315.1 77.3 %shard_map.247 = (f32[128,2048]{1,0:T(8,128)}, f32[1,2048]{1,0:T(1,128)}, bf16[8,128,2048]{2,1,0:T(8,128)(2,1)}, bf16[1024,256]{1,0:T(8,128)(2,1)}, f32[64,2048]{1,0:T(8,128)}) custom-call(bf16[1024,768]{1,0:T(8,128)(2,1)} %shard_map.246.d_ref, bf16[4,4,64,2048]{3,2,1,0:T(8,128)(2,1)} %bitcast.37, bf16[4,4,48,2048]{3,2,1,0:T(8,128)(2,1)} %get-tuple-element.47.w_ref.wo_ref, ...), custom_call_target="tpu_custom_call" | custom-call | tf_op jit(solution)/shard_map/pallas_call | solution.py:878
  392.4 23.0 %shard_map.248.d_ref = bf16[1024,512]{1,0:T(8,128)(2,1)} custom-call(bf16[1024,384]{1,0:T(8,128)(2,1)} %get-tuple-element.56.p_ref, bf16[1024,256]{1,0:T(8,128)(2,1)} %get-tuple-element.64.dy_ref, bf16[2,128,256]{2,1,0:T(8,128)(2,1)} %get-tuple-element.65.sv_ref, f32[2,8,256]{2,1,0:T(8,128)} %get-tuple-element.66.sn_ref, ...), custom_call_target="tpu_custom_call" | custom-call | tf_op jit(solution)/shard_map/pallas_call | solution.py:1381
  415.5 53.8 %shard_map.249 = (f32[128,2048]{1,0:T(8,128)}, f32[1,2048]{1,0:T(1,128)}, f32[1,2048]{1,0:T(1,128)}, f32[1,2048]{1,0:T(1,128)}, f32[48,2048]{1,0:T(8,128)}) custom-call(bf16[1024,512]{1,0:T(8,128)(2,1)} %shard_map.248.d_ref, bf16[4,4,48,2048]{3,2,1,0:T(8,128)(2,1)} %get-tuple-element.47.w_ref.wo_ref, bf16[8,128,2048]{2,1,0:T(8,128)(2,1)} %get-tuple-element.67.h_ref, ...), custom_call_target="tpu_custom_call" | custom-call | tf_op jit(solution)/shard_map/pallas_call | solution.py:1042
  469.3 1.7 slice.42
  470.9 0.7 slice.44
  471.6 1.6 slice_bitcast_fusion.3
  473.2 0.8 slice_bitcast_fusion.2
  474.0 1.9 add_convert_fusion
  475.9 1.2 convert_element_type.45
  477.2 1.4 copy.29
  478.7 0.8 slice.50
  479.5 1.0 copy.38
  480.4 0.6 copy.39
  481.0 0.6 copy.40
  481.6 0.6 copy.41
  (42 shorter events, 0.7 us)
Async XLA Ops:
  7.2 123.3 %all-gather.3.cloned.1.call-start = ((), (), s32[]{:S(2)}) async-start(), calls=%async_computation.2 | async-start | bytes 4456448 | tf_op jit(solution)/shard_map/all_gather | solution.py:1626
  7.2 3.8 copy-start.5
  9.0 193.4 %all-gather.5.cloned.1.call-start = ((), (), s32[]{:S(2)}) async-start(), calls=%async_computation.3 | async-start | bytes 10027008 | tf_op jit(solution)/shard_map/all_gather | solution.py:1629
  10.8 1.2 copy-start.6
  10.8 1.2 copy-start.7
  11.0 41.4 %copy-start.11 = (s32[1,3]{1,0:T(1,128)S(1)}, s32[1,3]{1,0:T(1,128)}, u32[]{:S(2)}) copy-start(s32[1,3]{1,0:T(1,128)} %param.18) | copy-start | bytes 40
  11.0 44.0 %copy-start.3 = (bf16[128,2048]{1,0:T(8,128)(2,1)S(1)}, bf16[128,2048]{1,0:T(8,128)(2,1)}, u32[]{:S(2)}) copy-start(bf16[128,2048]{1,0:T(8,128)(2,1)} %param.17) | copy-start | bytes 1572868
  11.9 462.0 %reduce-scatter.3.cloned.1.call-start = ((), (), s32[]{:S(2)}) async-start(), calls=%async_computation.4 | async-start | bytes 4718592 | tf_op jit(solution)/shard_map/reduce_scatter | solution.py:1669
  229.3 246.6 %reduce-scatter.5.cloned.1.call-start = ((), (), s32[]{:S(2)}) async-start(), calls=%async_computation.5 | async-start | bytes 10027008 | tf_op jit(solution)/shard_map/reduce_scatter | solution.py:1673
  415.5 55.5 %copy-start.4 = (f32[64,2048]{1,0:T(8,128)S(1)}, f32[64,2048]{1,0:T(8,128)}, u32[]{:S(2)}) copy-start(f32[64,2048]{1,0:T(8,128)} %get-tuple-element.76) | copy-start | bytes 1572868
  469.2 4.7 copy-start
  477.2 1.5 copy-start.1
  477.2 2.3 copy-start.2
  478.7 1.8 copy-start.10
  478.7 2.4 copy-start.9
  478.7 3.0 copy-start.8
Sparse Core Ops, SparseCore 0:
  10.7 57.1 all-gather.2
  70.7 78.6 all-gather.4
  229.4 49.0 reduce-scatter.2
  303.1 96.0 reduce-scatter.4

commit v3 on v2

--- a/solution.py
+++ b/solution.py
@@ -116,21 +116,25 @@
             advance(other)
 
 
-def gather_steps(ring, buf, out_ref, ss, rs, ls, rows, base=0, ready=None):
+CHUNKS = 2
+
+
+def gather_steps(ring, buf, out_ref, ss, rs, ls, rows, start=0, base=0, keep=True, ready=None):
     half = rows // 2
     me = ring.z * 2 + ring.c
     below, above, far = ring.zm * 2 + ring.c, ring.zp * 2 + ring.c, ring.zz * 2 + ring.c
 
     def send(slot, part, device, index):
-        piece = buf.at[slot, pl.ds(part * half, half), :]
+        piece = buf.at[slot, pl.ds(start + part * half, half), :]
         return remote(piece, piece, ss.at[base + index], rs.at[base + index], device)
 
     local = []
 
-    def keep(slot):
-        copy = pltpu.make_async_copy(buf.at[slot], out_ref.at[slot], ls.at[len(local)])
-        copy.start()
-        local.append(copy)
+    def save(slot):
+        if keep:
+            copy = pltpu.make_async_copy(buf.at[slot], out_ref.at[slot], ls.at[len(local)])
+            copy.start()
+            local.append(copy)
 
     def done(chip):
         if ready is not None:
@@ -144,47 +148,44 @@
     cp[3] = send(me, 0, dn, 3)
     cp[4] = send(me, 0, sib, 4)
     cp[5] = send(me, 1, sib, 5)
-    keep(me)
+    save(me)
     yield
     cp[0].wait_recv()
     cp[6] = send(below, 0, up, 6)
     cp[8] = send(below, 0, sib, 8)
-    yield
     cp[1].wait_recv()
     cp[7] = send(above, 1, dn, 7)
     cp[9] = send(above, 1, sib, 9)
     yield
     cp[2].wait_recv()
     cp[10] = send(below, 1, sib, 10)
-    keep(below)
+    save(below)
     cp[3].wait_recv()
     cp[11] = send(above, 0, sib, 11)
-    keep(above)
+    save(above)
     yield
     cp[4].wait_recv()
     cp[5].wait_recv()
-    keep(ring.z * 2 + ring.oc)
+    save(ring.z * 2 + ring.oc)
     done(ring.z)
-    yield
     cp[8].wait_recv()
     cp[10].wait_recv()
-    keep(ring.zm * 2 + ring.oc)
+    save(ring.zm * 2 + ring.oc)
     done(ring.zm)
     yield
     cp[6].wait_recv()
     cp[12] = send(far, 0, sib, 12)
     cp[7].wait_recv()
     cp[13] = send(far, 1, sib, 13)
-    keep(far)
-    yield
+    save(far)
     cp[9].wait_recv()
     cp[11].wait_recv()
-    keep(ring.zp * 2 + ring.oc)
+    save(ring.zp * 2 + ring.oc)
     done(ring.zp)
     yield
     cp[12].wait_recv()
     cp[13].wait_recv()
-    keep(ring.zz * 2 + ring.oc)
+    save(ring.zz * 2 + ring.oc)
     done(ring.zz)
     for index in range(14):
         cp[index].wait_send()
@@ -192,12 +193,18 @@
         copy.wait()
 
 
-def scatter_steps(ring, product, part, sib_in, far_in, end_in, ss, rs):
-    half = TOK // 2
+def scatter_steps(ring, product, part, sib_in, far_in, end_in, ss, rs, ready):
+    rows = TOK // CHUNKS
+    half = rows // 2
     c, oc = ring.c, ring.oc
     up, dn, sib = ring.up, ring.dn, ring.sib
     order = (ring.zz, ring.zp, ring.zm, ring.z)
     step = 512
+    cp = {}
+
+    def send(q, index, src, dst, device):
+        n = q * 10 + index
+        cp[q, index] = remote(src, dst, ss.at[n], rs.at[n], device)
 
     def multiply(index):
         row = pl.multiple_of(order[index] * (2 * TOK), 2 * TOK)
@@ -210,77 +217,156 @@
             return carry
 
         lax.fori_loop(0, D // step, one, 0)
-        return remote(part.at[index, oc], sib_in.at[index], ss.at[index], rs.at[index], sib)
-
-    def add(index, rows_start, rows, other):
+        for q in range(CHUNKS):
+            at = pl.ds(q * rows, rows)
+            send(q, index, part.at[index, oc, at, :], sib_in.at[index, at, :], sib)
+
+    def add(index, first, count, other):
         def one(i, carry):
-            at = pl.ds(pl.multiple_of(rows_start + i * 16, 16), 16)
-            part[index, c, at, :] = (part[index, c, at, :].astype(F32) + other(i, at)).astype(BF)
+            at = pl.ds(pl.multiple_of(first + i * 16, 16), 16)
+            part[index, c, at, :] = (part[index, c, at, :].astype(F32) + other(at)).astype(BF)
             return carry
 
-        lax.fori_loop(0, rows // 16, one, 0)
+        lax.fori_loop(0, count // 16, one, 0)
+
+    def add_sib(q, index):
+        cp[q, index].wait_recv()
+        add(index, q * rows, rows, lambda at: sib_in[index, at, :].astype(F32))
+
+    def piece(q, which):
+        return pl.ds(q * rows + which * half, half)
+
+    def far(q):
+        add_sib(q, 0)
+        send(q, 4, part.at[0, c, piece(q, 0), :], far_in.at[piece(q, 0), :], up)
+        send(q, 5, part.at[0, c, piece(q, 1), :], far_in.at[piece(q, 1), :], dn)
+
+    def near(q):
+        add_sib(q, 1)
+        send(q, 6, part.at[1, c, piece(q, 1), :], end_in.at[0, piece(q, 1), :], up)
+        add_sib(q, 2)
+        send(q, 7, part.at[2, c, piece(q, 0), :], end_in.at[1, piece(q, 0), :], dn)
+
+    def passed(q):
+        for which, device in ((0, up), (1, dn)):
+            cp[q, 4 + which].wait_recv()
+            at = piece(q, which)
+            add(1 + which, q * rows + which * half, half, lambda at: far_in[at, :].astype(F32))
+            send(q, 8 + which, part.at[1 + which, c, at, :], end_in.at[which, at, :], device)
+
+    multiply(0)
+    multiply(1)
+    far(0)
+    for q in range(1, CHUNKS):
+        far(q)
+    yield
+    multiply(2)
+    near(0)
+    multiply(3)
+    yield
+    passed(0)
+    for q in range(1, CHUNKS):
+        near(q)
+    yield
+    for q in range(1, CHUNKS):
+        passed(q)
+    for q in range(CHUNKS):
+        add_sib(q, 3)
+        for index in range(6, 10):
+            cp[q, index].wait_recv()
+        ready(q)
+        yield
+    for copy in cp.values():
+        copy.wait_send()
+
+
+def rows_reduce_steps(ring, src_ref, q, part, sib_in, far_in, end_in, ss, rs, ls, ready):
+    rows = TOK // CHUNKS
+    half = rows // 2
+    order = (ring.zz, ring.zp, ring.zm, ring.z)
+    up, dn, sib = ring.up, ring.dn, ring.sib
+    cp, loads = {}, []
+
+    def send(index, src, dst, device):
+        cp[index] = remote(src, dst, ss.at[index], rs.at[index], device)
+
+    def source(index, core):
+        start = order[index] * (2 * TOK) + core * TOK + q * rows
+        return src_ref.at[pl.ds(pl.multiple_of(start, 16), rows), :]
+
+    def add(index, first, count, other):
+        def one(i, carry):
+            at = pl.ds(pl.multiple_of(first + i * 16, 16), 16)
+            part[index, at, :] = (part[index, at, :].astype(F32) + other(at)).astype(BF)
+            return carry
+
+        lax.fori_loop(0, count // 16, one, 0)
 
     def add_sib(index):
-        add(index, 0, TOK, lambda i, at: sib_in[index, at, :].astype(F32))
-
-    def add_far(index, which):
-        add(
-            index,
-            which * half,
-            half,
-            lambda i, at: far_in[which, pl.ds(pl.multiple_of(i * 16, 16), 16), :].astype(F32),
-        )
-
-    def send(src, dst, device, index):
-        return remote(src, dst, ss.at[index], rs.at[index], device)
+        loads[index].wait()
+        cp[index].wait_recv()
+        add(index, 0, rows, lambda at: sib_in[index, at, :].astype(F32))
 
     low, high = pl.ds(0, half), pl.ds(half, half)
-    cp = {}
-    cp[0] = multiply(0)
-    cp[1] = multiply(1)
-    cp[0].wait_recv()
+    for index in range(4):
+        send(index, source(index, ring.oc), sib_in.at[index], sib)
+        loads.append(load(source(index, ring.c), part.at[index], ls.at[index]))
+    yield
     add_sib(0)
-    cp[4] = send(part.at[0, c, low, :], far_in.at[0], up, 4)
-    cp[5] = send(part.at[0, c, high, :], far_in.at[1], dn, 5)
-    cp[2] = multiply(2)
-    cp[1].wait_recv()
+    send(4, part.at[0, low, :], far_in.at[low, :], up)
+    send(5, part.at[0, high, :], far_in.at[high, :], dn)
     add_sib(1)
-    cp[6] = send(part.at[1, c, high, :], end_in.at[0, high, :], up, 6)
-    cp[3] = multiply(3)
-    cp[2].wait_recv()
+    send(6, part.at[1, high, :], end_in.at[0, high, :], up)
     add_sib(2)
-    cp[7] = send(part.at[2, c, low, :], end_in.at[1, low, :], dn, 7)
-    yield
-    cp[4].wait_recv()
-    add_far(1, 0)
-    cp[8] = send(part.at[1, c, low, :], end_in.at[0, low, :], up, 8)
-    cp[5].wait_recv()
-    add_far(2, 1)
-    cp[9] = send(part.at[2, c, high, :], end_in.at[1, high, :], dn, 9)
-    cp[3].wait_recv()
+    send(7, part.at[2, low, :], end_in.at[1, low, :], dn)
     add_sib(3)
     yield
-    cp[6].wait_recv()
-    cp[7].wait_recv()
+    for which, device in ((0, up), (1, dn)):
+        cp[4 + which].wait_recv()
+        at = (low, high)[which]
+        add(1 + which, which * half, half, lambda at: far_in[at, :].astype(F32))
+        send(8 + which, part.at[1 + which, at, :], end_in.at[which, at, :], device)
     yield
-    cp[8].wait_recv()
-    cp[9].wait_recv()
-    for index in range(10):
-        cp[index].wait_send()
-
-
+    for index in range(6, 10):
+        cp[index].wait_recv()
+
+    def total(i, carry):
+        at = pl.ds(pl.multiple_of(i * 16, 16), 16)
+        ready(
+            at,
+            pl.ds(pl.multiple_of(q * rows + i * 16, 16), 16),
+            part[3, at, :].astype(F32)
+            + end_in[0, at, :].astype(F32)
+            + end_in[1, at, :].astype(F32),
+        )
+        return carry
+
+    lax.fori_loop(0, rows // 16, total, 0)
+    for copy in cp.values():
+        copy.wait_send()
+
+
+ROWS_SCRATCH = [
+    pltpu.VMEM((4, TOK // CHUNKS, D), BF),
+    pltpu.VMEM((4, TOK // CHUNKS, D), BF),
+    pltpu.VMEM((TOK // CHUNKS, D), BF),
+    pltpu.VMEM((2, TOK // CHUNKS, D), BF),
+    pltpu.SemaphoreType.DMA((10,)),
+    pltpu.SemaphoreType.DMA((10,)),
+    pltpu.SemaphoreType.DMA((4,)),
+]
 SCATTER_SCRATCH = [
     pltpu.VMEM((4, 2, TOK, D), BF),
     pltpu.VMEM((4, TOK, D), BF),
-    pltpu.VMEM((2, TOK // 2, D), BF),
+    pltpu.VMEM((TOK, D), BF),
     pltpu.VMEM((2, TOK, D), BF),
-    pltpu.SemaphoreType.DMA((10,)),
-    pltpu.SemaphoreType.DMA((10,)),
+    pltpu.SemaphoreType.DMA((10 * CHUNKS,)),
+    pltpu.SemaphoreType.DMA((10 * CHUNKS,)),
 ]
 GATHER_SCRATCH = [
     pltpu.VMEM((8, TOK, D), BF),
-    pltpu.SemaphoreType.DMA((14,)),
-    pltpu.SemaphoreType.DMA((14,)),
+    pltpu.SemaphoreType.DMA((14 * CHUNKS,)),
+    pltpu.SemaphoreType.DMA((14 * CHUNKS,)),
     pltpu.SemaphoreType.DMA((8,)),
 ]
 HALF_SCRATCH = [pltpu.VMEM((8, TOK // 2, D), BF)] + GATHER_SCRATCH[1:]
@@ -333,7 +419,7 @@
     ]
 
 
-def plane_reduce_steps(plane, grads, far_a, end_a, far_b, end_b, ss, rs, out_ref):
+def plane_reduce_steps(plane, grads, far_a, end_a, far_b, end_b, ss, rs, outs):
     copies = []
     rows = grads.shape[2]
 
@@ -392,11 +478,13 @@
                     add(view(half, me, None), ends(half, side, None))
             else:
                 cols = pl.ds(half * (D // 2), D // 2)
-                out_ref[:, cols] = (
+                total = (
                     view(half, me, None)[...].astype(F32)
                     + end_in[half, 0].astype(F32)
                     + end_in[half, 1].astype(F32)
                 )
+                for start, out_ref in outs:
+                    out_ref[:, cols] = total[start : start + out_ref.shape[0]]
         yield
     for copy in copies:
         copy.wait_send()
@@ -422,12 +510,47 @@
     return lax.rsqrt(jnp.mean(rows * rows, axis=-1, keepdims=True) + EPSILON)
 
 
-def by_rows(one):
+def by_rows(one, start=0, rows=TOK):
     def step(i, carry):
-        one(pl.ds(pl.multiple_of(i * 16, 16), 16))
+        one(pl.ds(pl.multiple_of(start + i * 16, 16), 16))
         return carry
 
-    lax.fori_loop(0, TOK // 16, step, 0)
+    lax.fori_loop(0, rows // 16, step, 0)
+
+
+def scatter_gather(ring, product, one, scatter, gather, out_ref, done=None, others=()):
+    part, sib_in, far_in, end_in, sss, srs = scatter
+    buf, ss, rs, ls = gather
+    rows = TOK // CHUNKS
+    gathers = []
+
+    def ready(q):
+        by_rows(one, q * rows, rows)
+        last = q == CHUNKS - 1
+        steps = gather_steps(
+            ring,
+            buf,
+            out_ref,
+            ss,
+            rs,
+            ls,
+            rows,
+            start=q * rows,
+            base=14 * q,
+            keep=last,
+            ready=done if last else None,
+        )
+        advance(steps)
+        gathers.append(steps)
+
+    weave(scatter_steps(ring, product, part, sib_in, far_in, end_in, sss, srs, ready), *others)
+    for _ in range(5):
+        for steps in gathers:
+            advance(steps)
+        for other in others:
+            advance(other)
+    for steps in gathers:
+        finish(steps)
 
 
 def total_rows(part, end_in, c, at):
@@ -443,7 +566,7 @@
 
 
 def first_kernel(
-    x_ref, gain_ref, shard_ref, h_out, w_out, p_ref, wide, wss, wrs, buf, ss, rs, ls, wls
+    x_ref, gain_ref, in_ref, out_ref, h_out, w_out, p_ref, wide, wss, wrs, buf, ss, rs, ls, wls
 ):
     ring, plane = Ring(), Plane()
     me = ring.z * 2 + ring.c
@@ -451,7 +574,9 @@
     partners = (ring.up, ring.dn, ring.sib) + plane.neighbours()
     for device in partners:
         pl.semaphore_signal(barrier, inc=1, device_id=device, device_id_type=MESH)
-    wide[plane.x, plane.y] = shard_ref[...]
+    wide[plane.x, plane.y, BIN_PAD // 2 : BIN_PAD, :] = jnp.zeros((BIN_PAD // 2, D), BF)
+    wide[plane.x, plane.y, : in_ref.shape[0], :] = in_ref[...]
+    wide[plane.x, plane.y, BIN_PAD:, :] = out_ref[...]
 
     def one(at):
         rows = x_ref[at, :].astype(F32)
@@ -460,9 +585,15 @@
     by_rows(one)
     pl.semaphore_wait(barrier, len(partners))
     weights = plane_gather_steps(plane, wide, wss, wrs)
+    rows = gather_steps(ring, buf, h_out, ss, rs, ls, TOK)
     advance(weights)
-    rows = gather_steps(ring, buf, h_out, ss, rs, ls, TOK)
-    weave(rows, weights)
+    advance(rows)
+    advance(weights)
+    advance(weights)
+    advance(rows)
+    advance(rows)
+    advance(weights)
+    finish(rows)
     finish(weights)
     keep = load(wide, w_out, wls)
 
@@ -477,7 +608,7 @@
     keep.wait()
 
 
-def first_step(x, gain, shard):
+def first_step(x, gain, rows_in, rows_out):
     return pl.pallas_call(
         first_kernel,
         out_shape=(
@@ -485,7 +616,7 @@
             sds((4, 4, BIN_PAD + 16, D)),
             sds((HALF_TOK, 16 * BIN_PAD)),
         ),
-        in_specs=[VM] * 3,
+        in_specs=[VM] * 4,
         out_specs=(ANY, ANY, VM),
         scratch_shapes=[
             pltpu.VMEM((4, 4, BIN_PAD + 16, D), BF),
@@ -495,7 +626,7 @@
         + GATHER_SCRATCH
         + [pltpu.SemaphoreType.DMA],
         compiler_params=params(1),
-    )(x, gain, shard)
+    )(x, gain, rows_in, rows_out)
 
 
 def forward_kernel(
@@ -528,15 +659,13 @@
     def product(rows, col):
         return dnn(a_ref[rows, :], w[:, :, :, col].reshape(256, -1))
 
-    finish(scatter_steps(ring, product, part, sib_in, far_in, end_in, sss, srs))
-
     def one(at):
         rows = x_ref[at, :].astype(F32) + total_rows(part, end_in, ring.c, at)
         x_out[at, :] = rows
         buf[me, at, :] = (rows * scale_of(rows) * gain_ref[...]).astype(BF)
 
-    by_rows(one)
-    finish(gather_steps(ring, buf, h_out, ss, rs, ls, TOK))
+    scatter = (part, sib_in, far_in, end_in, sss, srs)
+    scatter_gather(ring, product, one, scatter, (buf, ss, rs, ls), h_out)
 
 
 def forward_step(a, w, off, x, gain, collective_id):
@@ -552,11 +681,10 @@
     )(a, w, x, gain)
 
 
-def norm_back_rows(v_ref, gain_ref, grads, at, gain_acc):
+def norm_back_rows(v_ref, gain_ref, grads, at):
     rows = v_ref[at, :].astype(F32)
     scale = scale_of(rows)
     unit = rows * scale
-    gain_acc[...] += grads * unit
     scaled = grads * gain_ref[...]
     return scale * (scaled - unit * jnp.mean(scaled * unit, axis=-1, keepdims=True))
 
@@ -637,9 +765,9 @@
     )(h, lo, hi, w)
 
 
-def mlp_grad_steps(jobs, stage, out_ref, sems):
+def mlp_grad_steps(jobs, stage, out_ref, sems, gain_acc):
     copies = []
-    for n, (lhs, col, rhs, off, half) in enumerate(jobs):
+    for n, (lhs, col, rhs, off, half, w) in enumerate(jobs):
         slot = n % 2
         if n >= 2:
             copies[n - 2].wait()
@@ -648,6 +776,9 @@
             cols = pl.ds(pl.multiple_of(k * 512, 512), 512)
             res = dtn(lhs[:, col : col + CHUNK], rhs[:, :, cols].reshape(HALF_TOK, 512))
             stage[slot, :, :, cols] = res.astype(BF).reshape(8, UNIT_PAD, 512)
+            if w is not None:
+                own = w[8 * half : 8 * half + 8, :, cols].reshape(CHUNK, 512).astype(F32)
+                gain_acc[:, cols] += jnp.sum(res * own, axis=0, keepdims=True)
             return carry
 
         lax.fori_loop(0, 4, one, 0)
@@ -721,32 +852,31 @@
     def grads():
         for copy in late:
             copy.wait()
-        jobs = [(d_ref, n * CHUNK, h, (n // 2) * UNIT_PAD, n % 2) for n in range(4)]
-        jobs += [(act_ref, n * CHUNK, cot, 2 * UNIT_PAD, n) for n in range(2)]
-        yield from mlp_grad_steps(jobs, stage, g_out, gsems)
+        jobs = [
+            (d_ref, n * CHUNK, h, (n // 2) * UNIT_PAD, n % 2, w.at[n // 2]) for n in range(4)
+        ]
+        jobs += [(act_ref, n * CHUNK, cot, 2 * UNIT_PAD, n, None) for n in range(2)]
+        yield from mlp_grad_steps(jobs, stage, g_out, gsems, gain_acc)
 
     weight_grads = grads()
-    weave(
-        scatter_steps(ring, product, part, sib_in, far_in, end_in, sss, srs),
-        weight_grads,
-    )
 
     def one(at):
         grad = total_rows(part, end_in, ring.c, at)
-        rows = res_ref[at, :] + norm_back_rows(v_ref, gain_ref, grad, at, gain_acc)
+        rows = res_ref[at, :].astype(F32) + norm_back_rows(v_ref, gain_ref, grad, at)
         d_out[at, :] = rows
         buf[me, at, :] = rows.astype(BF)
 
-    by_rows(one)
-
-    def ready(chip):
+    def done(chip):
         dy_out[chip_rows(chip), :] = dnt(
             buf[pl.ds(2 * chip, 2)].reshape(2 * TOK, D), wo[...].reshape(256, D)
         ).astype(BF)
 
-    weave(gather_steps(ring, buf, e_out, ss, rs, ls, TOK, ready=ready), weight_grads)
+    scatter = (part, sib_in, far_in, end_in, sss, srs)
+    scatter_gather(
+        ring, product, one, scatter, (buf, ss, rs, ls), e_out, done, (weight_grads,)
+    )
     finish(weight_grads)
-    gain_out[...] = jnp.sum(gain_acc[...], axis=0, keepdims=True)
+    gain_out[...] = gain_acc[...] / gain_ref[...]
 
 
 def mlp_back_step(d, act, w, wo, h, lo, hi, v, gain, res):
@@ -769,7 +899,7 @@
             pltpu.VMEM((2, 8, UNIT_PAD, D), BF),
             pltpu.SemaphoreType.DMA((6,)),
             pltpu.SemaphoreType.DMA((6,)),
-            pltpu.VMEM((16, D), F32),
+            pltpu.VMEM((1, D), F32),
         ]
         + SCATTER_SCRATCH
         + GATHER_SCRATCH,
@@ -799,12 +929,6 @@
     sems,
     gain_acc,
     grads,
-    far_a,
-    end_a,
-    far_b,
-    end_b,
-    gss,
-    grs,
     part,
     sib_in,
     far_in,
@@ -816,7 +940,7 @@
     rs,
     ls,
 ):
-    ring, plane = Ring(), Plane()
+    ring = Ring()
     me = ring.z * 2 + ring.c
     first = load(w_ref.at[:, :, pl.ds(0, 48), :], w, sems.at[0])
     late = [
@@ -824,7 +948,7 @@
         load(e_ref, e, sems.at[2]),
         load(wo_ref.at[:, :, pl.ds(BIN_PAD, 16), :], wo, sems.at[3]),
     ]
-    greet((ring.up, ring.dn, ring.sib) + plane.neighbours())
+    ring.greet()
     gain_acc[...] = jnp.zeros_like(gain_acc)
     first.wait()
 
@@ -835,43 +959,40 @@
         for copy in late:
             copy.wait()
 
-        def one(k, carry):
-            cols = pl.ds(pl.multiple_of(k * 512, 512), 512)
+        for k in range(4):
+            cols = slice(k * 512, (k + 1) * 512)
             rows = h[:, :, cols].reshape(HALF_TOK, 512)
             for i in range(2):
-                res = dtn(d_ref[:, i * 384 : (i + 1) * 384], rows).astype(BF)
-                grads[2 * i : 2 * i + 2, :, :48, cols] = res.reshape(2, 4, 48, 512)
+                res = dtn(d_ref[:, i * 384 : (i + 1) * 384], rows)
+                own = w[2 * i : 2 * i + 2, :, :, cols].reshape(384, 512).astype(F32)
+                gain_acc[:, cols] += jnp.sum(res * own, axis=0, keepdims=True)
+                grads[2 * i : 2 * i + 2, :, :48, cols] = res.astype(BF).reshape(2, 4, 48, 512)
             res = dtn(y_ref[...], e[:, :, cols].reshape(HALF_TOK, 512)).astype(BF)
             grads[:, :, 48:, cols] = res.reshape(4, 4, 16, 512)
-            return carry
-
-        lax.fori_loop(0, 4, one, 0)
-        yield from plane_reduce_steps(
-            plane, grads, far_a, end_a, far_b, end_b, gss, grs, g_out
-        )
+            yield
+        copy = load(grads, g_out, sems.at[4])
+        yield
+        copy.wait()
 
     weight_grads = weights()
-    weave(
-        scatter_steps(ring, product, part, sib_in, far_in, end_in, sss, srs),
-        weight_grads,
-    )
 
     def one(at):
         grad = total_rows(part, end_in, ring.c, at)
-        rows = res_ref[at, :] + norm_back_rows(v_ref, gain_ref, grad, at, gain_acc)
+        rows = res_ref[at, :].astype(F32) + norm_back_rows(v_ref, gain_ref, grad, at)
         d_out[at, :] = rows
         buf[me, at, :] = rows.astype(BF)
 
-    by_rows(one)
-
-    def ready(chip):
+    def done(chip):
         dy_out[chip_rows(chip), :] = dnt(
             buf[pl.ds(2 * chip, 2)].reshape(2 * TOK, D), wo[...].reshape(256, D)
         ).astype(BF)
 
-    weave(gather_steps(ring, buf, e_out, ss, rs, ls, TOK, ready=ready), weight_grads)
+    scatter = (part, sib_in, far_in, end_in, sss, srs)
+    scatter_gather(
+        ring, product, one, scatter, (buf, ss, rs, ls), e_out, done, (weight_grads,)
+    )
     finish(weight_grads)
-    gain_out[...] = jnp.sum(gain_acc[...], axis=0, keepdims=True)
+    gain_out[...] = gain_acc[...] / gain_ref[...]
 
 
 def window_back_out_step(d, w, wo, h, y, e, v, gain, res):
@@ -882,59 +1003,49 @@
             sds((1, D), F32),
             sds((8, TOK, D)),
             sds((HALF_TOK, 256)),
-            sds((64, D), F32),
+            sds((4, 4, 64, D)),
         ),
         in_specs=[VM, ANY, ANY, ANY, VM, ANY, VM, VM, VM],
-        out_specs=(VM, VM, ANY, VM, VM),
+        out_specs=(VM, VM, ANY, VM, ANY),
         scratch_shapes=[
             pltpu.VMEM((4, 4, 48, D), BF),
             pltpu.VMEM((4, 4, 16, D), BF),
             pltpu.VMEM((8, TOK, D), BF),
             pltpu.VMEM((8, TOK, D), BF),
-            pltpu.SemaphoreType.DMA((4,)),
-            pltpu.VMEM((16, D), F32),
+            pltpu.SemaphoreType.DMA((5,)),
+            pltpu.VMEM((1, D), F32),
+            pltpu.VMEM((4, 4, 64, D), BF),
         ]
-        + plane_reduce_scratch(64)
         + SCATTER_SCRATCH
         + GATHER_SCRATCH,
         compiler_params=params(5),
     )(d, w, wo, h, y, e, v, gain, res)
 
 
-def sum_everywhere(ring, plane, pack, ring_in, x_in, y_in, ss, rs):
+def sum_steps(ring, plane, pack, ring_in, x_in, y_in, ss, rs):
     copies = []
-    me = ring.z * 2 + ring.c
-
-    def exchange(value, dst, own, count, device_of):
-        pack[...] = value
-        dst[own] = value
+    stages = (
+        (ring_in, ring.z * 2 + ring.c, 8, lambda t: {"z": lax.div(t, 2), "c": lax.rem(t, 2)}),
+        (x_in, plane.x, 4, plane.at_x),
+        (y_in, plane.y, 4, plane.at_y),
+    )
+    for dst, own, count, device_of in stages:
+        dst[own] = pack[...]
         sent = []
         for o in range(1, count):
-            n = len(copies)
-            sent.append(
-                remote(
-                    pack,
-                    dst.at[own],
-                    ss.at[n],
-                    rs.at[n],
-                    device_of(lax.rem(own + o, count)),
-                )
-            )
-            copies.append(sent[-1])
+            n = len(copies) + len(sent)
+            device = device_of(lax.rem(own + o, count))
+            sent.append(remote(pack, dst.at[own], ss.at[n], rs.at[n], device))
+        yield
         for copy in sent:
             copy.wait_recv()
         for copy in sent:
             copy.wait_send()
+        copies += sent
         total = dst[0]
         for k in range(1, count):
             total = total + dst[k]
-        return total
-
-    total = exchange(
-        pack[...], ring_in, me, 8, lambda t: {"z": lax.div(t, 2), "c": lax.rem(t, 2)}
-    )
-    total = exchange(total, x_in, plane.x, 4, plane.at_x)
-    return exchange(total, y_in, plane.y, 4, plane.at_y)
+        pack[...] = total
 
 
 def last_kernel(
@@ -952,7 +1063,8 @@
     ga_out,
     gb_out,
     gc_out,
-    g_out,
+    in_out,
+    out_out,
     w,
     h,
     e,
@@ -990,54 +1102,70 @@
         partners.append(plane.at_x(lax.rem(plane.x + o, 4)))
         partners.append(plane.at_y(lax.rem(plane.y + o, 4)))
     greet(partners)
-    gain_acc[...] = jnp.zeros_like(gain_acc)
     first.wait()
 
     def product(rows, col):
         return dnn(d_ref[rows, :], w[:, :, :, col].reshape(16 * BIN_PAD, -1))
+
+    wide = D // 8
 
     def weights():
         for copy in late:
             copy.wait()
-
-        def one(k, carry):
-            cols = pl.ds(pl.multiple_of(k * 512, 512), 512)
-            res = dtn(d_ref[...], h[:, :, cols].reshape(HALF_TOK, 512)).astype(BF)
-            grads[:, :, :BIN_PAD, cols] = res.reshape(4, 4, BIN_PAD, 512)
+        for k in range(4):
+            cols = slice(k * 512, (k + 1) * 512)
+            res = dtn(d_ref[...], h[:, :, cols].reshape(HALF_TOK, 512))
+            own = w[:, :, :, cols].reshape(16 * BIN_PAD, 512).astype(F32)
+            gain_acc[:, cols] = jnp.sum(res * own, axis=0, keepdims=True)
+            grads[:, :, :BIN_PAD, cols] = res.astype(BF).reshape(4, 4, BIN_PAD, 512)
             res = dtn(y_ref[...], e[:, :, cols].reshape(HALF_TOK, 512)).astype(BF)
             grads[:, :, BIN_PAD:, cols] = res.reshape(4, 4, 16, 512)
-            return carry
-
-        lax.fori_loop(0, 4, one, 0)
-        yield from plane_reduce_steps(
-            plane, grads, far_a, end_a, far_b, end_b, gss, grs, g_out
+        reduce = plane_reduce_steps(
+            plane,
+            grads,
+            far_a,
+            end_a,
+            far_b,
+            end_b,
+            gss,
+            grs,
+            ((0, in_out), (BIN_PAD, out_out)),
         )
+        advance(reduce)
+        gains = (gain_acc[...] / gain_ref[...], gb_ref[...], gc_ref[...])
+        for n, gain in enumerate(gains):
+            for r in range(8):
+                pack[r : r + 1, n * wide : (n + 1) * wide] = gain[:, r * wide : (r + 1) * wide]
+        sums = sum_steps(ring, plane, pack, ring_in, x_in, y_in, pss, prs)
+        advance(sums)
+        yield
+        for _ in range(4):
+            advance(reduce)
+            advance(sums)
+            yield
+        finish(sums)
+        finish(reduce)
 
     weight_grads = weights()
-    weave(
-        scatter_steps(ring, product, part, sib_in, far_in, end_in, sss, srs),
-        weight_grads,
-    )
 
     def one(at):
         grad = total_rows(part, end_in, ring.c, at)
-        d_out[at, :] = res_ref[at, :] + norm_back_rows(v_ref, gain_ref, grad, at, gain_acc)
-
-    by_rows(one)
-    wide = D // 8
-    gains = (jnp.sum(gain_acc[...], axis=0, keepdims=True), gb_ref[...], gc_ref[...])
-    for n, gain in enumerate(gains):
-        for r in range(8):
-            pack[r : r + 1, n * wide : (n + 1) * wide] = gain[:, r * wide : (r + 1) * wide]
-    total = sum_everywhere(ring, plane, pack, ring_in, x_in, y_in, pss, prs)
-    pack[...] = total
+        d_out[at, :] = res_ref[at, :] + norm_back_rows(v_ref, gain_ref, grad, at)
+
+    def ready(q):
+        by_rows(one, q * (TOK // CHUNKS), TOK // CHUNKS)
+
+    weave(
+        scatter_steps(ring, product, part, sib_in, far_in, end_in, sss, srs, ready),
+        weight_grads,
+    )
+    finish(weight_grads)
     for n, out in enumerate((ga_out, gb_out, gc_out)):
         for r in range(8):
             out[:, r * wide : (r + 1) * wide] = pack[r : r + 1, n * wide : (n + 1) * wide]
-    finish(weight_grads)
-
-
-def last_step(d, w, h, y, e, v, gain, res, grad_b, grad_c):
+
+
+def last_step(d, w, h, y, e, v, gain, res, grad_b, grad_c, width):
     small = (8, 3 * D // 8)
     return pl.pallas_call(
         last_kernel,
@@ -1046,16 +1174,17 @@
             sds((1, D), F32),
             sds((1, D), F32),
             sds((1, D), F32),
-            sds((BIN_PAD + 16, D), F32),
+            sds((width, D), F32),
+            sds((16, D), F32),
         ),
         in_specs=[VM, ANY, ANY, VM, ANY, VM, VM, VM, VM, VM],
-        out_specs=(VM,) * 5,
+        out_specs=(VM,) * 6,
         scratch_shapes=[
             pltpu.VMEM((4, 4, BIN_PAD, D), BF),
             pltpu.VMEM((8, TOK, D), BF),
             pltpu.VMEM((8, TOK, D), BF),
             pltpu.SemaphoreType.DMA((3,)),
-            pltpu.VMEM((16, D), F32),
+            pltpu.VMEM((1, D), F32),
             pltpu.VMEM(small, F32),
             pltpu.VMEM((8,) + small, F32),
             pltpu.VMEM((4,) + small, F32),
@@ -1191,7 +1320,6 @@
     )
     for j in range(2):
         for r in range(NBLK):
-            advance(cots)
             queries = qs[j, rows_of(r), :]
             rows_num = jnp.zeros((BLK, HEAD_V), F32)
             rows_den = jnp.zeros((BLK, 1), F32)
@@ -1205,6 +1333,8 @@
                 )
             num[j, rows_of(r), :] = rows_num
             den[j, rows_of(r), :] = jnp.broadcast_to(rows_den, (BLK, HEAD_V))
+    advance(cots)
+    advance(cots)
     for copy in copies:
         copy.wait_recv()
     sv_ref[...] = sv_r[...]
@@ -1262,7 +1392,14 @@
     e_ref,
     t_ref,
     pick_ref,
+    down_ref,
+    x_ref,
+    low_ref,
+    g_ref,
     raw_ref,
+    out_ref,
+    gin_ref,
+    gout_ref,
     dp_ref,
     qs,
     ks,
@@ -1275,13 +1412,47 @@
     tn_r,
     ss,
     rs,
+    part,
+    sib_in,
+    far_in,
+    end_in,
+    bss,
+    brs,
+    bls,
+    gls,
+    grads,
+    far_a,
+    end_a,
+    far_b,
+    end_b,
+    gss,
+    grs,
 ):
+    ring, plane = Ring(), Plane()
+    loading = load(g_ref, grads, gls)
     xh = lax.axis_index("xh")
     partner = {"xh": 1 - xh}
     edge = jnp.where(xh == 0, EDGE, HALF_TOK - EDGE)
     bias1, bias2, coef = t_ref[0:1, :], t_ref[1:2, :], t_ref[2:3, :]
     barrier = pltpu.get_barrier_semaphore()
-    pl.semaphore_signal(barrier, inc=1, device_id=partner, device_id_type=MESH)
+    partners = (ring.up, ring.dn, ring.sib, partner) + plane.neighbours()
+    for device in partners:
+        pl.semaphore_signal(barrier, inc=1, device_id=device, device_id_type=MESH)
+    out_ref[: TOK // 2, :] = low_ref[...]
+
+    def write(at, rows, total):
+        out_ref[rows, :] = (x_ref[rows, :] + total).astype(BF)
+
+    sums = rows_reduce_steps(
+        ring, down_ref, 1, part, sib_in, far_in, end_in, bss, brs, bls, write
+    )
+    reduce = plane_reduce_steps(
+        plane, grads, far_a, end_a, far_b, end_b, gss, grs, ((0, gin_ref), (48, gout_ref))
+    )
+    pl.semaphore_wait(barrier, len(partners))
+    advance(sums)
+    loading.wait()
+    advance(reduce)
     small = p_ref[:, 2 * HEAD_V :]
     for j in range(2):
         qs[j] = dnn(small, pick_ref[2 * j]).astype(BF)
@@ -1305,8 +1476,11 @@
         tv = jnp.zeros((HEAD_V, STATE), F32)
         tn = jnp.zeros((1, STATE), F32)
         for r in range(NBLK):
+            if r == 2:
+                advance(sums)
+                advance(reduce)
             queries = qs[j, rows_of(r), :]
-            grads = dy_ref[rows_of(r), head]
+            grads_y = dy_ref[rows_of(r), head]
             one, two = factors_of(queries)
             phi = one * two
             slot = r * BLK + lax.broadcasted_iota(jnp.int32, (BLK, 1), 0)
@@ -1315,20 +1489,20 @@
             cross_num = dnt(phi.astype(BF), sv_ref[j])
             total = jnp.where(seen, cross_den, 0.0)
             dot = jnp.where(
-                seen, jnp.sum(cross_num * grads.astype(F32), axis=-1, keepdims=True), 0.0
+                seen, jnp.sum(cross_num * grads_y.astype(F32), axis=-1, keepdims=True), 0.0
             )
             kept = []
             for s in range(r + 1):
                 scores = dnt(queries, ks[j, rows_of(s), :]) * INV_ROOT
                 mask = causal_mask(r * BLK, s * BLK, BLK, BLK, edge)
                 kernel = jnp.where(mask, 1.0 + scores + 0.5 * scores * scores, 0.0)
-                weight_grad = dnt(grads, p_ref[rows_of(s), head])
+                weight_grad = dnt(grads_y, p_ref[rows_of(s), head])
                 total = total + jnp.sum(kernel, axis=-1, keepdims=True)
                 dot = dot + jnp.sum(kernel * weight_grad, axis=-1, keepdims=True)
                 kept.append((scores, mask, kernel, weight_grad))
             inverse = 1.0 / total
             mean = dot * inverse
-            grads_n = (grads.astype(F32) * inverse).astype(BF)
+            grads_n = (grads_y.astype(F32) * inverse).astype(BF)
             query_grad = jnp.zeros((BLK, 128), F32)
             for s in range(r + 1):
                 scores, mask, kernel, weight_grad = kept[s]
@@ -1346,14 +1520,17 @@
             tn = tn + jnp.sum(shift * phi, axis=0, keepdims=True)
         tv_s[j] = (tv * coef).astype(BF)
         tn_s[j] = jnp.broadcast_to(tn * coef, (8, STATE))
-    pl.semaphore_wait(barrier, 1)
     copies = (
         remote(tv_s, tv_r, ss.at[0], rs.at[0], partner),
         remote(tn_s, tn_r, ss.at[1], rs.at[1], partner),
     )
+    advance(sums)
+    advance(reduce)
     for copy in copies:
         copy.wait_recv()
     for r in range(NBLK):
+        if r == 2:
+            advance(reduce)
         placed = jnp.zeros((BLK, 128), F32)
         for j in range(2):
             head = slice(j * HEAD_V, (j + 1) * HEAD_V)
@@ -1375,14 +1552,21 @@
         raw_ref[rows_of(r), :] = dnt(dp_ref[rows_of(r), :], sel_ref[...]).astype(BF)
     for copy in copies:
         copy.wait_send()
-
-
-def linear_backward(p1, dy, sv, sn, select, tables):
+    finish(sums)
+    finish(reduce)
+
+
+def linear_backward(p1, dy, sv, sn, select, tables, down, x, low, grads):
     return pl.pallas_call(
         linear_backward_kernel,
-        out_shape=sds((HALF_TOK, 16 * BIN_PAD)),
-        in_specs=[VM] * 8,
-        out_specs=VM,
+        out_shape=(
+            sds((HALF_TOK, 16 * BIN_PAD)),
+            sds((TOK, D)),
+            sds((48, D), F32),
+            sds((16, D), F32),
+        ),
+        in_specs=[VM] * 8 + [ANY, VM, VM, ANY],
+        out_specs=(VM,) * 4,
         scratch_shapes=[
             pltpu.VMEM((HALF_TOK, 3 * HEAD_V), BF),
             pltpu.VMEM((2, HALF_TOK, 128), BF),
@@ -1396,14 +1580,30 @@
             pltpu.VMEM((2, 8, STATE), F32),
             pltpu.SemaphoreType.DMA((2,)),
             pltpu.SemaphoreType.DMA((2,)),
-        ],
+        ]
+        + ROWS_SCRATCH
+        + [pltpu.SemaphoreType.DMA]
+        + plane_reduce_scratch(64),
         compiler_params=params(8),
-    )(p1, dy, sv, sn, select, *tables)
+    )(p1, dy, sv, sn, select, *tables, down, x, low, grads)
 
 
 WBLK = 128
 WKEYS = WBLK + WINDOW
 INV_ROOT_V = 1.0 / math.sqrt(HEAD_V)
+
+
+def turn_tables():
+    slot = np.arange(2 * HALF_TOK)
+    last = 2 * HALF_TOK - EDGE
+    position = slot - np.where(slot < EDGE, 0, np.where(slot < last, EDGE, last))
+    frequency = np.exp(-math.log(10000.0) * np.arange(HEAD_V // 2) * 2.0 / HEAD_V)
+    angles = position[:, None] * frequency[None, :]
+    cosine, sine = np.cos(angles), np.sin(angles)
+    pair = np.stack(
+        [np.concatenate([cosine, cosine], axis=1), np.concatenate([-sine, sine], axis=1)]
+    )
+    return pair.reshape(2, 2, HALF_TOK, HEAD_V).transpose(1, 0, 2, 3).astype(np.float32)
 
 
 def window_mask(r, edge, lowest):
@@ -1415,8 +1615,7 @@
 def window_forward_kernel(
     h_ref,
     w_ref,
-    cos_ref,
-    sin_ref,
+    turn_ref,
     cot_ref,
     y_ref,
     q_ref,
@@ -1424,6 +1623,7 @@
     hi_ref,
     h,
     w,
+    turn,
     sems,
     xss,
     xrs,
@@ -1440,6 +1640,7 @@
     loads = (
         load(w_ref.at[:, :, pl.ds(0, 48), :], w, sems.at[0]),
         load(h_ref, h, sems.at[1]),
+        load(turn_ref.at[xh], turn, sems.at[2]),
     )
     barrier = pltpu.get_barrier_semaphore()
     for device in (ring.up, ring.dn, ring.sib, partner):
@@ -1455,7 +1656,7 @@
 
     def turned(vecs, rows):
         return (
-            vecs * cos_ref[rows, :] + pltpu.roll(vecs, HEAD_V // 2, 1) * sin_ref[rows, :]
+            vecs * turn[0, rows, :] + pltpu.roll(vecs, HEAD_V // 2, 1) * turn[1, rows, :]
         ).astype(BF)
 
     for r in (blocks - 1,) + tuple(range(blocks - 1)):
@@ -1476,7 +1677,8 @@
                 xrs,
                 partner,
             )
-        advance(cots)
+    advance(cots)
+    advance(cots)
     for r in tuple(range(1, HALF_TOK // WBLK)) + (0,):
         if r == 0:
             copy.wait_recv()
@@ -1492,12 +1694,11 @@
             y_ref[rows, head] = dnn(
                 probs.astype(BF), kv_ref[keys, (2 + j) * 128 : (3 + j) * 128]
             ).astype(BF)
-        advance(cots)
     copy.wait_send()
     finish(cots)
 
 
-def window_forward(h, w, cosine, sine, cot):
+def window_forward(h, w, turns, cot):
     return pl.pallas_call(
         window_forward_kernel,
         out_shape=(
@@ -1506,36 +1707,70 @@
             sds((HALF_TOK + WINDOW, 512)),
             sds((8, TOK // 2, D)),
         ),
-        in_specs=[ANY, ANY, VM, VM, VM],
+        in_specs=[ANY, ANY, ANY, VM],
         out_specs=(VM, VM, VM, ANY),
         scratch_shapes=[
             pltpu.VMEM((8, TOK, D), BF),
             pltpu.VMEM((4, 4, 48, D), BF),
-            pltpu.SemaphoreType.DMA((2,)),
+            pltpu.VMEM((2, HALF_TOK, HEAD_V), F32),
+            pltpu.SemaphoreType.DMA((3,)),
             pltpu.SemaphoreType.DMA,
             pltpu.SemaphoreType.DMA,
         ]
         + HALF_SCRATCH,
         compiler_params=params(9),
-    )(h, w, cosine, sine, cot)
+    )(h, w, turns, cot)
 
 
 def window_backward_kernel(
-    q_ref, kv_ref, dy_ref, cos_ref, sin_ref, dp_ref, dkv, halo, ss, rs
+    q_ref,
+    kv_ref,
+    dy_ref,
+    turn_ref,
+    down_ref,
+    x_ref,
+    dp_ref,
+    low_ref,
+    dkv,
+    halo,
+    turn,
+    tls,
+    ss,
+    rs,
+    part,
+    sib_in,
+    far_in,
+    end_in,
+    bss,
+    brs,
+    bls,
 ):
+    ring = Ring()
     xh = lax.axis_index("xh")
     partner = {"xh": 1 - xh}
+    turning = load(turn_ref.at[xh], turn, tls)
     edge = jnp.where(xh == 0, EDGE, HALF_TOK - EDGE)
     lowest = jnp.where(xh == 0, 0, -WINDOW)
     barrier = pltpu.get_barrier_semaphore()
-    pl.semaphore_signal(barrier, inc=1, device_id=partner, device_id_type=MESH)
+    for device in (ring.up, ring.dn, ring.sib, partner):
+        pl.semaphore_signal(barrier, inc=1, device_id=device, device_id_type=MESH)
     dkv[...] = jnp.zeros_like(dkv)
     blocks = HALF_TOK // WBLK
+
+    def write(at, rows, total):
+        low_ref[at, :] = (x_ref[rows, :] + total).astype(BF)
+
+    sums = rows_reduce_steps(
+        ring, down_ref, 0, part, sib_in, far_in, end_in, bss, brs, bls, write
+    )
+    pl.semaphore_wait(barrier, 4)
+    advance(sums)
+    turning.wait()
 
     def turned_back(r, grads):
         rows = slice(r * WBLK, (r + 1) * WBLK)
         return (
-            grads * cos_ref[rows, :] + pltpu.roll(grads * sin_ref[rows, :], HEAD_V // 2, 1)
+            grads * turn[0, rows, :] + pltpu.roll(grads * turn[1, rows, :], HEAD_V // 2, 1)
         ).astype(BF)
 
     for r in range(blocks):
@@ -1560,8 +1795,9 @@
             dkv[keys, head] += dtn(score_grad, queries) * INV_ROOT_V
             dkv[keys, vals] += dtn(probs.astype(BF), grads)
         if r == 0:
-            pl.semaphore_wait(barrier, 1)
             copy = remote(dkv.at[pl.ds(0, WINDOW), :], halo, ss, rs, partner)
+        if r in (1, 5, blocks - 1):
+            advance(sums)
     for r in range(blocks):
         rows = slice(r * WBLK, (r + 1) * WBLK)
         shifted = slice(WINDOW + r * WBLK, WINDOW + (r + 1) * WBLK)
@@ -1576,22 +1812,26 @@
                 shifted, (2 + j) * 128 : (3 + j) * 128
             ].astype(BF)
     copy.wait_send()
-
-
-def window_backward(q, kv, dy, cosine, sine):
+    finish(sums)
+
+
+def window_backward(q, kv, dy, turns, down, x):
     return pl.pallas_call(
         window_backward_kernel,
-        out_shape=jax.ShapeDtypeStruct((HALF_TOK, 768), BF),
-        in_specs=[VM] * 5,
-        out_specs=VM,
+        out_shape=(sds((HALF_TOK, 768)), sds((TOK // 2, D))),
+        in_specs=[VM, VM, VM, ANY, ANY, VM],
+        out_specs=(VM, VM),
         scratch_shapes=[
             pltpu.VMEM((HALF_TOK + WINDOW, 512), F32),
             pltpu.VMEM((WINDOW, 512), F32),
+            pltpu.VMEM((2, HALF_TOK, HEAD_V), F32),
             pltpu.SemaphoreType.DMA,
             pltpu.SemaphoreType.DMA,
-        ],
+            pltpu.SemaphoreType.DMA,
+        ]
+        + ROWS_SCRATCH,
         compiler_params=params(10),
-    )(q, kv, dy, cosine, sine)
+    )(q, kv, dy, turns, down, x)
 
 
 def padded(rows, count):
@@ -1646,53 +1886,46 @@
     )
     valid = (my_position < chosen)[:, None]
     cot_low = jnp.where(valid, cotangent, jnp.zeros_like(cotangent))
-    cot_local = cot_low.astype(F32)
-    frequency = jnp.exp(
-        -math.log(10000.0) * jnp.arange(HEAD_V // 2, dtype=F32) * 2.0 / HEAD_V
-    )
-    angles = position.astype(F32)[:, None] * frequency[None, :]
-    cosine, sine = jnp.cos(angles), jnp.sin(angles)
-    cosine = jnp.concatenate([cosine, cosine], axis=1)
-    sine = jnp.concatenate([-sine, sine], axis=1)
     tables = tuple(
         jnp.asarray(table, kind) for table, kind in zip(state_tables(), (BF, F32, BF))
     )
     select = jnp.asarray(select_table(wide), BF)
 
-    shard = jnp.concatenate([padded(based_in.T, BIN_PAD), based_out], axis=0)
-    h1, lin_all, raw = first_step(block_input, gains[0], shard)
+    turns = jnp.asarray(turn_tables())
+
+    h1, lin_all, raw = first_step(block_input, gains[0], based_in.T, based_out)
     y1, p1, state_v, state_n, cot_lo = linear_forward(raw, select, tables, cot_low)
     x2, h2 = forward_step(y1, lin_all, BIN_PAD, block_input, gains[1], 2)
-    y2, queries, key_vals, cot_hi = window_forward(h2, win_all, cosine, sine, cot_low)
+    y2, queries, key_vals, cot_hi = window_forward(h2, win_all, turns, cot_low)
     x3, h3 = forward_step(y2, win_all, 48, x2, gains[2], 3)
     act, d_gu, down = mlp_step(h3, cot_lo, cot_hi, ff_all)
-    out_sum = lax.psum_scatter(down, RING, scatter_dimension=0, tiled=True)
     dx3, grad_c, e3, d_y2, ff_grads = mlp_back_step(
-        d_gu, act, ff_all, win_all, h3, cot_lo, cot_hi, x3, gains[2], cot_local
+        d_gu, act, ff_all, win_all, h3, cot_lo, cot_hi, x3, gains[2], cot_low
     )
     ff_grads = lax.psum_scatter(
         ff_grads.reshape(-1, D), PLANE, scatter_dimension=0, tiled=True
     ).astype(F32)
-    d_p2 = window_backward(queries, key_vals, d_y2, cosine, sine)
+    d_p2, out_low = window_backward(queries, key_vals, d_y2, turns, down, x3)
     dx2, grad_b, e2, d_y1, win_grads = window_back_out_step(
         d_p2, win_all, lin_all, h2, y2, e3, x2, gains[1], dx3
     )
-    d_p1 = linear_backward(p1, d_y1, state_v, state_n, select, tables)
-    input_grad, grad_a, grad_b, grad_c, lin_grads = last_step(
-        d_p1, lin_all, h1, y1, e2, block_input, gains[0], dx2, grad_b, grad_c
-    )
-    block_output = (x3 + out_sum.astype(F32)).astype(BF)
+    d_p1, block_output, grad_win_in, grad_win_out = linear_backward(
+        p1, d_y1, state_v, state_n, select, tables, down, x3, out_low, win_grads
+    )
+    input_grad, grad_a, grad_b, grad_c, grad_lin_in, grad_lin_out = last_step(
+        d_p1, lin_all, h1, y1, e2, block_input, gains[0], dx2, grad_b, grad_c, wide
+    )
     gate_grad = ff_grads[:units]
     up_grad = ff_grads[UNIT_PAD : UNIT_PAD + units]
     return (
         block_output,
         input_grad,
         grad_a.reshape(D),
-        lin_grads[:wide].T,
-        lin_grads[BIN_PAD:],
+        grad_lin_in.T,
+        grad_lin_out,
         grad_b.reshape(D),
-        win_grads[:48].T,
-        win_grads[48:],
+        grad_win_in.T,
+        grad_win_out,
         grad_c.reshape(D),
         jnp.stack([gate_grad.T, up_grad.T], axis=1),
         ff_grads[2 * UNIT_PAD : 2 * UNIT_PAD + units],

time: 497 us -> 448 us (0.901)
  Pallas kernels: 449 us -> 408 us
  other arithmetic: 13.1 us -> 6.76 us
    pallas_call x2, Pallas kernels: 35.2 us -> 69.3 us  [the longest x1 49.8 us: linear_backward(): pl.pallas_call(linear_backward_kernel, out_shape=(sds((HALF_TOK, 16 * BIN...]
    pallas_call x1, Pallas kernels: 77.3 us -> 47.6 us  [window_back_out_step(): pl.pallas_call(window_back_out_kernel, out_shape=(sds((TOK, D), F32), sds...]
    pallas_call x1, Pallas kernels: 73.6 us -> 53.1 us  [mlp_back_step(): pl.pallas_call(mlp_back_kernel, out_shape=(sds((TOK, D), F32), sds((1, D)...]
    pallas_call x1, Pallas kernels: 53.8 us -> 40.8 us  [last_step(): pl.pallas_call(last_kernel, out_shape=(sds((TOK, D), F32), sds((1, D), F3...]
    pallas_call x2, Pallas kernels: 99 us -> 91.1 us  [forward_step(): pl.pallas_call(functools.partial(forward_kernel, off), out_shape=(sds((TO...]
  transfers between devices with their start and end apart: 4 -> 3, of which waited for: 0 -> 0; matrix products, arithmetic and copies ran while one was open for 4% -> 1% of each run, Pallas kernels for 86% -> 74%
where the time goes in v3:
time: 448 us; the launch traced here: 440 us
  Pallas kernels  408 us (91%)
  between operations  14.4 us (3%)
  local copies, waits for them, and re-layouts  11.1 us (2%)
  other arithmetic  6.76 us (2%)
    pallas_call x2, Pallas kernels, forward_step(): pl.pallas_call(functools.partial(forward_kernel, off), out_shape=(sds((TO...  91.1 us
    pallas_call x1, Pallas kernels, mlp_back_step(): pl.pallas_call(mlp_back_kernel, out_shape=(sds((TOK, D), F32), sds((1, D)...  53.1 us
    pallas_call x1, Pallas kernels, linear_backward(): pl.pallas_call(linear_backward_kernel, out_shape=(sds((HALF_TOK, 16 * BIN...  49.8 us
    pallas_call x1, Pallas kernels, window_back_out_step(): pl.pallas_call(window_back_out_kernel, out_shape=(sds((TOK, D), F32), sds...  47.6 us
    pallas_call x1, Pallas kernels, last_step(): pl.pallas_call(last_kernel, out_shape=(sds((TOK, D), F32), sds((1, D), F3...  40.8 us
    pallas_call x1, Pallas kernels, first_step(): pl.pallas_call(first_kernel, out_shape=(sds((8, TOK, D)), sds((4, 4, BIN_...  39 us
    pallas_call x1, Pallas kernels, mlp_step(): pl.pallas_call(mlp_kernel, out_shape=(sds((HALF_TOK, 2 * CHUNK)), sds((HA...  27.3 us
    pallas_call x1, Pallas kernels, window_forward(): pl.pallas_call(window_forward_kernel, out_shape=(sds((HALF_TOK, 256)), sd...  20.7 us
  transfers between devices with their start and end apart: 3, of which 0 were waited for; matrix products, arithmetic and copies ran while one was open for 1% of the time, Pallas kernels for 74%

profile of v3, /device:TPU:0, one launch (start us, length us, event | category | flops | bytes accessed | tf_op | source)
XLA Modules:
  0.0 440.2 jit_solution(9198620185632362461)
XLA Ops:
  7.2 1.7 pad_maximum_fusion.1
  9.0 1.7 fusion.9
  10.8 0.2 copy_bitcast_fusion
  11.0 0.9 fusion.5
  12.0 39.0 %shard_map.248 = (bf16[8,128,2048]{2,1,0:T(8,128)(2,1)}, bf16[4,4,48,2048]{3,2,1,0:T(8,128)(2,1)}, bf16[1024,512]{1,0:T(8,128)(2,1)}) custom-call(bf16[128,2048]{1,0:T(8,128)(2,1)} %v_ref.1, f32[1,2048]{1,0:T(1,128)} %bitcast.45, bf16[20,2048]{1,0:T(8,128)(2,1)} %bitcast.42, bf16[16,2048]{1,0:T(8,128)(2,1)} %out_ref.1), custom_call_target="tpu_custom_call" | custom-call | tf_op jit(solution)/shard_map/pallas_call | solution.py:612
  51.0 0.6 fusion.10
  51.6 2.0 fusion.8
  53.6 0.9 broadcast_select_fusion.cot_ref.res_ref
  54.5 18.7 %shard_map.249 = (bf16[1024,256]{1,0:T(8,128)(2,1)}, bf16[1024,384]{1,0:T(8,128)(2,1)}, bf16[2,128,256]{2,1,0:T(8,128)(2,1)}, f32[2,8,256]{2,1,0:T(8,128)}, bf16[8,64,2048]{2,1,0:T(8,128)(2,1)}) custom-call(bf16[1024,512]{1,0:T(8,128)(2,1)} %get-tuple-element.52.raw_ref, bf16[512,384]{1,0:T(8,128)(2,1)} %constant.46.clone.sel_ref, ...), custom_call_target="tpu_custom_call" | custom-call | tf_op jit(solution)/shard_map/pallas_call | solution.py:1358
  73.3 45.6 %shard_map.250 = (f32[128,2048]{1,0:T(8,128)}, bf16[8,128,2048]{2,1,0:T(8,128)(2,1)}) custom-call(bf16[1024,256]{1,0:T(8,128)(2,1)} %get-tuple-element.54.a_ref.y_ref, bf16[4,4,48,2048]{3,2,1,0:T(8,128)(2,1)} %get-tuple-element.55.w_ref.wo_ref, bf16[128,2048]{1,0:T(8,128)(2,1)} %v_ref.1, f32[1,2048]{1,0:T(1,128)} %bitcast.43), custom_call_target="tpu_custom_call" | custom-call | tf_op jit(solution)/shard_map/pallas_call | solution.py:672
  118.9 20.7 %shard_map.251 = (bf16[1024,256]{1,0:T(8,128)(2,1)}, bf16[1024,256]{1,0:T(8,128)(2,1)}, bf16[1088,512]{1,0:T(8,128)(2,1)}, bf16[8,64,2048]{2,1,0:T(8,128)(2,1)}) custom-call(bf16[8,128,2048]{2,1,0:T(8,128)(2,1)} %get-tuple-element.56.h_ref, bf16[4,4,64,2048]{3,2,1,0:T(8,128)(2,1)} %bitcast.32, f32[2,2,1024,128]{3,2,1,0:T(8,128)} %constant.47.clone.turn_ref, ...), custom_call_target="tpu_custom_call" | custom-call | tf_op jit(solution)/shard_map/pallas_call | solution.py:1702
  139.6 45.5 %shard_map.252 = (f32[128,2048]{1,0:T(8,128)}, bf16[8,128,2048]{2,1,0:T(8,128)(2,1)}) custom-call(bf16[1024,256]{1,0:T(8,128)(2,1)} %get-tuple-element.59.a_ref.y_ref, bf16[4,4,64,2048]{3,2,1,0:T(8,128)(2,1)} %bitcast.33, f32[128,2048]{1,0:T(8,128)} %get-tuple-element.60.x_ref.v_ref, f32[1,2048]{1,0:T(1,128)} %bitcast.47), custom_call_target="tpu_custom_call" | custom-call | tf_op jit(solution)/shard_map/pallas_call | solution.py:672
  185.2 27.3 %shard_map.253 = (bf16[1024,768]{1,0:T(8,128)(2,1)}, bf16[1024,1536]{1,0:T(8,128)(2,1)}, bf16[1024,2048]{1,0:T(8,128)(2,1)}) custom-call(bf16[8,128,2048]{2,1,0:T(8,128)(2,1)} %get-tuple-element.61.h_ref, bf16[8,64,2048]{2,1,0:T(8,128)(2,1)} %get-tuple-element.62.lo_ref, bf16[8,64,2048]{2,1,0:T(8,128)(2,1)} %get-tuple-element.63.hi_ref, ...), custom_call_target="tpu_custom_call" | custom-call | tf_op jit(solution)/shard_map/pallas_call | solution.py:749
  212.5 53.1 %shard_map.254 = (f32[128,2048]{1,0:T(8,128)}, f32[1,2048]{1,0:T(1,128)}, bf16[8,128,2048]{2,1,0:T(8,128)(2,1)}, bf16[1024,256]{1,0:T(8,128)(2,1)}, bf16[16,144,2048]{2,1,0:T(8,128)(2,1)}) custom-call(bf16[1024,1536]{1,0:T(8,128)(2,1)} %get-tuple-element.64.d_ref, bf16[1024,768]{1,0:T(8,128)(2,1)} %get-tuple-element.65.act_ref, ...), custom_call_target="tpu_custom_call" | custom-call | tf_op jit(solution)/shard_map/pallas_call | solution.py:883
  265.6 19.5 %shard_map.255 = (bf16[1024,768]{1,0:T(8,128)(2,1)}, bf16[64,2048]{1,0:T(8,128)(2,1)}) custom-call(bf16[1024,256]{1,0:T(8,128)(2,1)} %get-tuple-element.57.q_ref, bf16[1088,512]{1,0:T(8,128)(2,1)} %get-tuple-element.58.kv_ref, bf16[1024,256]{1,0:T(8,128)(2,1)} %get-tuple-element.67.dy_ref, f32[2,2,1024,128]{3,2,1,0:T(8,128)} %constant.47.clone.turn_ref, ...), custom_call_target="tpu_custom_call" | custom-call | tf_op jit(solution)/shard_map/pallas_call | solution.py:1819
  285.1 47.6 %shard_map.256 = (f32[128,2048]{1,0:T(8,128)}, f32[1,2048]{1,0:T(1,128)}, bf16[8,128,2048]{2,1,0:T(8,128)(2,1)}, bf16[1024,256]{1,0:T(8,128)(2,1)}, bf16[4,4,64,2048]{3,2,1,0:T(8,128)(2,1)}) custom-call(bf16[1024,768]{1,0:T(8,128)(2,1)} %get-tuple-element.69.d_ref, bf16[4,4,64,2048]{3,2,1,0:T(8,128)(2,1)} %bitcast.35, ...), custom_call_target="tpu_custom_call" | custom-call | tf_op jit(solution)/shard_map/pallas_call | solution.py:999
  332.7 49.8 %shard_map.257 = (bf16[1024,512]{1,0:T(8,128)(2,1)}, bf16[128,2048]{1,0:T(8,128)(2,1)}, f32[48,2048]{1,0:T(8,128)}, f32[16,2048]{1,0:T(8,128)}) custom-call(bf16[1024,384]{1,0:T(8,128)(2,1)} %get-tuple-element.53.p_ref, bf16[1024,256]{1,0:T(8,128)(2,1)} %get-tuple-element.72.dy_ref, bf16[2,128,256]{2,1,0:T(8,128)(2,1)} %get-tuple-element.73.sv_ref, ...), custom_call_target="tpu_custom_call" | custom-call | tf_op jit(solution)/shard_map/pallas_call | solution.py:1560
  382.5 40.8 %shard_map.258 = (f32[128,2048]{1,0:T(8,128)}, f32[1,2048]{1,0:T(1,128)}, f32[1,2048]{1,0:T(1,128)}, f32[1,2048]{1,0:T(1,128)}, f32[20,2048]{1,0:T(8,128)}, /*index=5*/f32[16,2048]{1,0:T(8,128)}) custom-call(bf16[1024,512]{1,0:T(8,128)(2,1)} %get-tuple-element.78.d_ref, bf16[4,4,48,2048]{3,2,1,0:T(8,128)(2,1)} %get-tuple-element.55.w_ref.wo_ref, ...), custom_call_target="tpu_custom_call" | custom-call | tf_op jit(solution)/shard_map/pallas_call | solution.py:1170
  423.3 1.2 convert_element_type.15
  424.5 0.1 slice_bitcast_fusion.1
  424.6 0.1 pad_maximum_fusion
  424.7 1.4 copy.30
  426.1 0.8 slice.34
  426.9 0.8 copy.44
  427.7 1.0 copy.45
  428.7 0.6 copy.46
  429.3 0.7 copy.47
  430.0 0.7 copy.48
  430.6 0.6 copy.49
  431.2 0.7 copy.50
  432.0 0.7 copy.51
  432.6 0.6 copy.52
  (36 shorter events, 0.3 us)
Async XLA Ops:
  7.2 111.7 %all-gather.3.cloned.1.call-start = ((), (), s32[]{:S(2)}) async-start(), calls=%async_computation.1 | async-start | bytes 4456448 | tf_op jit(solution)/shard_map/all_gather | solution.py:1866
  7.2 3.8 copy-start.5
  9.0 176.2 %all-gather.5.cloned.1.call-start = ((), (), s32[]{:S(2)}) async-start(), calls=%async_computation.2 | async-start | bytes 10027008 | tf_op jit(solution)/shard_map/all_gather | solution.py:1869
  10.8 40.2 %copy-start.12 = (s32[1,3]{1,0:T(1,128)S(1)}, s32[1,3]{1,0:T(1,128)}, u32[]{:S(2)}) copy-start(s32[1,3]{1,0:T(1,128)} %param.19) | copy-start | bytes 40
  10.8 42.8 %copy-start.3 = (bf16[128,2048]{1,0:T(8,128)(2,1)S(1)}, bf16[128,2048]{1,0:T(8,128)(2,1)}, u32[]{:S(2)}) copy-start(bf16[128,2048]{1,0:T(8,128)(2,1)} %param.18) | copy-start | bytes 1572868
  11.9 411.4 %reduce-scatter.2.cloned.1.call-start = ((), (), s32[]{:S(2)}) async-start(), calls=%async_computation.3 | async-start | bytes 10027008 | tf_op jit(solution)/shard_map/reduce_scatter | solution.py:1905
  424.6 1.5 copy-start
  424.6 2.3 copy-start.2
  424.7 3.0 copy-start.1
  426.9 1.8 copy-start.11
  426.9 2.4 copy-start.6
  426.9 3.1 copy-start.8
  427.7 2.9 copy-start.10
  427.7 3.5 copy-start.4
  427.7 4.3 copy-start.7
  427.7 4.9 %copy-start.9 = (f32[1,2048]{1,0:T(1,128)S(1)}, f32[1,2048]{1,0:T(1,128)}, u32[]{:S(2)}) copy-start(f32[1,2048]{1,0:T(1,128)} %get-tuple-element.91) | copy-start | bytes 24580
Sparse Core Ops, SparseCore 0:
  10.7 59.0 all-gather.2
  72.6 76.7 all-gather.4
  265.7 90.9 reduce-scatter.1

commit v4 on v0

v4 whole, which is shorter than its diff:
```python
import functools
import math
import types

import jax
import jax.numpy as jnp
import numpy as np
from jax import lax
from jax.experimental import pallas as pl
from jax.experimental.pallas import tpu as pltpu
from jax.sharding import Mesh
from jax.sharding import PartitionSpec as P

FEAT = 16
HEAD_V = 128
WINDOW = 64
EPSILON = 1e-05
D = 2048
TOK = 128
HALF_TOK = 1024
EDGE = 64
UNIT_PAD = 48
BIN_PAD = 32
STATE = 256
PLANE = ("xh", "xl", "y")
RING = ("z", "c")
ALL = ("xl", "y", "xh", "z", "c")
MESH = pl.DeviceIdType.MESH
BF = jnp.bfloat16
F32 = jnp.float32
VM = pl.BlockSpec(memory_space=pltpu.VMEM)
ANY = pl.BlockSpec(memory_space=pl.ANY)


def dnn(a, b):
    return lax.dot_general(a, b, (((1,), (0,)), ((), ())), preferred_element_type=F32)


def dnt(a, b):
    return lax.dot_general(a, b, (((1,), (1,)), ((), ())), preferred_element_type=F32)


def dtn(a, b):
    return lax.dot_general(a, b, (((0,), (0,)), ((), ())), preferred_element_type=F32)


def remote(src, dst, send_sem, recv_sem, device):
    copy = pltpu.make_async_remote_copy(
        src_ref=src,
        dst_ref=dst,
        send_sem=send_sem,
        recv_sem=recv_sem,
        device_id=device,
        device_id_type=MESH,
    )
    copy.start()
    return copy


def greet(devices):
    barrier = pltpu.get_barrier_semaphore()
    for device in devices:
        pl.semaphore_signal(barrier, inc=1, device_id=device, device_id_type=MESH)
    pl.semaphore_wait(barrier, len(devices))


class Ring:
    def __init__(self):
        self.z = lax.axis_index("z")
        self.c = lax.axis_index("c")
        self.oc = 1 - self.c
        self.zp = lax.rem(self.z + 1, 4)
        self.zm = lax.rem(self.z + 3, 4)
        self.zz = lax.rem(self.z + 2, 4)
        self.up = {"z": self.zp}
        self.dn = {"z": self.zm}
        self.sib = {"c": self.oc}

    def greet(self):
        greet((self.up, self.dn, self.sib))


class Plane:
    def __init__(self):
        self.x = lax.axis_index("xh") * 2 + lax.axis_index("xl")
        self.y = lax.axis_index("y")

    def at_x(self, x):
        return {"xh": lax.div(x, 2), "xl": lax.rem(x, 2)}

    def at_y(self, y):
        return {"y": y}

    def ring(self, along_x):
        me = self.x if along_x else self.y
        plus, minus, far = lax.rem(me + 1, 4), lax.rem(me + 3, 4), lax.rem(me + 2, 4)
        to = self.at_x if along_x else self.at_y
        return me, plus, minus, far, to(plus), to(minus)

    def neighbours(self):
        xs, ys = self.ring(True), self.ring(False)
        return (xs[4], xs[5], ys[4], ys[5])


def finish(steps):
    for _ in steps:
        pass


def advance(steps):
    next(steps, None)


def weave(main, *others):
    for _ in main:
        for other in others:
            advance(other)


CHUNKS = 2


def gather_steps(ring, buf, out_ref, ss, rs, ls, rows, start=0, base=0, keep=True, ready=None):
    half = rows // 2
    me = ring.z * 2 + ring.c
    below, above, far = ring.zm * 2 + ring.c, ring.zp * 2 + ring.c, ring.zz * 2 + ring.c

    def send(slot, part, device, index):
        piece = buf.at[slot, pl.ds(start + part * half, half), :]
        return remote(piece, piece, ss.at[base + index], rs.at[base + index], device)

    local = []

    def save(slot):
        if keep:
            copy = pltpu.make_async_copy(buf.at[slot], out_ref.at[slot], ls.at[len(local)])
            copy.start()
            local.append(copy)

    def done(chip):
        if ready is not None:
            ready(chip)

    up, dn, sib = ring.up, ring.dn, ring.sib
    cp = {}
    cp[0] = send(me, 0, up, 0)
    cp[1] = send(me, 1, dn, 1)
    cp[2] = send(me, 1, up, 2)
    cp[3] = send(me, 0, dn, 3)
    cp[4] = send(me, 0, sib, 4)
    cp[5] = send(me, 1, sib, 5)
    save(me)
    yield
    cp[0].wait_recv()
    cp[6] = send(below, 0, up, 6)
    cp[8] = send(below, 0, sib, 8)
    cp[1].wait_recv()
    cp[7] = send(above, 1, dn, 7)
    cp[9] = send(above, 1, sib, 9)
    yield
    cp[2].wait_recv()
    cp[10] = send(below, 1, sib, 10)
    save(below)
    cp[3].wait_recv()
    cp[11] = send(above, 0, sib, 11)
    save(above)
    yield
    cp[4].wait_recv()
    cp[5].wait_recv()
    save(ring.z * 2 + ring.oc)
    done(ring.z)
    cp[8].wait_recv()
    cp[10].wait_recv()
    save(ring.zm * 2 + ring.oc)
    done(ring.zm)
    yield
    cp[6].wait_recv()
    cp[12] = send(far, 0, sib, 12)
    cp[7].wait_recv()
    cp[13] = send(far, 1, sib, 13)
    save(far)
    cp[9].wait_recv()
    cp[11].wait_recv()
    save(ring.zp * 2 + ring.oc)
    done(ring.zp)
    yield
    cp[12].wait_recv()
    cp[13].wait_recv()
    save(ring.zz * 2 + ring.oc)
    done(ring.zz)
    for index in range(14):
        cp[index].wait_send()
    for copy in local:
        copy.wait()


def scatter_steps(ring, product, part, sib_in, far_in, end_in, ss, rs, ready):
    rows = TOK // CHUNKS
    half = rows // 2
    c, oc = ring.c, ring.oc
    up, dn, sib = ring.up, ring.dn, ring.sib
    order = (ring.zz, ring.zp, ring.zm, ring.z)
    step = 512
    cp = {}

    def send(q, index, src, dst, device):
        n = q * 10 + index
        cp[q, index] = remote(src, dst, ss.at[n], rs.at[n], device)

    def multiply(index):
        row = pl.multiple_of(order[index] * (2 * TOK), 2 * TOK)

        def one(n, carry):
            col = pl.ds(pl.multiple_of(n * step, step), step)
            res = product(pl.ds(row, 2 * TOK), col).astype(BF)
            part[index, 0, :, col] = res[:TOK]
            part[index, 1, :, col] = res[TOK:]
            return carry

        lax.fori_loop(0, D // step, one, 0)
        for q in range(CHUNKS):
            at = pl.ds(q * rows, rows)
            send(q, index, part.at[index, oc, at, :], sib_in.at[index, at, :], sib)

    def add(index, first, count, other):
        def one(i, carry):
            at = pl.ds(pl.multiple_of(first + i * 16, 16), 16)
            part[index, c, at, :] = (part[index, c, at, :].astype(F32) + other(at)).astype(BF)
            return carry

        lax.fori_loop(0, count // 16, one, 0)

    def add_sib(q, index):
        cp[q, index].wait_recv()
        add(index, q * rows, rows, lambda at: sib_in[index, at, :].astype(F32))

    def piece(q, which):
        return pl.ds(q * rows + which * half, half)

    def far(q):
        add_sib(q, 0)
        send(q, 4, part.at[0, c, piece(q, 0), :], far_in.at[piece(q, 0), :], up)
        send(q, 5, part.at[0, c, piece(q, 1), :], far_in.at[piece(q, 1), :], dn)

    def near(q):
        add_sib(q, 1)
        send(q, 6, part.at[1, c, piece(q, 1), :], end_in.at[0, piece(q, 1), :], up)
        add_sib(q, 2)
        send(q, 7, part.at[2, c, piece(q, 0), :], end_in.at[1, piece(q, 0), :], dn)

    def passed(q):
        for which, device in ((0, up), (1, dn)):
            cp[q, 4 + which].wait_recv()
            at = piece(q, which)
            add(1 + which, q * rows + which * half, half, lambda at: far_in[at, :].astype(F32))
            send(q, 8 + which, part.at[1 + which, c, at, :], end_in.at[which, at, :], device)

    multiply(0)
    multiply(1)
    far(0)
    for q in range(1, CHUNKS):
        far(q)
    yield
    multiply(2)
    near(0)
    multiply(3)
    yield
    passed(0)
    for q in range(1, CHUNKS):
        near(q)
    yield
    for q in range(1, CHUNKS):
        passed(q)
    for q in range(CHUNKS):
        add_sib(q, 3)
        for index in range(6, 10):
            cp[q, index].wait_recv()
        ready(q)
        yield
    for copy in cp.values():
        copy.wait_send()


def rows_reduce_steps(ring, src_ref, q, part, sib_in, far_in, end_in, ss, rs, ls, ready):
    rows = TOK // CHUNKS
    half = rows // 2
    order = (ring.zz, ring.zp, ring.zm, ring.z)
    up, dn, sib = ring.up, ring.dn, ring.sib
    cp, loads = {}, []

    def send(index, src, dst, device):
        cp[index] = remote(src, dst, ss.at[index], rs.at[index], device)

    def source(index, core):
        start = order[index] * (2 * TOK) + core * TOK + q * rows
        return src_ref.at[pl.ds(pl.multiple_of(start, 16), rows), :]

    def add(index, first, count, other):
        def one(i, carry):
            at = pl.ds(pl.multiple_of(first + i * 16, 16), 16)
            part[index, at, :] = (part[index, at, :].astype(F32) + other(at)).astype(BF)
            return carry

        lax.fori_loop(0, count // 16, one, 0)

    def add_sib(index):
        loads[index].wait()
        cp[index].wait_recv()
        add(index, 0, rows, lambda at: sib_in[index, at, :].astype(F32))

    low, high = pl.ds(0, half), pl.ds(half, half)
    for index in range(4):
        send(index, source(index, ring.oc), sib_in.at[index], sib)
        loads.append(load(source(index, ring.c), part.at[index], ls.at[index]))
    yield
    add_sib(0)
    send(4, part.at[0, low, :], far_in.at[low, :], up)
    send(5, part.at[0, high, :], far_in.at[high, :], dn)
    add_sib(1)
    send(6, part.at[1, high, :], end_in.at[0, high, :], up)
    add_sib(2)
    send(7, part.at[2, low, :], end_in.at[1, low, :], dn)
    add_sib(3)
    yield
    for which, device in ((0, up), (1, dn)):
        cp[4 + which].wait_recv()
        at = (low, high)[which]
        add(1 + which, which * half, half, lambda at: far_in[at, :].astype(F32))
        send(8 + which, part.at[1 + which, at, :], end_in.at[which, at, :], device)
    yield
    for index in range(6, 10):
        cp[index].wait_recv()

    def total(i, carry):
        at = pl.ds(pl.multiple_of(i * 16, 16), 16)
        ready(
            at,
            pl.ds(pl.multiple_of(q * rows + i * 16, 16), 16),
            part[3, at, :].astype(F32)
            + end_in[0, at, :].astype(F32)
            + end_in[1, at, :].astype(F32),
        )
        return carry

    lax.fori_loop(0, rows // 16, total, 0)
    for copy in cp.values():
        copy.wait_send()


ROWS_SCRATCH = {
    "bpart": pltpu.VMEM((4, TOK // CHUNKS, D), BF),
    "bsib": pltpu.VMEM((4, TOK // CHUNKS, D), BF),
    "bfar": pltpu.VMEM((TOK // CHUNKS, D), BF),
    "bend": pltpu.VMEM((2, TOK // CHUNKS, D), BF),
    "bss": pltpu.SemaphoreType.DMA((10,)),
    "brs": pltpu.SemaphoreType.DMA((10,)),
    "bls": pltpu.SemaphoreType.DMA((4,)),
}
SCATTER_SCRATCH = {
    "part": pltpu.VMEM((4, 2, TOK, D), BF),
    "sib_in": pltpu.VMEM((4, TOK, D), BF),
    "far_in": pltpu.VMEM((TOK, D), BF),
    "end_in": pltpu.VMEM((2, TOK, D), BF),
    "sss": pltpu.SemaphoreType.DMA((10 * CHUNKS,)),
    "srs": pltpu.SemaphoreType.DMA((10 * CHUNKS,)),
}
GATHER_SCRATCH = {
    "buf": pltpu.VMEM((8, TOK, D), BF),
    "ss": pltpu.SemaphoreType.DMA((14 * CHUNKS,)),
    "rs": pltpu.SemaphoreType.DMA((14 * CHUNKS,)),
    "ls": pltpu.SemaphoreType.DMA((8,)),
}
HALF_SCRATCH = {
    "cbuf": pltpu.VMEM((8, TOK // 2, D), BF),
    "css": pltpu.SemaphoreType.DMA((14,)),
    "crs": pltpu.SemaphoreType.DMA((14,)),
    "cls": pltpu.SemaphoreType.DMA((8,)),
}


def plane_view(plane, ref, half, stage, place, part):
    cols = pl.ds(half * (D // 2) + (part or 0) * (D // 4), D // 2 if part is None else D // 4)
    if stage == 0:
        return ref.at[place, plane.y, :, cols] if half == 0 else ref.at[plane.x, place, :, cols]
    return ref.at[:, place, :, cols] if half == 0 else ref.at[place, :, :, cols]


def plane_gather_steps(plane, buf, ss, rs):
    copies = []
    quarter = D // 4

    def view(half, first, second, part):
        x, y = (first, second) if half == 0 else (second, first)
        cols = pl.ds(half * 2 * quarter + (part or 0) * quarter, quarter if part is not None else 2 * quarter)
        return buf.at[x, y, :, cols]

    def send(ref, device):
        copies.append(remote(ref, ref, ss.at[len(copies)], rs.at[len(copies)], device))
        return copies[-1]

    firsts = [plane.ring(half == 0) for half in (0, 1)]
    seconds = [plane.ring(half == 1) for half in (0, 1)]
    near, passed, spread = {}, {}, {}

    def go_on(half, place):
        me, plus, minus, far, to_plus, to_minus = seconds[half]
        piece = view(half, place, me, None)
        spread[half, len(spread)] = (place, send(piece, to_plus), send(piece, to_minus))

    def pass_on(entry):
        half, (place, up, dn) = entry
        me, plus, minus, far, to_plus, to_minus = seconds[half]
        up.wait_recv()
        send(view(half, place, minus, 0), to_plus)
        dn.wait_recv()
        send(view(half, place, plus, 1), to_minus)

    for half in (0, 1):
        me, plus, minus, far, to_plus, to_minus = firsts[half]
        piece = view(half, me, seconds[half][0], None)
        near[half] = (send(piece, to_plus), send(piece, to_minus))
    for half in (0, 1):
        go_on(half, firsts[half][0])
    yield
    for half in (0, 1):
        me, plus, minus, far, to_plus, to_minus = firsts[half]
        other = seconds[half][0]
        near[half][0].wait_recv()
        up = send(view(half, minus, other, 0), to_plus)
        near[half][1].wait_recv()
        passed[half] = (up, send(view(half, plus, other, 1), to_minus))
    for half in (0, 1):
        go_on(half, firsts[half][2])
        go_on(half, firsts[half][1])
    yield
    for half in (0, 1):
        passed[half][0].wait_recv()
        passed[half][1].wait_recv()
        go_on(half, firsts[half][3])
    entries = [(key[0], value) for key, value in spread.items()]
    for entry in entries[:2]:
        pass_on(entry)
    yield
    for entry in entries[2:]:
        pass_on(entry)
    yield
    for copy in copies[-2 * len(entries) :]:
        copy.wait_recv()
    for copy in copies:
        copy.wait_send()


GATHER_COPIES = 40


def plane_reduce_scratch(name, rows):
    return {
        name: pltpu.VMEM((4, 4, rows, D), BF),
        name + "_far": pltpu.VMEM((2, 2, 4, rows, D // 4), BF),
        name + "_end": pltpu.VMEM((2, 2, 4, rows, D // 2), BF),
        name + "_far2": pltpu.VMEM((2, 2, rows, D // 4), BF),
        name + "_end2": pltpu.VMEM((2, 2, rows, D // 2), BF),
        name + "_ss": pltpu.SemaphoreType.DMA((24,)),
        name + "_rs": pltpu.SemaphoreType.DMA((24,)),
    }


def plane_reduce(plane, r, name, outs):
    refs = [getattr(r, name + end) for end in ("", "_far", "_end", "_far2", "_end2", "_ss", "_rs")]
    return plane_reduce_steps(plane, *refs, outs)


def plane_reduce_steps(plane, grads, far_a, end_a, far_b, end_b, ss, rs, outs):
    copies = []
    rows = grads.shape[2]

    def send(src, dst, device):
        copies.append(remote(src, dst, ss.at[len(copies)], rs.at[len(copies)], device))
        return copies[-1]

    def add(view, *others):
        def one(i, carry):
            at = pl.ds(pl.multiple_of(i * 16, 16), 16)
            piece = view.at[..., at, :]
            total = piece[...].astype(F32)
            for other in others:
                total = total + other.at[..., at, :][...].astype(F32)
            piece[...] = total.astype(BF)
            return carry

        lax.fori_loop(0, rows // 16, one, 0)

    for stage in (0, 1):
        rings = [plane.ring(half != stage) for half in (0, 1)]
        far_in, end_in = (far_a, end_a) if stage == 0 else (far_b, end_b)

        def view(half, place, part):
            return plane_view(plane, grads, half, 1 - stage, place, part)

        def ends(half, side, part):
            if part is None:
                return end_in.at[half, side]
            return end_in.at[half, side, ..., pl.ds(part * (D // 4), D // 4)]

        first, last = [], []
        for half in (0, 1):
            me, plus, minus, far, to_plus, to_minus = rings[half]
            first.append(
                (
                    send(view(half, far, 0), far_in.at[half, 0], to_plus),
                    send(view(half, far, 1), far_in.at[half, 1], to_minus),
                )
            )
            last.append(send(view(half, plus, 1), ends(half, 0, 1), to_plus))
            last.append(send(view(half, minus, 0), ends(half, 1, 0), to_minus))
        yield
        for half in (0, 1):
            me, plus, minus, far, to_plus, to_minus = rings[half]
            first[half][0].wait_recv()
            add(view(half, plus, 0), far_in.at[half, 0])
            last.append(send(view(half, plus, 0), ends(half, 0, 0), to_plus))
            first[half][1].wait_recv()
            add(view(half, minus, 1), far_in.at[half, 1])
            last.append(send(view(half, minus, 1), ends(half, 1, 1), to_minus))
        yield
        for copy in last:
            copy.wait_recv()
        for half in (0, 1):
            me = rings[half][0]
            if stage == 0:
                add(view(half, me, None), ends(half, 0, None), ends(half, 1, None))
            else:
                cols = pl.ds(half * (D // 2), D // 2)
                total = (
                    view(half, me, None)[...].astype(F32)
                    + end_in[half, 0].astype(F32)
                    + end_in[half, 1].astype(F32)
                )
                for start, out_ref in outs:
                    out_ref[:, cols] = total[start : start + out_ref.shape[0]]
        yield
    for copy in copies:
        copy.wait_send()


def load(src, dst, sem):
    copy = pltpu.make_async_copy(src, dst, sem)
    copy.start()
    return copy


def params(collective_id, limit=58):
    return pltpu.CompilerParams(
        collective_id=collective_id, has_side_effects=True, vmem_limit_bytes=limit << 20
    )


def sds(shape, dtype=BF):
    return jax.ShapeDtypeStruct(shape, dtype)


def scale_of(rows):
    return lax.rsqrt(jnp.mean(rows * rows, axis=-1, keepdims=True) + EPSILON)


def by_rows(one, start=0, rows=TOK):
    def step(i, carry):
        one(pl.ds(pl.multiple_of(start + i * 16, 16), 16))
        return carry

    lax.fori_loop(0, rows // 16, step, 0)


def total_rows(part, end_in, c, at):
    return (
        part[3, c, at, :].astype(F32)
        + end_in[0, at, :].astype(F32)
        + end_in[1, at, :].astype(F32)
    )


def chip_rows(chip):
    return pl.ds(pl.multiple_of(chip * (2 * TOK), 2 * TOK), 2 * TOK)


def build(body, inputs, outputs, scratch, collective_id):
    names = list(inputs) + list(outputs) + list(scratch)

    def kernel(*refs):
        body(types.SimpleNamespace(**dict(zip(names, refs))))

    results = pl.pallas_call(
        kernel,
        out_shape=tuple(shape for shape, _ in outputs.values()),
        in_specs=[spec for _, spec in inputs.values()],
        out_specs=tuple(spec for _, spec in outputs.values()),
        scratch_shapes=list(scratch.values()),
        compiler_params=params(collective_id),
    )(*[array for array, _ in inputs.values()])
    return types.SimpleNamespace(**dict(zip(outputs, results)))


def vm(array):
    return (array, VM)


def hbm(array):
    return (array, ANY)


def signal(partners):
    barrier = pltpu.get_barrier_semaphore()
    for device in partners:
        pl.semaphore_signal(barrier, inc=1, device_id=device, device_id_type=MESH)


def arrive(partners):
    pl.semaphore_wait(pltpu.get_barrier_semaphore(), len(partners))


def scatter(ring, r, product, ready):
    return scatter_steps(
        ring, product, r.part, r.sib_in, r.far_in, r.end_in, r.sss, r.srs, ready
    )


def scatter_gather(ring, r, product, one, out_ref, done=None, others=()):
    rows = TOK // CHUNKS
    gathers = []

    def ready(q):
        by_rows(one, q * rows, rows)
        last = q == CHUNKS - 1
        steps = gather_steps(
            ring,
            r.buf,
            out_ref,
            r.ss,
            r.rs,
            r.ls,
            rows,
            start=q * rows,
            base=14 * q,
            keep=last,
            ready=done if last else None,
        )
        advance(steps)
        gathers.append(steps)

    weave(scatter(ring, r, product, ready), *others)
    for _ in range(5):
        for steps in gathers:
            advance(steps)
        for other in others:
            advance(other)
    for steps in gathers:
        finish(steps)


def sums_of(r, ring, at):
    return total_rows(r.part, r.end_in, ring.c, at)


def half_gather(ring, r, out_ref):
    return gather_steps(ring, r.cbuf, out_ref, r.css, r.crs, r.cls, TOK // 2)


def rows_reduce(ring, r, q, ready):
    return rows_reduce_steps(
        ring, r.down, q, r.bpart, r.bsib, r.bfar, r.bend, r.bss, r.brs, r.bls, ready
    )


def norm_into(r, ring, x_ref, gain_ref, at, rows):
    r.buf[ring.z * 2 + ring.c, at, :] = (rows * scale_of(rows) * gain_ref[...]).astype(BF)


def first_body(r):
    ring, plane = Ring(), Plane()
    partners = (ring.up, ring.dn, ring.sib) + plane.neighbours()
    signal(partners)
    r.wide[plane.x, plane.y, BIN_PAD // 2 : BIN_PAD, :] = jnp.zeros((BIN_PAD // 2, D), BF)
    r.wide[plane.x, plane.y, : r.rows_in.shape[0], :] = r.rows_in[...]
    r.wide[plane.x, plane.y, BIN_PAD:, :] = r.rows_out[...]

    def one(at):
        rows = r.x[at, :].astype(F32)
        norm_into(r, ring, r.x, r.gain, at, rows)

    by_rows(one)
    arrive(partners)
    weights = plane_gather_steps(plane, r.wide, r.wss, r.wrs)
    rows = gather_steps(ring, r.buf, r.h, r.ss, r.rs, r.ls, TOK)
    advance(weights)
    advance(rows)
    advance(weights)
    advance(weights)
    advance(rows)
    advance(rows)
    advance(weights)
    finish(rows)
    finish(weights)
    keep = load(r.wide, r.w, r.wls)

    def project(i, carry):
        at = pl.ds(pl.multiple_of(i * 256, 256), 256)
        h = r.buf[pl.ds(2 * i, 2)].reshape(256, D)
        w = r.wide[:, :, :BIN_PAD, :].reshape(16 * BIN_PAD, D)
        r.raw[at, :] = dnt(h, w).astype(BF)
        return carry

    lax.fori_loop(0, 4, project, 0)
    keep.wait()


def first_step(x, gain, rows_in, rows_out):
    return build(
        first_body,
        {"x": vm(x), "gain": vm(gain), "rows_in": vm(rows_in), "rows_out": vm(rows_out)},
        {
            "h": (sds((8, TOK, D)), ANY),
            "w": (sds((4, 4, BIN_PAD + 16, D)), ANY),
            "raw": (sds((HALF_TOK, 16 * BIN_PAD)), VM),
        },
        {
            "wide": pltpu.VMEM((4, 4, BIN_PAD + 16, D), BF),
            "wss": pltpu.SemaphoreType.DMA((GATHER_COPIES,)),
            "wrs": pltpu.SemaphoreType.DMA((GATHER_COPIES,)),
            "wls": pltpu.SemaphoreType.DMA,
        }
        | GATHER_SCRATCH,
        1,
    )


def ring_forward(r, ring, y_ref, w_ref, others=()):
    def product(rows, col):
        return dnn(y_ref[rows, :], w_ref[:, :, :, col].reshape(256, -1))

    def one(at):
        rows = r.x[at, :].astype(F32) + sums_of(r, ring, at)
        r.x_out[at, :] = rows
        norm_into(r, ring, r.x, r.gain, at, rows)

    scatter_gather(ring, r, product, one, r.h_out, others=others)


def norm_back_rows(v_ref, gain_ref, grads, at):
    rows = v_ref[at, :].astype(F32)
    scale = scale_of(rows)
    unit = rows * scale
    scaled = grads * gain_ref[...]
    return scale * (scaled - unit * jnp.mean(scaled * unit, axis=-1, keepdims=True))


def ring_backward(r, ring, product, wo_ref, others):
    def one(at):
        grad = sums_of(r, ring, at)
        rows = r.res[at, :].astype(F32) + norm_back_rows(r.v, r.gain, grad, at)
        r.d_out[at, :] = rows
        r.buf[ring.z * 2 + ring.c, at, :] = rows.astype(BF)

    def done(chip):
        r.dy_out[chip_rows(chip), :] = dnt(
            r.buf[pl.ds(2 * chip, 2)].reshape(2 * TOK, D), wo_ref[...].reshape(256, D)
        ).astype(BF)

    scatter_gather(ring, r, product, one, r.e_out, done, others)


CHUNK = 8 * UNIT_PAD


def mlp_forward(r, copies):
    copies["h"].wait()
    copies["lo"].wait()
    copies["hi"].wait()
    for i in range(2):
        for name in ("gate", "up", "down"):
            copies[name, i].wait()
        units = slice(8 * i, 8 * i + 8)

        def one(n, carry):
            at = chip_rows(n)
            tokens = pl.ds(2 * n, 2)
            rows = r.hv[tokens].reshape(2 * TOK, D)
            gate = dnt(rows, r.wv[0, units].reshape(CHUNK, D))
            up = dnt(rows, r.wv[1, units].reshape(CHUNK, D))
            d_act = dnt(r.cotv[tokens].reshape(2 * TOK, D), r.downv[units].reshape(CHUNK, D))
            sig = 1.0 / (1.0 + jnp.exp(-gate))
            silu = gate * sig
            r.act[at, i * CHUNK : (i + 1) * CHUNK] = (silu * up).astype(BF)
            r.d_gu[at, i * CHUNK : (i + 1) * CHUNK] = (
                d_act * up * (sig * (1.0 + gate * (1.0 - sig)))
            ).astype(BF)
            r.d_gu[at, (2 + i) * CHUNK : (3 + i) * CHUNK] = (d_act * silu).astype(BF)
            return carry

        lax.fori_loop(0, 4, one, 0)


def mlp_down_steps(r):
    for n in range(4):
        at = slice(2 * TOK * n, 2 * TOK * (n + 1))
        for col in range(0, D, 512):
            r.outv[at, col : col + 512] = dnn(
                r.act[at, :], r.downv[:, :, col : col + 512].reshape(2 * CHUNK, 512)
            ).astype(BF)
        if n == 1:
            yield
    copy = load(r.outv, r.down, r.msem.at[9])
    yield
    copy.wait()


def mlp_grad_steps(r, jobs):
    copies = []
    for n, (lhs, col, rhs, off, half, w) in enumerate(jobs):
        slot = n % 2
        if n >= 2:
            copies[n - 2].wait()

        def one(k, carry):
            cols = pl.ds(pl.multiple_of(k * 512, 512), 512)
            res = dtn(lhs[:, col : col + CHUNK], rhs[:, :, cols].reshape(HALF_TOK, 512))
            r.stage[slot, :, :, cols] = res.astype(BF).reshape(8, UNIT_PAD, 512)
            if w is not None:
                own = w[8 * half : 8 * half + 8, :, cols].reshape(CHUNK, 512).astype(F32)
                r.gacc[:, cols] += jnp.sum(res * own, axis=0, keepdims=True)
            return carry

        lax.fori_loop(0, 4, one, 0)
        copies.append(
            load(
                r.stage.at[slot],
                r.grads.at[pl.ds(8 * half, 8), pl.ds(off, UNIT_PAD), :],
                r.gsem.at[n],
            )
        )
        yield
    copies[-2].wait()
    copies[-1].wait()


def mlp_body(r):
    ring = Ring()
    partners = (ring.up, ring.dn, ring.sib)
    copies = {"h": load(r.h, r.hv, r.msem.at[0])}
    for n, (name, ref) in enumerate((("gate", r.wv.at[0]), ("up", r.wv.at[1]), ("down", r.downv))):
        for i in range(2):
            copies[name, i] = load(
                r.w.at[pl.ds(8 * i, 8), pl.ds(n * UNIT_PAD, UNIT_PAD), :],
                ref.at[pl.ds(8 * i, 8)],
                r.msem.at[3 + 2 * n + i],
            )
        if n == 0:
            copies["lo"] = load(r.lo, r.cotv.at[:, pl.ds(0, TOK // 2), :], r.msem.at[1])
            copies["hi"] = load(r.hi, r.cotv.at[:, pl.ds(TOK // 2, TOK // 2), :], r.msem.at[2])
    late = load(r.wo.at[:, :, pl.ds(48, 16), :], r.wov, r.msem.at[10])
    signal(partners)
    r.gacc[...] = jnp.zeros_like(r.gacc)
    mlp_forward(r, copies)
    late.wait()
    arrive(partners)

    def product(rows, col):
        return dnn(r.d_gu[rows, :], r.wv[:, :, :, col].reshape(4 * CHUNK, -1))

    def weights():
        yield from mlp_down_steps(r)
        jobs = [
            (r.d_gu, n * CHUNK, r.hv, (n // 2) * UNIT_PAD, n % 2, r.wv.at[n // 2])
            for n in range(4)
        ]
        jobs += [(r.act, n * CHUNK, r.cotv, 2 * UNIT_PAD, n, None) for n in range(2)]
        yield from mlp_grad_steps(r, jobs)

    weight_grads = weights()
    ring_backward(r, ring, product, r.wov, (weight_grads,))
    finish(weight_grads)
    r.gain_out[...] = r.gacc[...] / r.gain[...]


def mlp_step(h, lo, hi, w, wo, v, gain, cot):
    return build(
        mlp_body,
        {
            "h": hbm(h),
            "lo": hbm(lo),
            "hi": hbm(hi),
            "w": hbm(w),
            "wo": hbm(wo),
            "v": vm(v),
            "gain": vm(gain),
            "res": vm(cot),
        },
        {
            "down": (sds((HALF_TOK, D)), ANY),
            "d_out": (sds((TOK, D), F32), VM),
            "gain_out": (sds((1, D), F32), VM),
            "e_out": (sds((8, TOK, D)), ANY),
            "dy_out": (sds((HALF_TOK, 256)), VM),
            "grads": (sds((16, 3 * UNIT_PAD, D)), ANY),
        },
        {
            "hv": pltpu.VMEM((8, TOK, D), BF),
            "cotv": pltpu.VMEM((8, TOK, D), BF),
            "wv": pltpu.VMEM((2, 16, UNIT_PAD, D), BF),
            "downv": pltpu.VMEM((16, UNIT_PAD, D), BF),
            "wov": pltpu.VMEM((4, 4, 16, D), BF),
            "act": pltpu.VMEM((HALF_TOK, 2 * CHUNK), BF),
            "d_gu": pltpu.VMEM((HALF_TOK, 4 * CHUNK), BF),
            "outv": pltpu.VMEM((HALF_TOK, D), BF),
            "stage": pltpu.VMEM((2, 8, UNIT_PAD, D), BF),
            "gacc": pltpu.VMEM((1, D), F32),
            "msem": pltpu.SemaphoreType.DMA((11,)),
            "gsem": pltpu.SemaphoreType.DMA((6,)),
        }
        | SCATTER_SCRATCH
        | GATHER_SCRATCH,
        4,
    )


def state_tables():
    first = np.zeros((128, STATE), np.float32)
    second = np.zeros((128, STATE), np.float32)
    bias = np.zeros((8, STATE), np.float32)
    coef = np.zeros((8, STATE), np.float32)
    bias[0, 0] = bias[1, 0] = 1.0
    coef[0, 0] = 1.0
    at = 1
    for i in range(FEAT):
        first[i, at] = 1.0
        bias[1, at] = 1.0
        coef[0, at] = 1.0 / math.sqrt(FEAT)
        at += 1
    for i in range(FEAT):
        for j in range(i, FEAT):
            first[i, at] = 1.0
            second[j, at] = 1.0
            coef[0, at] = (0.5 if i == j else 1.0) / FEAT
            at += 1
    picks = np.zeros((4, 128, 128), np.float32)
    for which in range(4):
        for i in range(FEAT):
            picks[which, which * FEAT + i, i] = 1.0
    return (
        np.stack([first, second]),
        np.concatenate([bias[:2], coef[:1], np.zeros((5, STATE), np.float32)]),
        picks,
    )


def select_table(width):
    table = np.zeros((16 * BIN_PAD, 3 * HEAD_V), np.float32)
    for shard in range(16):
        for i in range(width):
            head, col = shard // 8, (shard % 8) * width + i
            to = 2 * HEAD_V + 2 * FEAT * head + col if col < 2 * FEAT else head * HEAD_V + col - 2 * FEAT
            table[shard * BIN_PAD + i, to] = 1.0
    return table


BLK = 256
NBLK = HALF_TOK // BLK
INV_ROOT = 1.0 / math.sqrt(FEAT)


def rows_of(b):
    return slice(b * BLK, (b + 1) * BLK)


def head_of(j):
    return slice(j * HEAD_V, (j + 1) * HEAD_V)


def causal_mask(start, edge):
    t = start + lax.broadcasted_iota(jnp.int32, (BLK, BLK), 0)
    u = start + lax.broadcasted_iota(jnp.int32, (BLK, BLK), 1)
    return (u <= t) & ((t >= edge) == (u >= edge))


class Linear:
    def __init__(self, r):
        self.r = r
        self.xh = lax.axis_index("xh")
        self.partner = {"xh": 1 - self.xh}
        self.edge = jnp.where(self.xh == 0, EDGE, HALF_TOK - EDGE)
        self.second = jnp.where(self.xh == 1, 1.0, 0.0)
        self.coef = r.t[2:3, :]

    def vectors(self):
        r = self.r
        small = r.p[:, 2 * HEAD_V :]
        for j in range(2):
            r.qs[j] = dnn(small, r.pick[2 * j]).astype(BF)
            r.ks[j] = dnn(small, r.pick[2 * j + 1]).astype(BF)

    def factors(self, vecs):
        r = self.r
        return dnn(vecs, r.e[0]) + r.t[0:1, :], dnn(vecs, r.e[1]) + r.t[1:2, :]

    def factors_back(self, grad, one, two):
        r = self.r
        return dnt((grad * two).astype(BF), r.e[0]) + dnt((grad * one).astype(BF), r.e[1])

    def key_open(self, width):
        slot = lax.broadcasted_iota(jnp.int32, (BLK, width), 0)
        return (slot >= EDGE) | (self.xh == 1)

    def sees_state(self, b, width):
        slot = b * BLK + lax.broadcasted_iota(jnp.int32, (BLK, width), 0)
        return (slot < HALF_TOK - EDGE) | (self.xh == 0)

    def scores(self, j, b):
        r = self.r
        scores = dnt(r.qs[j, rows_of(b), :], r.ks[j, rows_of(b), :]) * INV_ROOT
        mask = causal_mask(b * BLK, self.edge)
        return scores, mask, jnp.where(mask, 1.0 + scores + 0.5 * scores * scores, 0.0)


def linear_forward_part(r, ring, cots):
    lin = Linear(r)
    for b in range(NBLK):
        r.p[rows_of(b), :] = dnn(r.raw[rows_of(b), :], r.sel[...]).astype(BF)
    lin.vectors()
    for j in range(2):
        sv = jnp.zeros((HEAD_V, STATE), F32)
        sn = jnp.zeros((1, STATE), F32)
        for b in range(NBLK):
            r.pre_v[j, b] = sv
            r.pre_n[j, b] = jnp.broadcast_to(sn, (8, STATE))
            one, two = lin.factors(r.ks[j, rows_of(b), :])
            phi = one * two
            if b == 0:
                phi = jnp.where(lin.key_open(STATE), phi, 0.0)
            sv = sv + dtn(r.p[rows_of(b), head_of(j)], phi.astype(BF)) * lin.coef
            sn = sn + jnp.sum(phi, axis=0, keepdims=True) * lin.coef
        r.sv_s[j] = sv.astype(BF)
        r.sn_s[j] = jnp.broadcast_to(sn, (8, STATE))
    copies = (
        remote(r.sv_s, r.sv_r, r.xss.at[0], r.xrs.at[0], lin.partner),
        remote(r.sn_s, r.sn_r, r.xss.at[1], r.xrs.at[1], lin.partner),
    )
    for j in range(2):
        for b in range(NBLK):
            _, _, kernel = lin.scores(j, b)
            r.num[j, rows_of(b), :] = dnn(kernel.astype(BF), r.p[rows_of(b), head_of(j)])
            r.den[j, rows_of(b), :] = jnp.broadcast_to(
                jnp.sum(kernel, axis=-1, keepdims=True), (BLK, HEAD_V)
            )
    advance(cots)
    for copy in copies:
        copy.wait_recv()
    for j in range(2):
        if j == 1:
            advance(cots)
        got_v = r.sv_r[j].astype(F32) * lin.second
        got_n = r.sn_r[j] * lin.second
        for b in range(NBLK):
            state_v = (r.pre_v[j, b] + got_v).astype(BF)
            state_n = r.pre_n[j, b] + got_n
            r.sv[j, b] = state_v
            r.sn[j, b] = state_n
            one, two = lin.factors(r.qs[j, rows_of(b), :])
            phi = one * two
            den = jnp.sum(phi * state_n[0:1, :], axis=-1, keepdims=True)
            num = dnt(phi.astype(BF), state_v)
            seen = lin.sees_state(b, HEAD_V)
            top = r.num[j, rows_of(b), :] + jnp.where(seen, num, 0.0)
            bottom = r.den[j, rows_of(b), :] + jnp.where(seen, den, 0.0)
            r.y[rows_of(b), head_of(j)] = (top / bottom).astype(BF)
    for copy in copies:
        copy.wait_send()


STATE_SCRATCH = {
    "qs": pltpu.VMEM((2, HALF_TOK, 128), BF),
    "ks": pltpu.VMEM((2, HALF_TOK, 128), BF),
    "sv_s": pltpu.VMEM((2, HEAD_V, STATE), BF),
    "sn_s": pltpu.VMEM((2, 8, STATE), F32),
    "sv_r": pltpu.VMEM((2, HEAD_V, STATE), BF),
    "sn_r": pltpu.VMEM((2, 8, STATE), F32),
    "pre_v": pltpu.VMEM((2, NBLK, HEAD_V, STATE), F32),
    "pre_n": pltpu.VMEM((2, NBLK, 8, STATE), F32),
    "xss": pltpu.SemaphoreType.DMA((2,)),
    "xrs": pltpu.SemaphoreType.DMA((2,)),
}


def linear_body(r):
    ring = Ring()
    partners = (ring.up, ring.dn, ring.sib, {"xh": 1 - lax.axis_index("xh")})
    signal(partners)
    loading = load(r.w.at[:, :, pl.ds(BIN_PAD, 16), :], r.wv, r.wls)
    r.cbuf[ring.z * 2 + ring.c] = r.cot[: TOK // 2, :]
    arrive(partners)
    cots = half_gather(ring, r, r.lo)
    advance(cots)
    linear_forward_part(r, ring, cots)
    loading.wait()
    ring_forward(r, ring, r.y, r.wv, (cots,))
    finish(cots)


def linear_step(raw, select, tables, cot, w, x, gain):
    return build(
        linear_body,
        {
            "raw": vm(raw),
            "sel": vm(select),
            "e": vm(tables[0]),
            "t": vm(tables[1]),
            "pick": vm(tables[2]),
            "cot": vm(cot),
            "w": hbm(w),
            "x": vm(x),
            "gain": vm(gain),
        },
        {
            "y": (sds((HALF_TOK, 2 * HEAD_V)), VM),
            "p": (sds((HALF_TOK, 3 * HEAD_V)), VM),
            "sv": (sds((2, NBLK, HEAD_V, STATE)), VM),
            "sn": (sds((2, NBLK, 8, STATE), F32), VM),
            "lo": (sds((8, TOK // 2, D)), ANY),
            "x_out": (sds((TOK, D), F32), VM),
            "h_out": (sds((8, TOK, D)), ANY),
        },
        {
            "num": pltpu.VMEM((2, HALF_TOK, HEAD_V), F32),
            "den": pltpu.VMEM((2, HALF_TOK, HEAD_V), F32),
            "wv": pltpu.VMEM((4, 4, 16, D), BF),
            "wls": pltpu.SemaphoreType.DMA,
        }
        | STATE_SCRATCH
        | HALF_SCRATCH
        | SCATTER_SCRATCH
        | GATHER_SCRATCH,
        2,
    )


def linear_backward_part(r, others):
    lin = Linear(r)
    lin.vectors()
    for j in range(2):
        tv = jnp.zeros((HEAD_V, STATE), F32)
        tn = jnp.zeros((1, STATE), F32)
        for b in range(NBLK):
            queries = r.qs[j, rows_of(b), :]
            grads = r.dy[rows_of(b), head_of(j)]
            one, two = lin.factors(queries)
            phi = one * two
            phi_low = phi.astype(BF)
            seen = lin.sees_state(b, 1)
            state_v, state_n = r.sv[j, b], r.sn[j, b, 0:1, :]
            scores, mask, kernel = lin.scores(j, b)
            weight_grad = dnt(grads, r.p[rows_of(b), head_of(j)])
            den = jnp.sum(phi * state_n, axis=-1, keepdims=True)
            num = dnt(phi_low, state_v)
            dot = jnp.sum(num * grads.astype(F32), axis=-1, keepdims=True)
            total = jnp.where(seen, den, 0.0) + jnp.sum(kernel, axis=-1, keepdims=True)
            dot = jnp.where(seen, dot, 0.0) + jnp.sum(kernel * weight_grad, axis=-1, keepdims=True)
            inverse = 1.0 / total
            mean = dot * inverse
            grads_n = (grads.astype(F32) * inverse).astype(BF)
            score_grad = jnp.where(
                mask, (weight_grad - mean) * inverse * (1.0 + scores), 0.0
            ).astype(BF)
            r.dk[j, rows_of(b), :] = dtn(score_grad, queries)
            r.dv[j, rows_of(b), :] = dtn(kernel.astype(BF), grads_n)
            shift = jnp.where(seen, -(mean * inverse), 0.0)
            grads_s = jnp.where(seen, grads_n, jnp.zeros_like(grads_n))
            phi_grad = dnn(grads_s, state_v) + shift * state_n
            r.dq[j, rows_of(b), :] = dnn(
                score_grad, r.ks[j, rows_of(b), :]
            ) * INV_ROOT + lin.factors_back(phi_grad, one, two)
            own_v = dtn(grads_s, phi_low) * lin.coef
            own_n = jnp.sum(shift * phi, axis=0, keepdims=True) * lin.coef
            r.pre_v[j, b] = own_v
            r.pre_n[j, b] = jnp.broadcast_to(own_n, (8, STATE))
            tv, tn = tv + own_v, tn + own_n
            if (j, b) in ((0, 2), (1, 1)):
                for other in others:
                    advance(other)
        r.sv_s[j] = tv.astype(BF)
        r.sn_s[j] = jnp.broadcast_to(tn, (8, STATE))
    copies = (
        remote(r.sv_s, r.sv_r, r.xss.at[0], r.xrs.at[0], lin.partner),
        remote(r.sn_s, r.sn_r, r.xss.at[1], r.xrs.at[1], lin.partner),
    )
    for other in others:
        advance(other)
    for copy in copies:
        copy.wait_recv()
    after_v = [r.sv_r[j].astype(F32) * (1.0 - lin.second) for j in range(2)]
    after_n = [r.sn_r[j, 0:1, :] * (1.0 - lin.second) for j in range(2)]
    for b in reversed(range(NBLK)):
        placed = jnp.zeros((BLK, 128), F32)
        for j in range(2):
            one, two = lin.factors(r.ks[j, rows_of(b), :])
            phi = one * two
            state = after_v[j].astype(BF)
            phi_grad = dnn(r.p[rows_of(b), head_of(j)], state) + after_n[j]
            if b == 0:
                visible = lin.key_open(STATE)
                phi = jnp.where(visible, phi, 0.0)
                phi_grad = jnp.where(visible, phi_grad, 0.0)
            key_grad = r.dk[j, rows_of(b), :] * INV_ROOT + lin.factors_back(phi_grad, one, two)
            value_grad = r.dv[j, rows_of(b), :] + dnt(phi.astype(BF), state)
            r.dp[rows_of(b), head_of(j)] = value_grad.astype(BF)
            placed = placed + dnt(r.dq[j, rows_of(b), :].astype(BF), r.pick[2 * j])
            placed = placed + dnt(key_grad.astype(BF), r.pick[2 * j + 1])
            after_v[j] = after_v[j] + r.pre_v[j, b]
            after_n[j] = after_n[j] + r.pre_n[j, b, 0:1, :]
        r.dp[rows_of(b), 2 * HEAD_V :] = placed.astype(BF)
        r.draw[rows_of(b), :] = dnt(r.dp[rows_of(b), :], r.sel[...]).astype(BF)
    for copy in copies:
        copy.wait_send()


def sum_steps(ring, plane, r):
    copies = []
    stages = (
        (r.ring_in, ring.z * 2 + ring.c, 8, lambda t: {"z": lax.div(t, 2), "c": lax.rem(t, 2)}),
        (r.x_in, plane.x, 4, plane.at_x),
        (r.y_in, plane.y, 4, plane.at_y),
    )
    for dst, own, count, device_of in stages:
        dst[own] = r.pack[...]
        sent = []
        for o in range(1, count):
            n = len(copies) + len(sent)
            device = device_of(lax.rem(own + o, count))
            sent.append(remote(r.pack, dst.at[own], r.pss.at[n], r.prs.at[n], device))
        yield
        for copy in sent:
            copy.wait_recv()
        for copy in sent:
            copy.wait_send()
        copies += sent
        total = dst[0]
        for k in range(1, count):
            total = total + dst[k]
        r.pack[...] = total


def last_body(r):
    ring, plane = Ring(), Plane()
    me = ring.z * 2 + ring.c
    partners = []
    for o in range(1, 8):
        to = lax.rem(me + o, 8)
        partners.append({"z": lax.div(to, 2), "c": lax.rem(to, 2)})
    for o in range(1, 4):
        partners.append(plane.at_x(lax.rem(plane.x + o, 4)))
        partners.append(plane.at_y(lax.rem(plane.y + o, 4)))
    signal(partners)
    loads = [
        load(r.g, r.win, r.lsem.at[0]),
        load(r.w.at[:, :, pl.ds(0, BIN_PAD), :], r.wv, r.lsem.at[1]),
        load(r.h, r.hv, r.lsem.at[2]),
        load(r.e2, r.ev, r.lsem.at[3]),
    ]
    r.out[: TOK // 2, :] = r.low[...]

    def write(at, rows, total):
        r.out[rows, :] = (r.x3[rows, :] + total).astype(BF)

    sums = rows_reduce(ring, r, 1, write)
    win = plane_reduce(plane, r, "win", ((0, r.win_in), (48, r.win_out)))
    arrive(partners)
    advance(sums)
    loads[0].wait()
    advance(win)
    linear_backward_part(r, (sums, win))
    finish(sums)
    for copy in loads[1:]:
        copy.wait()
    wide = D // 8

    def product(rows, col):
        return dnn(r.draw[rows, :], r.wv[:, :, :, col].reshape(16 * BIN_PAD, -1))

    def weights():
        for k in range(4):
            cols = slice(k * 512, (k + 1) * 512)
            res = dtn(r.draw[...], r.hv[:, :, cols].reshape(HALF_TOK, 512))
            own = r.wv[:, :, :, cols].reshape(16 * BIN_PAD, 512).astype(F32)
            r.gacc[:, cols] = jnp.sum(res * own, axis=0, keepdims=True)
            r.lin[:, :, :BIN_PAD, cols] = res.astype(BF).reshape(4, 4, BIN_PAD, 512)
            res = dtn(r.y[...], r.ev[:, :, cols].reshape(HALF_TOK, 512)).astype(BF)
            r.lin[:, :, BIN_PAD:, cols] = res.reshape(4, 4, 16, 512)
        reduce = plane_reduce(plane, r, "lin", ((0, r.lin_in), (BIN_PAD, r.lin_out)))
        advance(reduce)
        gains = (r.gacc[...] / r.gain[...], r.gain_b[...], r.gain_c[...])
        for n, gain in enumerate(gains):
            for i in range(8):
                r.pack[i : i + 1, n * wide : (n + 1) * wide] = gain[:, i * wide : (i + 1) * wide]
        gain_sums = sum_steps(ring, plane, r)
        advance(gain_sums)
        yield
        for _ in range(4):
            advance(win)
            advance(reduce)
            advance(gain_sums)
            yield
        finish(win)
        finish(gain_sums)
        finish(reduce)

    weight_grads = weights()

    def one(at):
        r.d_out[at, :] = r.res[at, :] + norm_back_rows(r.v, r.gain, sums_of(r, ring, at), at)

    def ready(q):
        by_rows(one, q * (TOK // CHUNKS), TOK // CHUNKS)

    weave(scatter(ring, r, product, ready), weight_grads)
    finish(weight_grads)
    for n, out in enumerate((r.ga, r.gb, r.gc)):
        for i in range(8):
            out[:, i * wide : (i + 1) * wide] = r.pack[i : i + 1, n * wide : (n + 1) * wide]


def last_step(lin, dy, select, tables, down, x3, low, g, w, h, e2, v, gain, res, gain_b, gain_c, width):
    small = (8, 3 * D // 8)
    return build(
        last_body,
        {
            "p": vm(lin.p),
            "dy": vm(dy),
            "sv": vm(lin.sv),
            "sn": vm(lin.sn),
            "sel": vm(select),
            "e": vm(tables[0]),
            "t": vm(tables[1]),
            "pick": vm(tables[2]),
            "down": hbm(down),
            "x3": vm(x3),
            "low": vm(low),
            "g": hbm(g),
            "w": hbm(w),
            "h": hbm(h),
            "e2": hbm(e2),
            "y": vm(lin.y),
            "v": vm(v),
            "gain": vm(gain),
            "res": vm(res),
            "gain_b": vm(gain_b),
            "gain_c": vm(gain_c),
        },
        {
            "out": (sds((TOK, D)), VM),
            "d_out": (sds((TOK, D), F32), VM),
            "ga": (sds((1, D), F32), VM),
            "gb": (sds((1, D), F32), VM),
            "gc": (sds((1, D), F32), VM),
            "win_in": (sds((48, D), F32), VM),
            "win_out": (sds((16, D), F32), VM),
            "lin_in": (sds((width, D), F32), VM),
            "lin_out": (sds((16, D), F32), VM),
        },
        {
            "dp": pltpu.VMEM((HALF_TOK, 3 * HEAD_V), BF),
            "draw": pltpu.VMEM((HALF_TOK, 16 * BIN_PAD), BF),
            "dq": pltpu.VMEM((2, HALF_TOK, 128), F32),
            "dk": pltpu.VMEM((2, HALF_TOK, 128), F32),
            "dv": pltpu.VMEM((2, HALF_TOK, HEAD_V), F32),
            "wv": pltpu.VMEM((4, 4, BIN_PAD, D), BF),
            "hv": pltpu.VMEM((8, TOK, D), BF),
            "ev": pltpu.VMEM((8, TOK, D), BF),
            "gacc": pltpu.VMEM((1, D), F32),
            "pack": pltpu.VMEM(small, F32),
            "ring_in": pltpu.VMEM((8,) + small, F32),
            "x_in": pltpu.VMEM((4,) + small, F32),
            "y_in": pltpu.VMEM((4,) + small, F32),
            "pss": pltpu.SemaphoreType.DMA((13,)),
            "prs": pltpu.SemaphoreType.DMA((13,)),
            "lsem": pltpu.SemaphoreType.DMA((4,)),
        }
        | STATE_SCRATCH
        | ROWS_SCRATCH
        | plane_reduce_scratch("win", 64)
        | plane_reduce_scratch("lin", BIN_PAD + 16)
        | SCATTER_SCRATCH,
        6,
    )


WBLK = 128
WKEYS = WBLK + WINDOW
INV_ROOT_V = 1.0 / math.sqrt(HEAD_V)


def turn_tables():
    slot = np.arange(2 * HALF_TOK)
    last = 2 * HALF_TOK - EDGE
    position = slot - np.where(slot < EDGE, 0, np.where(slot < last, EDGE, last))
    frequency = np.exp(-math.log(10000.0) * np.arange(HEAD_V // 2) * 2.0 / HEAD_V)
    angles = position[:, None] * frequency[None, :]
    cosine, sine = np.cos(angles), np.sin(angles)
    pair = np.stack(
        [np.concatenate([cosine, cosine], axis=1), np.concatenate([-sine, sine], axis=1)]
    )
    return pair.reshape(2, 2, HALF_TOK, HEAD_V).transpose(1, 0, 2, 3).astype(np.float32)


class Window:
    def __init__(self):
        self.xh = lax.axis_index("xh")
        self.partner = {"xh": 1 - self.xh}
        self.edge = jnp.where(self.xh == 0, EDGE, HALF_TOK - EDGE)
        self.lowest = jnp.where(self.xh == 0, 0, -WINDOW)

    def mask(self, b):
        t = b * WBLK + lax.broadcasted_iota(jnp.int32, (WBLK, WKEYS), 0)
        u = b * WBLK - WINDOW + lax.broadcasted_iota(jnp.int32, (WBLK, WKEYS), 1)
        same = (t >= self.edge) == (u >= self.edge)
        return (u <= t) & (t - u < WINDOW) & same & (u >= self.lowest)

    def probs(self, r, b, j):
        rows, keys, head = window_rows(b), window_keys(b), head_of(j)
        scores = dnt(r.q[rows, head], r.kv[keys, head]) * INV_ROOT_V
        scores = jnp.where(self.mask(b), scores, -1e30)
        exps = jnp.exp(scores - jnp.max(scores, axis=-1, keepdims=True))
        return exps / jnp.sum(exps, axis=-1, keepdims=True)


def window_rows(b):
    return slice(b * WBLK, (b + 1) * WBLK)


def window_keys(b):
    return slice(b * WBLK, b * WBLK + WKEYS)


def window_forward_part(r, cots):
    win = Window()
    size = 2 * TOK
    blocks = HALF_TOK // size

    def turned(vecs, rows):
        return (
            vecs * r.turn[0, rows, :] + pltpu.roll(vecs, HEAD_V // 2, 1) * r.turn[1, rows, :]
        ).astype(BF)

    for b in (blocks - 1,) + tuple(range(blocks - 1)):
        rows = slice(b * size, (b + 1) * size)
        shifted = slice(WINDOW + b * size, WINDOW + (b + 1) * size)
        tokens = r.hv[2 * b : 2 * b + 2].reshape(size, D)
        for j in range(2):
            proj = dnt(tokens, r.wiv[2 * j : 2 * j + 2].reshape(384, D))
            r.q[rows, head_of(j)] = turned(proj[:, :128], rows)
            r.kv[shifted, head_of(j)] = turned(proj[:, 128:256], rows)
            r.kv[shifted, head_of(2 + j)] = proj[:, 256:].astype(BF)
        if b == blocks - 1:
            copy = remote(
                r.kv.at[pl.ds(HALF_TOK, WINDOW), :],
                r.kv.at[pl.ds(0, WINDOW), :],
                r.xss,
                r.xrs,
                win.partner,
            )
    advance(cots)
    for b in tuple(range(1, HALF_TOK // WBLK)) + (0,):
        if b == 0:
            copy.wait_recv()
        for j in range(2):
            r.y[window_rows(b), head_of(j)] = dnn(
                win.probs(r, b, j).astype(BF), r.kv[window_keys(b), head_of(2 + j)]
            ).astype(BF)
        if b == 4:
            advance(cots)
    copy.wait_send()


def window_body(r):
    ring = Ring()
    partners = (ring.up, ring.dn, ring.sib, {"xh": 1 - lax.axis_index("xh")})
    signal(partners)
    loads = (
        load(r.w.at[:, :, pl.ds(0, 48), :], r.wiv, r.lsem.at[0]),
        load(r.h, r.hv, r.lsem.at[1]),
        load(r.turns.at[lax.axis_index("xh")], r.turn, r.lsem.at[2]),
        load(r.w.at[:, :, pl.ds(48, 16), :], r.wov, r.lsem.at[3]),
    )
    r.cbuf[ring.z * 2 + ring.c] = r.cot[TOK // 2 :, :]
    arrive(partners)
    cots = half_gather(ring, r, r.hi)
    advance(cots)
    for copy in loads:
        copy.wait()
    window_forward_part(r, cots)
    ring_forward(r, ring, r.y, r.wov, (cots,))
    finish(cots)


def window_step(h, w, turns, cot, x, gain):
    return build(
        window_body,
        {
            "h": hbm(h),
            "w": hbm(w),
            "turns": hbm(turns),
            "cot": vm(cot),
            "x": vm(x),
            "gain": vm(gain),
        },
        {
            "y": (sds((HALF_TOK, 256)), VM),
            "q": (sds((HALF_TOK, 256)), VM),
            "kv": (sds((HALF_TOK + WINDOW, 512)), VM),
            "hi": (sds((8, TOK // 2, D)), ANY),
            "x_out": (sds((TOK, D), F32), VM),
            "h_out": (sds((8, TOK, D)), ANY),
        },
        {
            "hv": pltpu.VMEM((8, TOK, D), BF),
            "wiv": pltpu.VMEM((4, 4, 48, D), BF),
            "wov": pltpu.VMEM((4, 4, 16, D), BF),
            "turn": pltpu.VMEM((2, HALF_TOK, HEAD_V), F32),
            "lsem": pltpu.SemaphoreType.DMA((4,)),
            "xss": pltpu.SemaphoreType.DMA,
            "xrs": pltpu.SemaphoreType.DMA,
        }
        | HALF_SCRATCH
        | SCATTER_SCRATCH
        | GATHER_SCRATCH,
        3,
    )


def window_backward_part(r, sums):
    win = Window()
    blocks = HALF_TOK // WBLK

    def turned_back(b, grads):
        rows = window_rows(b)
        return (
            grads * r.turn[0, rows, :] + pltpu.roll(grads * r.turn[1, rows, :], HEAD_V // 2, 1)
        ).astype(BF)

    for b in range(blocks):
        rows, keys = window_rows(b), window_keys(b)
        for j in range(2):
            head, vals = head_of(j), head_of(2 + j)
            queries, grads = r.q[rows, head], r.dy[rows, head]
            probs = win.probs(r, b, j)
            prob_grad = dnt(grads, r.kv[keys, vals])
            score_grad = (
                probs * (prob_grad - jnp.sum(prob_grad * probs, axis=-1, keepdims=True))
            ).astype(BF)
            r.dp[rows, head_of(3 * j)] = turned_back(
                b, dnn(score_grad, r.kv[keys, head]) * INV_ROOT_V
            )
            r.dkv[keys, head] += dtn(score_grad, queries) * INV_ROOT_V
            r.dkv[keys, vals] += dtn(probs.astype(BF), grads)
        if b == 0:
            copy = remote(r.dkv.at[pl.ds(0, WINDOW), :], r.halo, r.xss, r.xrs, win.partner)
        if b in (2, 6):
            advance(sums)
    for b in range(blocks):
        shifted = slice(WINDOW + b * WBLK, WINDOW + (b + 1) * WBLK)
        if b == blocks - 1:
            copy.wait_recv()
            r.dkv[HALF_TOK : HALF_TOK + WINDOW, :] += r.halo[...]
        for j in range(2):
            r.dp[window_rows(b), head_of(3 * j + 1)] = turned_back(b, r.dkv[shifted, head_of(j)])
            r.dp[window_rows(b), head_of(3 * j + 2)] = r.dkv[shifted, head_of(2 + j)].astype(BF)
    copy.wait_send()


def window_back_body(r):
    ring = Ring()
    partners = (ring.up, ring.dn, ring.sib, {"xh": 1 - lax.axis_index("xh")})
    signal(partners)
    turning = load(r.turns.at[lax.axis_index("xh")], r.turn, r.lsem.at[0])
    loads = [
        load(r.w.at[:, :, pl.ds(0, 48), :], r.wiv, r.lsem.at[1]),
        load(r.h, r.hv, r.lsem.at[2]),
        load(r.e, r.ev, r.lsem.at[3]),
        load(r.wo.at[:, :, pl.ds(BIN_PAD, 16), :], r.wov, r.lsem.at[4]),
    ]
    r.dkv[...] = jnp.zeros_like(r.dkv)
    r.gacc[...] = jnp.zeros_like(r.gacc)

    def write(at, rows, total):
        r.low[at, :] = (r.x3[rows, :] + total).astype(BF)

    sums = rows_reduce(ring, r, 0, write)
    arrive(partners)
    advance(sums)
    turning.wait()
    window_backward_part(r, sums)
    finish(sums)
    for copy in loads:
        copy.wait()

    def product(rows, col):
        return dnn(r.dp[rows, :], r.wiv[:, :, :, col].reshape(768, -1))

    def weights():
        for k in range(4):
            cols = slice(k * 512, (k + 1) * 512)
            rows = r.hv[:, :, cols].reshape(HALF_TOK, 512)
            for i in range(2):
                res = dtn(r.dp[:, i * 384 : (i + 1) * 384], rows)
                own = r.wiv[2 * i : 2 * i + 2, :, :, cols].reshape(384, 512).astype(F32)
                r.gacc[:, cols] += jnp.sum(res * own, axis=0, keepdims=True)
                r.gstage[2 * i : 2 * i + 2, :, :48, cols] = res.astype(BF).reshape(2, 4, 48, 512)
            res = dtn(r.y[...], r.ev[:, :, cols].reshape(HALF_TOK, 512)).astype(BF)
            r.gstage[:, :, 48:, cols] = res.reshape(4, 4, 16, 512)
            yield
        copy = load(r.gstage, r.grads, r.lsem.at[5])
        yield
        copy.wait()

    weight_grads = weights()
    ring_backward(r, ring, product, r.wov, (weight_grads,))
    finish(weight_grads)
    r.gain_out[...] = r.gacc[...] / r.gain[...]


def window_back_step(win, dy, turns, down, x3, w, wo, h, e, v, gain, res):
    return build(
        window_back_body,
        {
            "q": vm(win.q),
            "kv": vm(win.kv),
            "dy": vm(dy),
            "turns": hbm(turns),
            "down": hbm(down),
            "x3": vm(x3),
            "w": hbm(w),
            "wo": hbm(wo),
            "h": hbm(h),
            "e": hbm(e),
            "y": vm(win.y),
            "v": vm(v),
            "gain": vm(gain),
            "res": vm(res),
        },
        {
            "low": (sds((TOK // 2, D)), VM),
            "d_out": (sds((TOK, D), F32), VM),
            "gain_out": (sds((1, D), F32), VM),
            "e_out": (sds((8, TOK, D)), ANY),
            "dy_out": (sds((HALF_TOK, 256)), VM),
            "grads": (sds((4, 4, 64, D)), ANY),
        },
        {
            "dkv": pltpu.VMEM((HALF_TOK + WINDOW, 512), F32),
            "halo": pltpu.VMEM((WINDOW, 512), F32),
            "turn": pltpu.VMEM((2, HALF_TOK, HEAD_V), F32),
            "dp": pltpu.VMEM((HALF_TOK, 768), BF),
            "wiv": pltpu.VMEM((4, 4, 48, D), BF),
            "wov": pltpu.VMEM((4, 4, 16, D), BF),
            "hv": pltpu.VMEM((8, TOK, D), BF),
            "ev": pltpu.VMEM((8, TOK, D), BF),
            "gstage": pltpu.VMEM((4, 4, 64, D), BF),
            "gacc": pltpu.VMEM((1, D), F32),
            "lsem": pltpu.SemaphoreType.DMA((6,)),
            "xss": pltpu.SemaphoreType.DMA,
            "xrs": pltpu.SemaphoreType.DMA,
        }
        | ROWS_SCRATCH
        | SCATTER_SCRATCH
        | GATHER_SCRATCH,
        5,
    )


def padded(rows, count):
    return jnp.pad(rows, ((0, count - rows.shape[0]), (0, 0)))


def place():
    slot = lax.axis_index("xh") * HALF_TOK + jnp.arange(HALF_TOK, dtype=jnp.int32)
    last = 2 * HALF_TOK - EDGE
    segment = (slot >= EDGE).astype(jnp.int32) + (slot >= last).astype(jnp.int32)
    start = jnp.where(segment == 0, 0, jnp.where(segment == 1, EDGE, last)).astype(jnp.int32)
    return segment, slot - start


def body(
    block_input,
    cotangent,
    lengths,
    gain_a,
    based_in,
    based_out,
    gain_b,
    swa_in,
    swa_out,
    gain_c,
    mlp_in,
    mlp_down,
):
    gains = [gain.reshape(1, D) for gain in (gain_a, gain_b, gain_c)]
    units = mlp_down.shape[0]
    wide = based_in.shape[1]
    win_all = lax.all_gather(
        jnp.concatenate([swa_in.T, swa_out], axis=0), PLANE, axis=0, tiled=True
    ).reshape(4, 4, 64, D)
    ff_all = lax.all_gather(
        jnp.concatenate(
            [padded(part, UNIT_PAD) for part in (mlp_in[:, 0, :].T, mlp_in[:, 1, :].T, mlp_down)],
            axis=0,
        ),
        PLANE,
        axis=0,
        tiled=True,
    ).reshape(16, 3 * UNIT_PAD, D)
    segment, position = place()
    first = (lax.axis_index("z") * 2 + lax.axis_index("c")) * TOK
    my_segment = lax.dynamic_slice_in_dim(segment, first, TOK)
    my_position = lax.dynamic_slice_in_dim(position, first, TOK)
    chosen = jnp.where(
        my_segment == 0,
        lengths[0, 0],
        jnp.where(my_segment == 1, lengths[0, 1], lengths[0, 2]),
    )
    valid = (my_position < chosen)[:, None]
    cot_low = jnp.where(valid, cotangent, jnp.zeros_like(cotangent))
    tables = tuple(
        jnp.asarray(table, kind) for table, kind in zip(state_tables(), (BF, F32, BF))
    )
    select = jnp.asarray(select_table(wide), BF)

    turns = jnp.asarray(turn_tables())

    start = first_step(block_input, gains[0], based_in.T, based_out)
    lin = linear_step(start.raw, select, tables, cot_low, start.w, block_input, gains[1])
    win = window_step(lin.h_out, win_all, turns, cot_low, lin.x_out, gains[2])
    mlp = mlp_step(win.h_out, lin.lo, win.hi, ff_all, win_all, win.x_out, gains[2], cot_low)
    ff_grads = lax.psum_scatter(
        mlp.grads.reshape(-1, D), PLANE, scatter_dimension=0, tiled=True
    ).astype(F32)
    back = window_back_step(
        win,
        mlp.dy_out,
        turns,
        mlp.down,
        win.x_out,
        win_all,
        start.w,
        lin.h_out,
        mlp.e_out,
        lin.x_out,
        gains[1],
        mlp.d_out,
    )
    end = last_step(
        lin,
        back.dy_out,
        select,
        tables,
        mlp.down,
        win.x_out,
        back.low,
        back.grads,
        start.w,
        start.h,
        back.e_out,
        block_input,
        gains[0],
        back.d_out,
        back.gain_out,
        mlp.gain_out,
        wide,
    )
    gate_grad = ff_grads[:units]
    up_grad = ff_grads[UNIT_PAD : UNIT_PAD + units]
    return (
        end.out,
        end.d_out,
        end.ga.reshape(D),
        end.lin_in.T,
        end.lin_out,
        end.gb.reshape(D),
        end.win_in.T,
        end.win_out,
        end.gc.reshape(D),
        jnp.stack([gate_grad.T, up_grad.T], axis=1),
        ff_grads[2 * UNIT_PAD : 2 * UNIT_PAD + units],
    )


def solution(mesh):
    grid = Mesh(mesh.devices.reshape(2, 4, 2, 4, 2), ALL)
    tokens = P(ALL, None)
    weight = ("xh", "z", "c", "xl", "y")
    rows, cols = P(weight, None), P(None, weight)
    return jax.shard_map(
        body,
        mesh=grid,
        in_specs=(
            tokens,
            tokens,
            P(("xl", "y"), None),
            P(),
            cols,
            rows,
            P(),
            cols,
            rows,
            P(),
            P(None, None, weight),
            rows,
        ),
        out_specs=(
            tokens,
            tokens,
            P(),
            cols,
            rows,
            P(),
            cols,
            rows,
            P(),
            P(None, None, weight),
            rows,
        ),
        check_vma=False,
    )
```

time: 1570 us -> 414 us (0.26)
  waiting for transfers between devices: 1070 us -> 0.11 us
  Pallas kernels: 0 us -> 374 us
  blocking collectives: 198 us -> 0 us
  matrix products: 165 us -> 0 us
  other arithmetic: 61.1 us -> 6.75 us
    reduce_scatter x9 -> x1, waiting for transfers between devices: 686 us -> 0.02 us  [body(): lax.psum_scatter(mlp.grads.reshape(-1, D), PLANE, scatter_dimension=0, ti...]
    all_gather x9 -> x2, waiting for transfers between devices: 381 us -> 0.04 us  [the longest x1 0.02 us: body(): lax.all_gather(jnp.concatenate([swa_in.T, swa_out], axis=0), PLANE, axis=...]
    pallas_call x0 -> x6, Pallas kernels: none -> 374 us  [build(): pl.pallas_call(kernel, out_shape=tuple((shape for shape, _ in outputs.val...]
    dot_general x52 -> x0, matrix products: 165 us -> none  [the longest x6 43.9 us: contract_cols(): lax.dot_general(left_side, right_side, (((1,), (1,)), ((), ())), preferre...]
    all_gather x3 -> x0, blocking collectives: 93.7 us -> none  [the longest x1 32 us: body(): lax.all_gather(based_in, 'dp', axis=1, tiled=True)]
    psum x1 -> x0, blocking collectives: 64.9 us -> none  [body(): lax.psum((gain_a_grad, gain_b_grad, gain_c_grad), ('dp', 'head'))]
    unnamed x1 -> x0, blocking collectives: 39.1 us -> none
    convert_element_type x20 -> x1, other arithmetic: 36.8 us -> 1.18 us  [body(): ff_grads = lax.psum_scatter(mlp.grads.reshape(-1, D), PLANE, scatter_dime...]
  transfers between devices with their start and end apart: 22 -> 3, of which waited for: 18 -> 0; matrix products, arithmetic and copies ran while one was open for 11% -> 2% of each run, Pallas kernels for 0% -> 75%
where the time goes in v4:
time: 414 us; the launch traced here: 407 us
  Pallas kernels  374 us (90%)
  between operations  14.4 us (3%)
  local copies, waits for them, and re-layouts  11.1 us (3%)
  other arithmetic  6.75 us (2%)
    pallas_call x6, Pallas kernels, build(): pl.pallas_call(kernel, out_shape=tuple((shape for shape, _ in outputs.val...  374 us
  transfers between devices with their start and end apart: 3, of which 0 were waited for; matrix products, arithmetic and copies ran while one was open for 2% of the time, Pallas kernels for 75%

profile of v4, /device:TPU:0, one launch (start us, length us, event | category | flops | bytes accessed | tf_op | source)
XLA Modules:
  0.0 406.9 jit_solution(9305824432105947224)
XLA Ops:
  7.2 0.0 all-gather.3.cloned.1.call-start
  7.2 1.7 pad_maximum_fusion.1
  9.0 0.0 all-gather.5.cloned.1.call-start
  9.0 1.7 fusion.9
  10.8 0.2 copy_bitcast_fusion
  11.0 0.9 fusion.5
  11.9 0.0 reduce-scatter.2.cloned.1.call-start
  12.0 35.9 %shard_map.248 = (bf16[8,128,2048]{2,1,0:T(8,128)(2,1)}, bf16[4,4,48,2048]{3,2,1,0:T(8,128)(2,1)}, bf16[1024,512]{1,0:T(8,128)(2,1)}) custom-call(bf16[128,2048]{1,0:T(8,128)(2,1)} %refs_16_.1, f32[1,2048]{1,0:T(1,128)} %bitcast.43, bf16[20,2048]{1,0:T(8,128)(2,1)} %bitcast.40, bf16[16,2048]{1,0:T(8,128)(2,1)} %refs_3_.3), custom_call_target="tpu_custom_call" | custom-call | tf_op jit(solution)/shard_map/pallas_call | solution.py:592
  47.9 0.6 fusion.10
  48.5 2.0 fusion.8
  50.5 0.9 broadcast_select_fusion.refs_5_.refs_3_.refs_7_
  51.4 60.5 %shard_map.249 = (bf16[1024,256]{1,0:T(8,128)(2,1)}, bf16[1024,384]{1,0:T(8,128)(2,1)}, bf16[2,4,128,256]{3,2,1,0:T(8,128)(2,1)}, f32[2,4,8,256]{3,2,1,0:T(8,128...) custom-call(bf16[1024,512]{1,0:T(8,128)(2,1)} %get-tuple-element.48.refs_0_, ...), custom_call_target="tpu_custom_call" | custom-call | tf_op jit(solution)/shard_map/pallas_call | solution.py:592
  111.9 0.0 all-gather.3.cloned.1.call-done
  111.9 58.6 %shard_map.250 = (bf16[1024,256]{1,0:T(8,128)(2,1)}, bf16[1024,256]{1,0:T(8,128)(2,1)}, bf16[1088,512]{1,0:T(8,128)(2,1)}, bf16[8,64,2048]{2,1,0:T(8,128)(2,1)},...) custom-call(bf16[8,128,2048]{2,1,0:T(8,128)(2,1)} %get-tuple-element.51.refs_0_.refs_8_, ...), custom_call_target="tpu_custom_call" | custom-call | tf_op jit(solution)/shard_map/pallas_call | solution.py:592
  170.5 0.0 all-gather.5.cloned.1.call-done
  170.5 70.6 %shard_map.251 = (bf16[1024,2048]{1,0:T(8,128)(2,1)}, f32[128,2048]{1,0:T(8,128)}, f32[1,2048]{1,0:T(1,128)}, bf16[8,128,2048]{2,1,0:T(8,128)(2,1)}, bf16[1024,2...) custom-call(bf16[8,128,2048]{2,1,0:T(8,128)(2,1)} %get-tuple-element.55.refs_0_, ...), custom_call_target="tpu_custom_call" | custom-call | tf_op jit(solution)/shard_map/pallas_call | solution.py:592
  241.1 63.2 %shard_map.252 = (bf16[64,2048]{1,0:T(8,128)(2,1)}, f32[128,2048]{1,0:T(8,128)}, f32[1,2048]{1,0:T(1,128)}, bf16[8,128,2048]{2,1,0:T(8,128)(2,1)}, bf16[1024,256...) custom-call(bf16[1024,256]{1,0:T(8,128)(2,1)} %get-tuple-element.53.refs_0_, bf16[1088,512]{1,0:T(8,128)(2,1)} %get-tuple-element.54.refs_1_, ...), custom_call_target="tpu_custom_call" | custom-call | tf_op jit(solution)/shard_map/pallas_call | solution.py:592
  304.4 85.6 %shard_map.253 = (bf16[128,2048]{1,0:T(8,128)(2,1)}, f32[128,2048]{1,0:T(8,128)}, f32[1,2048]{1,0:T(1,128)}, f32[1,2048]{1,0:T(1,128)}, f32[1,2048]{1,0:T(1,128)...) custom-call(bf16[1024,384]{1,0:T(8,128)(2,1)} %get-tuple-element.50.refs_0_, ...), custom_call_target="tpu_custom_call" | custom-call | tf_op jit(solution)/shard_map/pallas_call | solution.py:592
  390.0 1.2 convert_element_type.15
  391.2 0.1 slice_bitcast_fusion.1
  391.3 0.1 pad_maximum_fusion
  391.4 1.4 copy.30
  392.8 0.8 slice.34
  393.6 0.8 copy.44
  394.4 1.0 copy.45
  395.3 0.6 copy.46
  396.0 0.7 copy.47
  396.6 0.7 copy.48
  397.3 0.6 copy.49
  397.9 0.7 copy.50
  398.6 0.7 copy.51
  399.3 0.6 copy.52
  (31 shorter events, 0.1 us)
Async XLA Ops:
  7.2 3.8 copy-start.5
  7.2 104.7 %all-gather.3.cloned.1.call-start = ((), (), s32[]{:S(2)}) async-start(), calls=%async_computation.1 | async-start | bytes 4456448 | tf_op jit(solution)/shard_map/all_gather | solution.py:1705
  9.0 161.5 %all-gather.5.cloned.1.call-start = ((), (), s32[]{:S(2)}) async-start(), calls=%async_computation.2 | async-start | bytes 10027008 | tf_op jit(solution)/shard_map/all_gather | solution.py:1708
  10.8 37.1 %copy-start.12 = (s32[1,3]{1,0:T(1,128)S(1)}, s32[1,3]{1,0:T(1,128)}, u32[]{:S(2)}) copy-start(s32[1,3]{1,0:T(1,128)} %param.19) | copy-start | bytes 40
  10.8 39.7 %copy-start.3 = (bf16[128,2048]{1,0:T(8,128)(2,1)S(1)}, bf16[128,2048]{1,0:T(8,128)(2,1)}, u32[]{:S(2)}) copy-start(bf16[128,2048]{1,0:T(8,128)(2,1)} %param.18) | copy-start | bytes 1572868
  11.9 378.1 %reduce-scatter.2.cloned.1.call-start = ((), (), s32[]{:S(2)}) async-start(), calls=%async_computation.3 | async-start | bytes 10027008 | tf_op jit(solution)/shard_map/reduce_scatter | solution.py:1739
  391.2 1.6 copy-start
  391.3 2.3 copy-start.2
  391.3 3.1 copy-start.1
  392.8 2.6 copy-start.11
  392.8 3.2 copy-start.6
  392.8 3.8 copy-start.8
  393.6 3.7 copy-start.10
  393.6 4.3 %copy-start.4 = (f32[48,2048]{1,0:T(8,128)S(1)}, f32[48,2048]{1,0:T(8,128)}, u32[]{:S(2)}) copy-start(f32[48,2048]{1,0:T(8,128)} %get-tuple-element.81) | copy-start | bytes 1179652
  393.6 5.1 %copy-start.7 = (f32[16,2048]{1,0:T(8,128)S(1)}, f32[16,2048]{1,0:T(8,128)}, u32[]{:S(2)}) copy-start(f32[16,2048]{1,0:T(8,128)} %get-tuple-element.125) | copy-start | bytes 393220
  394.4 4.9 %copy-start.9 = (f32[1,2048]{1,0:T(1,128)S(1)}, f32[1,2048]{1,0:T(1,128)}, u32[]{:S(2)}) copy-start(f32[1,2048]{1,0:T(1,128)} %get-tuple-element.83) | copy-start | bytes 24580
Sparse Core Ops, SparseCore 0:
  10.7 59.1 all-gather.2
  72.7 76.5 all-gather.4
  241.2 92.8 reduce-scatter.1
